TPU v7x, 32 devices: a whole 2x2x4 slice. The times are simulated.
32 devices in a mesh: dp: 8 (over z, x), seq: 4 (over y, core).
Axes of the slice: x: 2, y: 2, z: 4, core: 2. Of those that a mesh axis runs over, the one named last changes fastest.
Arguments:
- tokens: bfloat16 [8, 2048, 1024], P('dp', 'seq'), may hold values from -6 to 6
- cotangent: bfloat16 [8, 2048, 1024], P('dp', 'seq'), may hold values from -6 to 6
- w_qkv: bfloat16 [1024, 3072], P('dp'), may hold values from -0.1875 to 0.1875
- w_attn: bfloat16 [1024, 1024], P('dp'), may hold values from -1.5 to 1.5
- w_fc: bfloat16 [1024, 4096], P('dp'), may hold values from -0.1875 to 0.1875
- w_proj: bfloat16 [4096, 1024], P('dp'), may hold values from -0.09375 to 0.09375
- bias_query: bfloat16 [1024], P('dp'), may hold values from -3 to 3
- bias_value: bfloat16 [1024], P('dp'), may hold values from -3 to 3
- bias_attn: bfloat16 [1024], P('dp'), may hold values from -3 to 3
- gain_one: bfloat16 [1024], P('dp'), may hold values from 0.5 to 1.5
- shift_one: bfloat16 [1024], P('dp'), may hold values from -3 to 3
- gain_two: bfloat16 [1024], P('dp'), may hold values from 0.5 to 1.5
- shift_two: bfloat16 [1024], P('dp'), may hold values from -3 to 3
- bias_fc: bfloat16 [4096], P('dp'), may hold values from -3 to 3
- bias_proj: bfloat16 [1024], P('dp'), may hold values from -3 to 3
Outputs:
- output: bfloat16 [8, 2048, 1024], P('dp', 'seq')
- grad_tokens: float32 [8, 2048, 1024], P('dp', 'seq')
- grad_w_qkv: float32 [1024, 3072], P('dp')
- grad_w_attn: float32 [1024, 1024], P('dp')
- grad_w_fc: float32 [1024, 4096], P('dp')
- grad_w_proj: float32 [4096, 1024], P('dp')
- grad_bias_query: float32 [1024], P('dp')
- grad_bias_value: float32 [1024], P('dp')
- grad_bias_attn: float32 [1024], P('dp')
- grad_gain_one: float32 [1024], P('dp')
- grad_shift_one: float32 [1024], P('dp')
- grad_gain_two: float32 [1024], P('dp')
- grad_shift_two: float32 [1024], P('dp')
- grad_bias_fc: float32 [4096], P('dp')
- grad_bias_proj: float32 [1024], P('dp')
All inputs are finite; a program needn't handle non-finite values.
Results may differ from a plain program's by a relative error of at most 0.018.
Values may be sent and summed in bfloat16 or wider, within the bound.
No kernel may reach another device: no remote copies, remote signals or barrier semaphores. Data moves between devices by JAX's collectives and lax.ppermute only.
A program may use at most 256 MiB of HBM per device.

v0:
```python
import jax
import jax.numpy as jnp
from jax import lax
from jax.sharding import PartitionSpec as P

HEAD_DIM = 64
ROW_BLOCK = 512


EPSILON = 1e-05
ROOT_COEF = 0.7978845608028654


def layer_norm(values, gain_vec, shift_vec):
    average = jnp.mean(values, axis=-1, keepdims=True)
    centered = values - average
    variance = jnp.mean(centered * centered, axis=-1, keepdims=True)
    return centered * lax.rsqrt(variance + EPSILON) * gain_vec + shift_vec


def gelu_tanh(values):
    return (
        0.5 * values * (1.0 + jnp.tanh(ROOT_COEF * (values + 0.044715 * values * values * values)))
    )


def matmul(left_side, right_side):
    return jnp.dot(left_side, right_side, preferred_element_type=jnp.float32)


def matmul_back(left_side, right_side):
    return lax.dot_general(
        left_side,
        right_side,
        (((left_side.ndim - 1,), (1,)), ((), ())),
        preferred_element_type=jnp.float32,
    )


def weight_grad(left_side, right_side):
    return lax.dot_general(
        left_side, right_side, (((0,), (0,)), ((), ())), preferred_element_type=jnp.float32
    )


def flatten(array):
    return array.reshape(-1, array.shape[-1])


def causal_mask(first_row, block_rows, stop_row):
    row_pos = first_row + jnp.arange(block_rows, dtype=jnp.int32)
    col_pos = jnp.arange(stop_row, dtype=jnp.int32)
    return row_pos[:, None] >= col_pos[None, :]


def split_heads(received):
    seqs_here, length = (received.shape[0], received.shape[1])
    heads_here = received.shape[-1] // HEAD_DIM
    shaped = received.reshape(seqs_here, length, 3, heads_here, HEAD_DIM)
    return (shaped[:, :, 0], shaped[:, :, 1], shaped[:, :, 2])


def block_scores(query_block, key_rows, first_row, stop_row):
    score_scale = HEAD_DIM ** (-0.5)
    scores = (
        jnp.einsum(
            "sqhd,skhd->shqk",
            query_block,
            key_rows[:, :stop_row],
            preferred_element_type=jnp.float32,
        )
        * score_scale
    )
    return jnp.where(causal_mask(first_row, query_block.shape[1], stop_row), scores, -1e30)


def attend_items(received):
    query_rows, key_rows, value_rows = split_heads(received)
    seqs_here, length = (received.shape[0], received.shape[1])
    block_rows = ROW_BLOCK
    pieces = []
    log_parts = []
    for block_index in range(length // block_rows):
        first_row = block_index * block_rows
        stop_row = first_row + block_rows
        scores = block_scores(query_rows[:, first_row:stop_row], key_rows, first_row, stop_row)
        largest = jnp.max(scores, axis=-1, keepdims=True)
        weights = jnp.exp(scores - largest)
        row_total = jnp.sum(weights, axis=-1, keepdims=True)
        probability = (weights / row_total).astype(jnp.bfloat16)
        pieces.append(
            jnp.einsum(
                "shqk,skhd->sqhd",
                probability,
                value_rows[:, :stop_row],
                preferred_element_type=jnp.float32,
            )
        )
        log_parts.append((largest + jnp.log(row_total))[..., 0])
    attended = jnp.concatenate(pieces, axis=1).astype(jnp.bfloat16)
    attended = attended.reshape(seqs_here, length, 1, received.shape[-1])
    return (attended, jnp.concatenate(log_parts, axis=-1), received)


def attend_backward(received, log_totals, grad_heads):
    query_rows, key_rows, value_rows = split_heads(received)
    seqs_here, length = (received.shape[0], received.shape[1])
    heads_here = received.shape[-1] // HEAD_DIM
    grad_rows = grad_heads.reshape(seqs_here, length, heads_here, HEAD_DIM)
    score_scale = HEAD_DIM ** (-0.5)
    block_rows = ROW_BLOCK
    grad_query_parts = []
    grad_key = jnp.zeros(query_rows.shape, jnp.float32)
    grad_value = jnp.zeros(query_rows.shape, jnp.float32)
    for block_index in range(length // block_rows):
        first_row = block_index * block_rows
        stop_row = first_row + block_rows
        query_block = query_rows[:, first_row:stop_row]
        grad_block = grad_rows[:, first_row:stop_row]
        scores = block_scores(query_block, key_rows, first_row, stop_row)
        probability = jnp.exp(scores - log_totals[:, :, first_row:stop_row, None])
        grad_probs = jnp.einsum(
            "sqhd,skhd->shqk",
            grad_block,
            value_rows[:, :stop_row],
            preferred_element_type=jnp.float32,
        )
        inner = jnp.sum(probability * grad_probs, axis=-1, keepdims=True)
        grad_scores = (probability * (grad_probs - inner)).astype(jnp.bfloat16)
        grad_value = grad_value.at[:, :stop_row].add(
            jnp.einsum(
                "shqk,sqhd->skhd",
                probability.astype(jnp.bfloat16),
                grad_block,
                preferred_element_type=jnp.float32,
            )
        )
        grad_query_parts.append(
            jnp.einsum(
                "shqk,skhd->sqhd",
                grad_scores,
                key_rows[:, :stop_row],
                preferred_element_type=jnp.float32,
            )
            * score_scale
        )
        grad_key = grad_key.at[:, :stop_row].add(
            jnp.einsum(
                "shqk,sqhd->skhd", grad_scores, query_block, preferred_element_type=jnp.float32
            )
            * score_scale
        )
    grad_query = jnp.concatenate(grad_query_parts, axis=1)
    stacked = jnp.stack([grad_query, grad_key, grad_value], axis=2).astype(jnp.bfloat16)
    return stacked.reshape(seqs_here, length, 3, 1, received.shape[-1])


def per_device(
    tokens,
    cotangent,
    w_qkv,
    w_attn,
    w_fc,
    w_proj,
    bias_query,
    bias_value,
    bias_attn,
    gain_one,
    shift_one,
    gain_two,
    shift_two,
    bias_fc,
    bias_proj,
):
    seq_count = lax.axis_size("seq")
    seqs_dev, rows_dev, model_width = tokens.shape
    gathered = (
        lax.all_gather(w_qkv, "dp", axis=0, tiled=True),
        lax.all_gather(w_attn, "dp", axis=0, tiled=True),
        lax.all_gather(w_fc, "dp", axis=0, tiled=True),
        lax.all_gather(w_proj, "dp", axis=0, tiled=True),
        lax.all_gather(bias_query, "dp", axis=0, tiled=True),
        lax.all_gather(bias_value, "dp", axis=0, tiled=True),
        lax.all_gather(bias_attn, "dp", axis=0, tiled=True),
        lax.all_gather(gain_one, "dp", axis=0, tiled=True),
        lax.all_gather(shift_one, "dp", axis=0, tiled=True),
        lax.all_gather(gain_two, "dp", axis=0, tiled=True),
        lax.all_gather(shift_two, "dp", axis=0, tiled=True),
        lax.all_gather(bias_fc, "dp", axis=0, tiled=True),
        lax.all_gather(bias_proj, "dp", axis=0, tiled=True),
    )
    full_qkv, full_attn, full_fc, full_proj = (gathered[0], gathered[1], gathered[2], gathered[3])
    (
        query_bias,
        value_bias,
        attn_bias,
        gain_first,
        shift_first,
        gain_second,
        shift_second,
        fc_bias,
        proj_bias,
    ) = tuple((item.astype(jnp.float32) for item in gathered[4:]))
    inputs = tokens.astype(jnp.float32)
    normed = layer_norm(inputs, gain_first, shift_first).astype(jnp.bfloat16)
    joint_bias = jnp.concatenate([query_bias, jnp.zeros_like(query_bias), value_bias])
    mixed_rows = (matmul(normed, full_qkv) + joint_bias).astype(jnp.bfloat16)
    group_width = model_width // seq_count
    packed = mixed_rows.reshape(seqs_dev, rows_dev, 3, seq_count, group_width)
    attended, log_totals, received = attend_items(
        lax.all_to_all(packed, "seq", split_axis=3, concat_axis=1, tiled=True)
    )
    joined = lax.all_to_all(attended, "seq", split_axis=1, concat_axis=2, tiled=True).reshape(
        seqs_dev, rows_dev, model_width
    )
    branch = matmul(joined, full_attn) + attn_bias
    middle = inputs + branch
    normed_two = layer_norm(middle, gain_second, shift_second).astype(jnp.bfloat16)
    hidden = matmul(normed_two, full_fc) + fc_bias
    active = gelu_tanh(hidden).astype(jnp.bfloat16)
    output = (middle + matmul(active, full_proj) + proj_bias).astype(jnp.bfloat16)
    back_qkv, back_attn, back_fc, back_proj = (full_qkv, full_attn, full_fc, full_proj)
    upstream = cotangent.astype(jnp.float32)
    grad_w_proj = weight_grad(flatten(active), flatten(cotangent))
    grad_bias_proj = jnp.sum(flatten(upstream), axis=0)
    grad_active = matmul_back(cotangent, back_proj)
    grad_hidden = jax.vjp(gelu_tanh, hidden)[1](grad_active)[0].astype(jnp.bfloat16)
    grad_w_fc = weight_grad(flatten(normed_two), flatten(grad_hidden))
    grad_bias_fc = jnp.sum(flatten(grad_hidden), axis=0, dtype=jnp.float32)
    grad_normed_two = matmul_back(grad_hidden, back_fc)
    grad_middle_part, grad_gain_two, grad_shift_two = jax.vjp(
        layer_norm, middle, gain_second, shift_second
    )[1](grad_normed_two)
    grad_middle = upstream + grad_middle_part
    grad_branch = grad_middle.astype(jnp.bfloat16)
    grad_w_attn = weight_grad(flatten(joined), flatten(grad_branch))
    grad_bias_attn = jnp.sum(flatten(grad_branch), axis=0, dtype=jnp.float32)
    grad_joined = matmul_back(grad_branch, back_attn).astype(jnp.bfloat16)
    grad_joined = grad_joined.reshape(seqs_dev, rows_dev, seq_count, group_width)
    grad_heads = lax.all_to_all(grad_joined, "seq", split_axis=2, concat_axis=1, tiled=True)
    grad_packed = attend_backward(received, log_totals, grad_heads)
    grad_mixed = lax.all_to_all(
        grad_packed, "seq", split_axis=1, concat_axis=3, tiled=True
    ).reshape(seqs_dev, rows_dev, 3 * model_width)
    grad_w_qkv = weight_grad(flatten(normed), flatten(grad_mixed))
    column_sums = jnp.sum(flatten(grad_mixed), axis=0, dtype=jnp.float32)
    grad_bias_query = column_sums[:model_width]
    grad_bias_value = column_sums[2 * model_width :]
    grad_normed = matmul_back(grad_mixed, back_qkv)
    grad_input_part, grad_gain_one, grad_shift_one = jax.vjp(
        layer_norm, inputs, gain_first, shift_first
    )[1](grad_normed)
    grad_tokens = grad_middle + grad_input_part
    local_grads = (
        grad_w_qkv,
        grad_w_attn,
        grad_w_fc,
        grad_w_proj,
        grad_bias_query,
        grad_bias_value,
        grad_bias_attn,
        grad_gain_one,
        grad_shift_one,
        grad_gain_two,
        grad_shift_two,
        grad_bias_fc,
        grad_bias_proj,
    )
    shards = (
        lax.psum_scatter(
            local_grads[0].astype(jnp.bfloat16), "dp", scatter_dimension=0, tiled=True
        ).astype(jnp.float32),
        lax.psum_scatter(
            local_grads[1].astype(jnp.bfloat16), "dp", scatter_dimension=0, tiled=True
        ).astype(jnp.float32),
        lax.psum_scatter(
            local_grads[2].astype(jnp.bfloat16), "dp", scatter_dimension=0, tiled=True
        ).astype(jnp.float32),
        lax.psum_scatter(
            local_grads[3].astype(jnp.bfloat16), "dp", scatter_dimension=0, tiled=True
        ).astype(jnp.float32),
        lax.psum_scatter(
            local_grads[4].astype(jnp.bfloat16), "dp", scatter_dimension=0, tiled=True
        ).astype(jnp.float32),
        lax.psum_scatter(
            local_grads[5].astype(jnp.bfloat16), "dp", scatter_dimension=0, tiled=True
        ).astype(jnp.float32),
        lax.psum_scatter(
            local_grads[6].astype(jnp.bfloat16), "dp", scatter_dimension=0, tiled=True
        ).astype(jnp.float32),
        lax.psum_scatter(
            local_grads[7].astype(jnp.bfloat16), "dp", scatter_dimension=0, tiled=True
        ).astype(jnp.float32),
        lax.psum_scatter(
            local_grads[8].astype(jnp.bfloat16), "dp", scatter_dimension=0, tiled=True
        ).astype(jnp.float32),
        lax.psum_scatter(
            local_grads[9].astype(jnp.bfloat16), "dp", scatter_dimension=0, tiled=True
        ).astype(jnp.float32),
        lax.psum_scatter(
            local_grads[10].astype(jnp.bfloat16), "dp", scatter_dimension=0, tiled=True
        ).astype(jnp.float32),
        lax.psum_scatter(
            local_grads[11].astype(jnp.bfloat16), "dp", scatter_dimension=0, tiled=True
        ).astype(jnp.float32),
        lax.psum_scatter(
            local_grads[12].astype(jnp.bfloat16), "dp", scatter_dimension=0, tiled=True
        ).astype(jnp.float32),
    )
    summed = (
        lax.psum(shards[0].astype(jnp.bfloat16), "seq").astype(jnp.float32),
        lax.psum(shards[1].astype(jnp.bfloat16), "seq").astype(jnp.float32),
        lax.psum(shards[2].astype(jnp.bfloat16), "seq").astype(jnp.float32),
        lax.psum(shards[3].astype(jnp.bfloat16), "seq").astype(jnp.float32),
        lax.psum(shards[4].astype(jnp.bfloat16), "seq").astype(jnp.float32),
        lax.psum(shards[5].astype(jnp.bfloat16), "seq").astype(jnp.float32),
        lax.psum(shards[6].astype(jnp.bfloat16), "seq").astype(jnp.float32),
        lax.psum(shards[7].astype(jnp.bfloat16), "seq").astype(jnp.float32),
        lax.psum(shards[8].astype(jnp.bfloat16), "seq").astype(jnp.float32),
        lax.psum(shards[9].astype(jnp.bfloat16), "seq").astype(jnp.float32),
        lax.psum(shards[10].astype(jnp.bfloat16), "seq").astype(jnp.float32),
        lax.psum(shards[11].astype(jnp.bfloat16), "seq").astype(jnp.float32),
        lax.psum(shards[12].astype(jnp.bfloat16), "seq").astype(jnp.float32),
    )
    return (
        output,
        grad_tokens,
        summed[0],
        summed[1],
        summed[2],
        summed[3],
        summed[4],
        summed[5],
        summed[6],
        summed[7],
        summed[8],
        summed[9],
        summed[10],
        summed[11],
        summed[12],
    )


def solution(mesh):
    in_specs = (
        P("dp", "seq", None),
        P("dp", "seq", None),
        P("dp", None),
        P("dp", None),
        P("dp", None),
        P("dp", None),
        P("dp"),
        P("dp"),
        P("dp"),
        P("dp"),
        P("dp"),
        P("dp"),
        P("dp"),
        P("dp"),
        P("dp"),
    )
    out_specs = (
        P("dp", "seq", None),
        P("dp", "seq", None),
        P("dp", None),
        P("dp", None),
        P("dp", None),
        P("dp", None),
        P("dp"),
        P("dp"),
        P("dp"),
        P("dp"),
        P("dp"),
        P("dp"),
        P("dp"),
        P("dp"),
        P("dp"),
    )
    return jax.shard_map(
        per_device, mesh=mesh, in_specs=in_specs, out_specs=out_specs, check_vma=False
    )
```

profile of v0, /device:TPU:0, one launch (start us, length us, event | category | flops | bytes accessed | tf_op | source)
XLA Modules:
  0.0 1167.0 jit_solution(419654509652365653)
XLA Ops:
  9.4 22.5 %all-gather.2 = bf16[8,1,128]{2,1,0:T(2,128)(2,1)S(1)} all-gather(bf16[1,1,128]{2,1,0:T(2,128)(2,1)} %bitcast.361), channel_id=1, replica_groups=mesh['dp'=8,'seq'=4] {'dp'}, dimensions={0}, use_global_device_ids=true | all-gather | bytes 2304 | tf_op jit(solution)/shard_map/all_gather | solution.py:182
  31.9 16.7 %all-gather.3 = bf16[8,1,128]{2,1,0:T(2,128)(2,1)S(1)} all-gather(bf16[1,1,128]{2,1,0:T(2,128)(2,1)} %bitcast.362), channel_id=1, replica_groups=mesh['dp'=8,'seq'=4] {'dp'}, dimensions={0}, use_global_device_ids=true | all-gather | bytes 2304 | tf_op jit(solution)/shard_map/all_gather | solution.py:183
  48.6 18.4 %all-gather = bf16[8,1,128]{2,1,0:T(2,128)(2,1)S(1)} all-gather(bf16[1,1,128]{2,1,0:T(2,128)(2,1)} %bitcast.363), channel_id=1, replica_groups=mesh['dp'=8,'seq'=4] {'dp'}, dimensions={0}, use_global_device_ids=true | all-gather | bytes 2304 | tf_op jit(solution)/shard_map/all_gather | solution.py:185
  67.0 16.8 %all-gather.1 = bf16[8,1,128]{2,1,0:T(2,128)(2,1)S(1)} all-gather(bf16[1,1,128]{2,1,0:T(2,128)(2,1)} %bitcast.364), channel_id=1, replica_groups=mesh['dp'=8,'seq'=4] {'dp'}, dimensions={0}, use_global_device_ids=true | all-gather | bytes 2304 | tf_op jit(solution)/shard_map/all_gather | solution.py:186
  87.6 24.5 %all-gather.14.cloned.1.call-done = bf16[1024,3072]{1,0:T(8,128)(2,1)} async-done(((bf16[128,3072]{1,0:T(8,128)(2,1)}), bf16[1024,3072]{1,0:T(8,128)(2,1)}) %all-gather.14.cloned.1.call-update) | async-done | bytes 6291472 | tf_op jit(solution)/shard_map/all_gather | solution.py:178
  140.1 32.1 %all-to-all-done = bf16[1,512,3,4,256]{4,1,2,0,3:T(8,128)(2,1)} async-done(((bf16[1,512,3,4,256]{4,1,2,0,3:T(8,128)(2,1)}), bf16[1,512,3,4,256]{4,1,2,0,3:T(8,128)(2,1)}, u32[]{:S(2)}, u32[]{:S(2)}) %all-to-all-start) | async-done | bytes 3145760 | tf_op jit(solution)/shard_map/all_to_all | solution.py:211
  213.3 10.6 fusion.130
  240.9 12.0 %fusion.136 = bf16[2048,1,1,256]{3,2,1,0:T(2,128)(2,1)S(1)} fusion(bf16[1,512,1,256]{3,2,0,1:T(2,128)(2,1)} %copy.81, bf16[1,512,1,256]{3,2,0,1:T(2,128)(2,1)} %copy.80, bf16[1,512,1,256]{3,2,0,1:T(2,128)(2,1)} %copy.79, bf16[1,512,1,256]{3,2,0,1:T(2,128)(2,1)} %copy.78), kind=kLoop, calls=%fused_computation.202 | loop fusion | flops 1572864 | bytes 2097152
  253.5 12.0 %reduce.64 = bf16[2048,256]{1,0:T(8,128)(2,1)} reduce(bf16[2048,1,1,256]{3,2,1,0:T(2,128)(2,1)S(1)} %fusion.136, bf16[]{:T(256)} %broadcast.497), dimensions={1,2}, to_apply=%fusion.136.reduce_sub_computation | reduce | bytes 2097154
  273.2 17.5 %all-gather.4 = bf16[8,1,128]{2,1,0:T(2,128)(2,1)S(1)} all-gather(bf16[1,1,128]{2,1,0:T(2,128)(2,1)S(1)} %bitcast.365), channel_id=1, replica_groups=mesh['dp'=8,'seq'=4] {'dp'}, dimensions={0}, use_global_device_ids=true | all-gather | bytes 2304 | tf_op jit(solution)/shard_map/all_gather | solution.py:184
  290.7 17.0 %all-gather.5 = bf16[8,1,128]{2,1,0:T(2,128)(2,1)S(1)} all-gather(bf16[1,1,128]{2,1,0:T(2,128)(2,1)S(1)} %bitcast.366), channel_id=1, replica_groups=mesh['dp'=8,'seq'=4] {'dp'}, dimensions={0}, use_global_device_ids=true | all-gather | bytes 2304 | tf_op jit(solution)/shard_map/all_gather | solution.py:187
  307.6 17.8 %all-gather.6 = bf16[8,1,128]{2,1,0:T(2,128)(2,1)S(1)} all-gather(bf16[1,1,128]{2,1,0:T(2,128)(2,1)S(1)} %bitcast.367), channel_id=1, replica_groups=mesh['dp'=8,'seq'=4] {'dp'}, dimensions={0}, use_global_device_ids=true | all-gather | bytes 2304 | tf_op jit(solution)/shard_map/all_gather | solution.py:188
  325.4 26.3 %all-gather.7 = bf16[8,1,512]{2,1,0:T(2,128)(2,1)S(1)} all-gather(bf16[1,1,512]{2,1,0:T(2,128)(2,1)S(1)} %reshape.1084), channel_id=1, replica_groups=mesh['dp'=8,'seq'=4] {'dp'}, dimensions={0}, use_global_device_ids=true | all-gather | bytes 9216 | tf_op jit(solution)/shard_map/all_gather | solution.py:189
  361.5 10.6 fusion.125
  372.2 40.6 %all-gather.20.cloned.1.call-done = bf16[4096,1024]{1,0:T(8,128)(2,1)} async-done(((bf16[512,1024]{1,0:T(8,128)(2,1)}), bf16[4096,1024]{1,0:T(8,128)(2,1)}) %all-gather.20.cloned.1.call-update) | async-done | bytes 8388624 | tf_op jit(solution)/shard_map/all_gather | solution.py:181
  412.8 15.3 %fusion.135 = (bf16[4096]{0:T(1024)(128)(2,1)}, bf16[512,4096]{1,0:T(8,128)(2,1)S(1)}) fusion(bf16[4096,1024]{1,0:T(8,128)(2,1)} %all-gather.20.cloned.1.call-done, bf16[1,512,1024]{2,1,0:T(8,128)(2,1)S(1)} %copy-done.22, f32[512,4096]{1,0:T(8,128)} %fusion.125, f32[4096]{0:T(1024)S(1)} %bitcast.345), kind=kOutput, calls=%fused_computation.201 | convolution fusion | flops 4349489152 | bytes 22044672 | tf_op jit(solution)/shard_map/dot_general | solution.py:32
  448.4 11.7 %all-to-all-done.2 = bf16[1,512,4,256]{3,1,0,2:T(8,128)(2,1)S(1)} async-done(((bf16[1,512,4,256]{3,1,0,2:T(8,128)(2,1)}), bf16[1,512,4,256]{3,1,0,2:T(8,128)(2,1)S(1)}, u32[]{:S(2)}, u32[]{:S(2)}) %all-to-all-start.2) | async-done | bytes 1048608 | tf_op jit(solution)/shard_map/all_to_all | solution.py:240
  479.4 10.7 multiply_reduce_fusion.1
  497.1 9.6 multiply_reduce_fusion
  517.2 9.0 multiply_convert_fusion.2
  533.4 9.2 multiply_convert_fusion.1
  549.5 10.4 multiply_convert_fusion
  598.0 50.7 %all_to_all.60 = bf16[1,2048,3,1,256]{4,2,3,0,1:T(4,128)(2,1)S(1)} all-to-all(bf16[1,2048,3,1,256]{4,2,3,0,1:T(4,128)(2,1)S(1)} %pad_maximum_fusion), channel_id=1, replica_groups=mesh['dp'=8,'seq'=4] {'seq'}, dimensions={1} | all-to-all | bytes 6291456 | tf_op jit(solution)/shard_map/all_to_all | solution.py:242
  661.2 13.3 %convolution_convert_fusion = bf16[4096,1024]{1,0:T(8,128)(2,1)} fusion(bf16[1,512,1024]{2,1,0:T(8,128)(2,1)} %param.36, f32[512,4096]{1,0:T(8,128)} %fusion.125, f32[4096]{0:T(1024)S(1)} %bitcast.346), kind=kOutput, calls=%fused_computation.36 | convolution fusion | flops 4320133120 | bytes 17842176 | tf_op jit(solution)/shard_map/dot_general | solution.py:41
  675.2 10.8 convolution_convert_fusion.1
  688.5 18.7 %all-gather.8 = bf16[8,1,128]{2,1,0:T(2,128)(2,1)S(1)} all-gather(bf16[1,1,128]{2,1,0:T(2,128)(2,1)S(1)} %bitcast.368), channel_id=1, replica_groups=mesh['dp'=8,'seq'=4] {'dp'}, dimensions={0}, use_global_device_ids=true | all-gather | bytes 2304 | tf_op jit(solution)/shard_map/all_gather | solution.py:190
  709.0 13.0 %fusion.66 = bf16[1,512,1024]{2,1,0:T(8,128)(2,1)} fusion(f32[1,512,1024]{2,1,0:T(8,128)} %copy-done.12, bf16[4096,1024]{1,0:T(8,128)(2,1)} %all-gather.20.cloned.1.call-done, f32[1024]{0:T(1024)S(1)} %bitcast.360, f32[512,4096]{1,0:T(8,128)} %fusion.125, f32[4096]{0:T(1024)S(1)} %bitcast.347), kind=kOutput, calls=%fused_computation.97 | convolution fusion | flops 4317511680 | bytes 19943424 | tf_op jit(solution)/shard_map/dot_general | solution.py:28
  722.0 54.5 %reduce-scatter.5.cloned.1.call-done = bf16[128,3072]{1,0:T(8,128)(2,1)} async-done(((bf16[1024,3072]{1,0:T(8,128)(2,1)}), bf16[128,3072]{1,0:T(8,128)(2,1)}) %reduce-scatter.5.cloned.1.call-update) | async-done | bytes 786448 | tf_op jit(solution)/shard_map/reduce_scatter | solution.py:270
  776.5 151.8 %reduce-scatter.11.cloned.1.call-done = bf16[512,1024]{1,0:T(8,128)(2,1)} async-done(((bf16[4096,1024]{1,0:T(8,128)(2,1)}), bf16[512,1024]{1,0:T(8,128)(2,1)}) %reduce-scatter.11.cloned.1.call-update) | async-done | bytes 1048592 | tf_op jit(solution)/shard_map/reduce_scatter | solution.py:279
  928.4 152.1 %reduce-scatter.9.cloned.1.call-done = bf16[128,4096]{1,0:T(8,128)(2,1)} async-done(((bf16[1024,4096]{1,0:T(8,128)(2,1)}), bf16[128,4096]{1,0:T(8,128)(2,1)}) %reduce-scatter.9.cloned.1.call-update) | async-done | bytes 1048592 | tf_op jit(solution)/shard_map/reduce_scatter | solution.py:276
  1080.5 8.9 fusion.60
  1094.8 35.2 %all-reduce.11 = (bf16[1024]{0:T(1024)(128)(2,1)S(1)}, bf16[1024]{0:T(1024)(128)(2,1)S(1)}, bf16[1024]{0:T(1024)(128)(2,1)S(1)}, bf16[1024]{0:T(1024)(128)(2,1)S...) all-reduce(bf16[1024]{0:T(1024)(128)(2,1)S(1)} %bitcast.355, ...), channel_id=6, replica_groups=mesh['dp'=8,'seq'=4] {'dp'}, use_global_device_ids=true, to_apply=%region_29.30.clone | all-reduce | flops 12288 | bytes 49152
  (282 shorter events, 270.2 us)
Async XLA Ops:
  7.2 104.9 %copy-start.6 = (bf16[1,512,1024]{2,1,0:T(8,128)(2,1)S(1)}, bf16[1,512,1024]{2,1,0:T(8,128)(2,1)}, u32[]{:S(2)}) copy-start(bf16[1,512,1024]{2,1,0:T(8,128)(2,1)} %param.35) | copy-start | bytes 3145732
  7.2 104.9 %all-gather.14.cloned.1.call-start = ((), (), s32[]{:S(2)}) async-start(), calls=%async_computation.8 | async-start | bytes 7077888 | tf_op jit(solution)/shard_map/all_gather | solution.py:178
  7.9 349.9 %all-gather.16.cloned.1.call-start = ((), (), s32[]{:S(2)}) async-start(), calls=%async_computation.9 | async-start | bytes 2359296 | tf_op jit(solution)/shard_map/all_gather | solution.py:179
  8.7 352.8 %all-gather.18.cloned.1.call-start = ((), (), s32[]{:S(2)}) async-start(), calls=%async_computation.10 | async-start | bytes 9437184 | tf_op jit(solution)/shard_map/all_gather | solution.py:180
  67.0 52.9 %copy-start.28 = (f32[8,1,128]{2,1,0:T(1,128)}, f32[8,1,128]{2,1,0:T(1,128)S(1)}, u32[]{:S(2)}) copy-start(f32[8,1,128]{2,1,0:T(1,128)S(1)} %convert_element_type.290) | copy-start | bytes 12292
  83.8 36.1 %copy-start.41 = (f32[8,1,128]{2,1,0:T(1,128)}, f32[8,1,128]{2,1,0:T(1,128)S(1)}, u32[]{:S(2)}) copy-start(f32[8,1,128]{2,1,0:T(1,128)S(1)} %convert_element_type.291) | copy-start | bytes 12292
  85.3 34.6 %copy-start.30 = (f32[512]{0:T(512)}, f32[512]{0:T(512)S(1)}, u32[]{:S(2)}) copy-start(f32[512]{0:T(512)S(1)} %broadcast_multiply_fusion.1) | copy-start | bytes 6148
  87.6 32.3 %copy-start.32 = (f32[512]{0:T(512)}, f32[512]{0:T(512)S(1)}, u32[]{:S(2)}) copy-start(f32[512]{0:T(512)S(1)} %fusion.119) | copy-start | bytes 6148
  130.6 41.6 %all-to-all-start = ((bf16[1,512,3,4,256]{4,1,2,0,3:T(8,128)(2,1)}), bf16[1,512,3,4,256]{4,1,2,0,3:T(8,128)(2,1)}, u32[]{:S(2)}, u32[]{:S(2)}) async-start(bf16[1,512,3,4,256]{4,1,2,0,3:T(8,128)(2,1)} %copy.75), calls=%async_computation | async-start | bytes 6291456 | tf_op jit(solution)/shard_map/all_to_all | solution.py:211
  135.2 277.5 %all-gather.20.cloned.1.call-start = ((), (), s32[]{:S(2)}) async-start(), calls=%async_computation.11 | async-start | bytes 9437184 | tf_op jit(solution)/shard_map/all_gather | solution.py:181
  186.8 19.2 %copy-start.16 = (bf16[1,2048,4,64]{1,3,2,0:T(8,128)(2,1)}, bf16[1,2048,4,64]{1,3,2,0:T(8,128)(2,1)S(1)}, u32[]{:S(2)}) copy-start(bf16[1,2048,4,64]{1,3,2,0:T(8,128)(2,1)S(1)} %get-tuple-element.157) | copy-start | bytes 3145732
  252.9 20.3 %copy-start.46 = (bf16[512]{0:T(512)(128)(2,1)S(1)}, bf16[512]{0:T(512)(128)(2,1)}, u32[]{:S(2)}) copy-start(bf16[512]{0:T(512)(128)(2,1)} %param.48) | copy-start | bytes 3076
  252.9 20.3 %copy-start.47 = (bf16[128]{0:T(256)(128)(2,1)S(1)}, bf16[128]{0:T(256)(128)(2,1)}, u32[]{:S(2)}) copy-start(bf16[128]{0:T(256)(128)(2,1)} %param.43) | copy-start | bytes 772
  252.9 37.7 %copy-start.48 = (bf16[128]{0:T(256)(128)(2,1)S(1)}, bf16[128]{0:T(256)(128)(2,1)}, u32[]{:S(2)}) copy-start(bf16[128]{0:T(256)(128)(2,1)} %param.46) | copy-start | bytes 772
  252.9 54.7 %copy-start.49 = (bf16[128]{0:T(256)(128)(2,1)S(1)}, bf16[128]{0:T(256)(128)(2,1)}, u32[]{:S(2)}) copy-start(bf16[128]{0:T(256)(128)(2,1)} %param.47) | copy-start | bytes 772
  268.9 82.9 %all-to-all-start.1 = ((bf16[4,2,65536]{2,1,0:T(2,128)(2,1)}), bf16[4,2,65536]{2,1,0:T(2,128)(2,1)}, u32[]{:S(2)}, u32[]{:S(2)}) async-start(bf16[4,2,65536]{2,1,0:T(2,128)(2,1)} %reshape.1106), calls=%async_computation.1 | async-start | bytes 2097152 | tf_op jit(solution)/shard_map/all_to_all | solution.py:213
  325.4 36.1 %copy-start.43 = (f32[8,1,128]{2,1,0:T(1,128)}, f32[8,1,128]{2,1,0:T(1,128)S(1)}, u32[]{:S(2)}) copy-start(f32[8,1,128]{2,1,0:T(1,128)S(1)} %convert_element_type.296) | copy-start | bytes 12292
  361.1 72.4 %copy-start.12 = (f32[1,512,1024]{2,1,0:T(8,128)}, f32[1,512,1024]{2,1,0:T(8,128)S(1)}, u32[]{:S(2)}) copy-start(f32[1,512,1024]{2,1,0:T(8,128)S(1)} %get-tuple-element.172) | copy-start | bytes 6291460
  361.5 51.3 %copy-start.22 = (bf16[1,512,1024]{2,1,0:T(8,128)(2,1)S(1)}, bf16[1,512,1024]{2,1,0:T(8,128)(2,1)}, u32[]{:S(2)}) copy-start(bf16[1,512,1024]{2,1,0:T(8,128)(2,1)} %param.36) | copy-start | bytes 3145732
  442.1 18.0 %all-to-all-start.2 = ((bf16[1,512,4,256]{3,1,0,2:T(8,128)(2,1)}), bf16[1,512,4,256]{3,1,0,2:T(8,128)(2,1)S(1)}, u32[]{:S(2)}, u32[]{:S(2)}) async-start(bf16[1,512,4,256]{3,1,0,2:T(8,128)(2,1)} %copy.83), calls=%async_computation.2 | async-start | bytes 2097152 | tf_op jit(solution)/shard_map/all_to_all | solution.py:240
  445.6 276.4 %reduce-scatter.7.cloned.1.call-start = ((), (), s32[]{:S(2)}) async-start(), calls=%async_computation.13 | async-start | bytes 2359296 | tf_op jit(solution)/shard_map/reduce_scatter | solution.py:273
  448.3 328.2 %reduce-scatter.5.cloned.1.call-start = ((), (), s32[]{:S(2)}) async-start(), calls=%async_computation.12 | async-start | bytes 7077888 | tf_op jit(solution)/shard_map/reduce_scatter | solution.py:270
  479.3 17.4 %slice-start = ((s8[16777216]{0:T(1024)(128)(4,1)}), s8[4194304]{0:T(1024)(128)(4,1)S(1)}, s32[]{:S(2)}) async-start(s8[16777216]{0:T(1024)(128)(4,1)} %bitcast.317), calls=%async_computation.17 | async-start | bytes 8388608
  479.3 17.4 %slice-start.1 = ((s8[16777216]{0:T(1024)(128)(4,1)}), s8[4194304]{0:T(1024)(128)(4,1)S(1)}, s32[]{:S(2)}) async-start(s8[16777216]{0:T(1024)(128)(4,1)} %bitcast.317), calls=%async_computation.18 | async-start | bytes 8388608
  479.4 17.4 %slice-start.2 = ((s8[16777216]{0:T(1024)(128)(4,1)}), s8[4194304]{0:T(1024)(128)(4,1)S(1)}, s32[]{:S(2)}) async-start(s8[16777216]{0:T(1024)(128)(4,1)} %bitcast.317), calls=%async_computation.19 | async-start | bytes 8388608
  517.2 16.2 %slice-start.4 = ((s8[12582912]{0:T(1024)(128)(4,1)}), s8[4194304]{0:T(1024)(128)(4,1)S(1)}, s32[]{:S(2)}) async-start(s8[12582912]{0:T(1024)(128)(4,1)} %bitcast.319), calls=%async_computation.21 | async-start | bytes 8388608
  660.9 267.4 %reduce-scatter.11.cloned.1.call-start = ((), (), s32[]{:S(2)}) async-start(), calls=%async_computation.15 | async-start | bytes 9437184 | tf_op jit(solution)/shard_map/reduce_scatter | solution.py:279
  674.5 406.0 %reduce-scatter.9.cloned.1.call-start = ((), (), s32[]{:S(2)}) async-start(), calls=%async_computation.14 | async-start | bytes 9437184 | tf_op jit(solution)/shard_map/reduce_scatter | solution.py:276
  686.0 465.3 %all-reduce.16.cloned.1.call-start = ((), (), s32[]{:S(2)}) async-start(), calls=%async_computation.16 | async-start | bytes 6291456 | tf_op jit(solution)/shard_map/psum | solution.py:311
  1089.4 52.4 %copy-start.35 = (f32[512]{0:T(512)S(1)}, f32[512]{0:T(512)}, u32[]{:S(2)}) copy-start(f32[512]{0:T(512)} %copy-done.34) | copy-start | bytes 6148
  1089.9 51.9 %copy-start.7 = (bf16[1,512,1024]{2,1,0:T(8,128)(2,1)S(1)}, bf16[1,512,1024]{2,1,0:T(8,128)(2,1)}, u32[]{:S(2)}) copy-start(bf16[1,512,1024]{2,1,0:T(8,128)(2,1)} %param.35) | copy-start | bytes 3145732
  1089.9 51.9 %copy-start.9 = (f32[1,512,1024]{2,1,0:T(8,128)S(1)}, f32[1,512,1024]{2,1,0:T(8,128)}, u32[]{:S(2)}) copy-start(f32[1,512,1024]{2,1,0:T(8,128)} %copy-done.8) | copy-start | bytes 6291460
  (43 other events, 235.8 us)
Sparse Core Ops, SparseCore 0:
  10.2 101.8 all-gather.13
  114.2 47.4 all-gather.15
  163.9 123.4 all-gather.17
  289.3 123.3 all-gather.19
  449.7 66.2 reduce-scatter.6
  661.1 115.4 reduce-scatter.4
  780.2 148.1 reduce-scatter.10
  932.4 148.0 reduce-scatter.8
  1083.1 68.2 all-reduce.15
where the time goes:
time: 1170 us
  waiting for transfers between devices  475 us (41%)
  blocking collectives  264 us (23%)
  matrix products  212 us (18%)
  other arithmetic  113 us (10%)
  local copies, waits for them, and re-layouts  72.7 us (6%)
  between operations  16.6 us (1%)
  starting transfers between devices  13 us (1%)
    reduce_scatter x1, waiting for transfers between devices, per_device(): lax.psum_scatter(local_grads[2].astype(jnp.bfloat16), 'dp', scatter_dimen...  152 us
    reduce_scatter x1, waiting for transfers between devices, per_device(): lax.psum_scatter(local_grads[3].astype(jnp.bfloat16), 'dp', scatter_dimen...  152 us
    reduce_scatter x1, waiting for transfers between devices, per_device(): lax.psum_scatter(local_grads[0].astype(jnp.bfloat16), 'dp', scatter_dimen...  54.5 us
    all_to_all x1, blocking collectives, per_device(): lax.all_to_all(grad_packed, 'seq', split_axis=1, concat_axis=3, tiled=True)  50.7 us
    all_gather x1, waiting for transfers between devices, per_device(): lax.all_gather(w_proj, 'dp', axis=0, tiled=True)  40.6 us
    dot_general x4, matrix products, weight_grad(): lax.dot_general(left_side, right_side, (((0,), (0,)), ((), ())), preferre...  35.5 us
    unnamed x1, blocking collectives  35.2 us
    dot_general x4, matrix products, matmul(): return jnp.dot(left_side, right_side, preferred_element_type=jnp.float32)  34.7 us
  transfers between devices with their start and end apart: 12, of which 8 were waited for; matrix products, arithmetic and copies ran while one was open for 30% of the time, Pallas kernels for 0%

commit v1 on v0

v1 whole, which is shorter than its diff:
```python
import functools

import jax
import jax.numpy as jnp
from jax import lax
from jax.experimental import pallas as pl
from jax.experimental.pallas import tpu as pltpu
from jax.sharding import PartitionSpec as P

HEAD_DIM = 64
EPSILON = 1e-05
ROOT_COEF = 0.7978845608028654
SCALE = HEAD_DIM ** (-0.5)
BF16 = jnp.bfloat16
F32 = jnp.float32
LOG_ROWS = 8
VMEM_BYTES = 56 * 1024 * 1024


def gelu_tanh(values):
    return (
        0.5 * values * (1.0 + jnp.tanh(ROOT_COEF * (values + 0.044715 * values * values * values)))
    )


def dot_nn(left_side, right_side):
    return lax.dot_general(
        left_side, right_side, (((1,), (0,)), ((), ())), preferred_element_type=F32
    )


def dot_nt(left_side, right_side):
    return lax.dot_general(
        left_side, right_side, (((1,), (1,)), ((), ())), preferred_element_type=F32
    )


def dot_tn(left_side, right_side):
    return lax.dot_general(
        left_side, right_side, (((0,), (0,)), ((), ())), preferred_element_type=F32
    )


def head_lanes(array, head):
    lanes = lax.broadcasted_iota(jnp.int32, array.shape, 1)
    owner = lax.shift_right_logical(lanes, 6)
    return jnp.where(owner == head, array.astype(F32), 0.0)


def attend_kernel(mixed_ref, out_ref, log_ref, *, block, width):
    length = mixed_ref.shape[1]
    heads = width // HEAD_DIM
    step = 2 if heads % 2 == 0 else 1
    for index in range(length // block):
        first, stop = index * block, (index + 1) * block
        query = mixed_ref[0, first:stop, 0:width]
        row_pos = lax.broadcasted_iota(jnp.int32, (block, block), 0)
        col_pos = lax.broadcasted_iota(jnp.int32, (block, block), 1)
        allowed = row_pos >= col_pos
        log_lanes = lax.broadcasted_iota(jnp.int32, (block, 128), 1)

        def one_head(head, carry):
            total, logs = carry
            masked = (head_lanes(query, head) * SCALE).astype(BF16)
            diagonal = dot_nt(masked, mixed_ref[0, first:stop, width : 2 * width])
            diagonal = jnp.where(allowed, diagonal, -1e30)
            largest = jnp.max(diagonal, axis=1, keepdims=True)
            if first:
                scores = dot_nt(masked, mixed_ref[0, 0:first, width : 2 * width])
                largest = jnp.maximum(largest, jnp.max(scores, axis=1, keepdims=True))
            weights = jnp.exp(diagonal - largest)
            row_total = jnp.sum(weights, axis=1, keepdims=True)
            mixed = dot_nn(
                weights.astype(BF16), mixed_ref[0, first:stop, 2 * width : 3 * width]
            )
            if first:
                weights = jnp.exp(scores - largest)
                row_total = row_total + jnp.sum(weights, axis=1, keepdims=True)
                mixed = mixed + dot_nn(
                    weights.astype(BF16), mixed_ref[0, 0:first, 2 * width : 3 * width]
                )
            total = total + head_lanes(mixed * (1.0 / row_total), head)
            logs = jnp.where(log_lanes == head, largest + jnp.log(row_total), logs)
            return (total, logs)

        def some_heads(group, carry):
            for inner in range(step):
                carry = one_head(group * step + inner, carry)
            return carry

        total, logs = lax.fori_loop(
            0,
            heads // step,
            some_heads,
            (jnp.zeros((block, width), F32), jnp.zeros((block, 128), F32)),
        )
        out_ref[0, first:stop, :] = total.astype(BF16)
        log_ref[0, :, first:stop] = jnp.transpose(logs)[0:LOG_ROWS]


def attend(mixed, width):
    seqs, length, _ = mixed.shape
    block = min(256, length)
    return pl.pallas_call(
        functools.partial(attend_kernel, block=block, width=width),
        grid=(seqs,),
        in_specs=[pl.BlockSpec((1, length, 3 * width), lambda s: (s, 0, 0))],
        out_specs=[
            pl.BlockSpec((1, length, width), lambda s: (s, 0, 0)),
            pl.BlockSpec((1, LOG_ROWS, length), lambda s: (s, 0, 0)),
        ],
        out_shape=[
            jax.ShapeDtypeStruct((seqs, length, width), BF16),
            jax.ShapeDtypeStruct((seqs, LOG_ROWS, length), F32),
        ],
        compiler_params=pltpu.CompilerParams(vmem_limit_bytes=VMEM_BYTES),
        cost_estimate=pl.CostEstimate(
            flops=4 * seqs * length * length * width,
            bytes_accessed=8 * seqs * length * width,
            transcendentals=seqs * length * length * width // HEAD_DIM // 2,
        ),
    )(mixed)


def attend_back_kernel(
    mixed_ref,
    out_ref,
    grad_ref,
    log_ref,
    result_ref,
    query_heads,
    key_heads,
    grad_heads,
    grad_query,
    grad_key,
    grad_value,
    inner_rows,
    *,
    block,
    width,
):
    length = mixed_ref.shape[1]
    heads = width // HEAD_DIM
    blocks = length // block
    owner = lax.shift_right_logical(lax.broadcasted_iota(jnp.int32, (LOG_ROWS, width), 1), 6)
    picks = (owner == lax.broadcasted_iota(jnp.int32, (LOG_ROWS, width), 0)).astype(F32)

    def prepare(index, carry):
        rows = pl.ds(pl.multiple_of(index * block, block), block)
        query = mixed_ref[0, rows, 0:width]
        key = mixed_ref[0, rows, width : 2 * width]
        grad = grad_ref[0, rows, :]
        for head in range(heads):
            query_heads[head, rows, :] = (head_lanes(query, head) * SCALE).astype(BF16)
            key_heads[head, rows, :] = head_lanes(key, head).astype(BF16)
            grad_heads[head, rows, :] = head_lanes(grad, head).astype(BF16)
        product = grad.astype(F32) * out_ref[0, rows, :].astype(F32)
        inner_rows[:, rows] = lax.dot_general(
            picks,
            product,
            (((1,), (1,)), ((), ())),
            precision=lax.Precision.HIGHEST,
            preferred_element_type=F32,
        )
        zeros = jnp.zeros((block, width), F32)
        grad_query[rows, :] = zeros
        grad_key[rows, :] = zeros
        grad_value[rows, :] = zeros
        return carry

    lax.fori_loop(0, blocks, prepare, 0)

    def tile(row_block, col_block, on_diagonal):
        rows = pl.ds(pl.multiple_of(row_block * block, block), block)
        cols = pl.ds(pl.multiple_of(col_block * block, block), block)
        key = mixed_ref[0, cols, width : 2 * width]
        value = mixed_ref[0, cols, 2 * width : 3 * width]
        add_query = add_key = add_value = None
        for head in range(heads):
            query = query_heads[head, rows, :]
            grad = grad_heads[head, rows, :]
            probs = jnp.exp(dot_nt(key, query) - log_ref[0, head : head + 1, rows])
            if on_diagonal:
                key_pos = lax.broadcasted_iota(jnp.int32, (block, block), 0)
                row_pos = lax.broadcasted_iota(jnp.int32, (block, block), 1)
                probs = jnp.where(row_pos >= key_pos, probs, 0.0)
            grad_probs = dot_nt(value, grad)
            grad_scores = (probs * (grad_probs - inner_rows[head : head + 1, rows])).astype(BF16)
            one_value = dot_nn(probs.astype(BF16), grad)
            one_key = dot_nn(grad_scores, query)
            one_query = dot_tn(grad_scores, key_heads[head, cols, :])
            add_value = one_value if head == 0 else add_value + one_value
            add_key = one_key if head == 0 else add_key + one_key
            add_query = one_query if head == 0 else add_query + one_query
        grad_value[cols, :] += add_value
        grad_key[cols, :] += add_key
        grad_query[rows, :] += add_query

    def row_step(row_block, carry):
        def col_step(col_block, inner_carry):
            tile(row_block, col_block, False)
            return inner_carry

        lax.fori_loop(0, row_block, col_step, 0)
        tile(row_block, row_block, True)
        return carry

    lax.fori_loop(0, blocks, row_step, 0)

    def finish(index, carry):
        rows = pl.ds(pl.multiple_of(index * block, block), block)
        result_ref[0, rows, 0:width] = (grad_query[rows, :] * SCALE).astype(BF16)
        result_ref[0, rows, width : 2 * width] = grad_key[rows, :].astype(BF16)
        result_ref[0, rows, 2 * width : 3 * width] = grad_value[rows, :].astype(BF16)
        return carry

    lax.fori_loop(0, blocks, finish, 0)


def attend_back(mixed, attended, grad_attended, logs, width):
    seqs, length, _ = mixed.shape
    heads = width // HEAD_DIM
    block = min(256, length)
    return pl.pallas_call(
        functools.partial(attend_back_kernel, block=block, width=width),
        grid=(seqs,),
        in_specs=[
            pl.BlockSpec((1, length, 3 * width), lambda s: (s, 0, 0)),
            pl.BlockSpec((1, length, width), lambda s: (s, 0, 0)),
            pl.BlockSpec((1, length, width), lambda s: (s, 0, 0)),
            pl.BlockSpec((1, LOG_ROWS, length), lambda s: (s, 0, 0)),
        ],
        out_specs=pl.BlockSpec((1, length, 3 * width), lambda s: (s, 0, 0)),
        out_shape=jax.ShapeDtypeStruct((seqs, length, 3 * width), BF16),
        scratch_shapes=[
            pltpu.VMEM((heads, length, width), BF16),
            pltpu.VMEM((heads, length, width), BF16),
            pltpu.VMEM((heads, length, width), BF16),
            pltpu.VMEM((length, width), F32),
            pltpu.VMEM((length, width), F32),
            pltpu.VMEM((length, width), F32),
            pltpu.VMEM((LOG_ROWS, length), F32),
        ],
        compiler_params=pltpu.CompilerParams(vmem_limit_bytes=VMEM_BYTES),
        cost_estimate=pl.CostEstimate(
            flops=10 * seqs * length * length * width,
            bytes_accessed=16 * seqs * length * width,
            transcendentals=seqs * length * length * width // HEAD_DIM // 2,
        ),
    )(mixed, attended, grad_attended, logs)


def swap(array, offset):
    ranks = lax.axis_size("seq")
    return lax.ppermute(array, "seq", [(rank, rank ^ offset) for rank in range(ranks)])


def bits_up():
    ranks, bits, bit = (lax.axis_size("seq"), [], 1)
    while bit < ranks:
        bits.append(bit)
        bit *= 2
    return bits


def gather_offsets(array):
    found = {0: array}
    for bit in reversed(bits_up()):
        for offset in sorted(found):
            found[offset | bit] = swap(found[offset], bit)
    return [found[offset] for offset in range(len(found))]


def reduce_offsets(blocks):
    left = dict(enumerate(blocks))
    for bit in bits_up():
        for offset in sorted(left, reverse=True):
            if offset & bit:
                arrived = swap(left.pop(offset).astype(BF16), bit)
                left[offset ^ bit] = left[offset ^ bit].astype(F32) + arrived.astype(F32)
    return left[0]


def in_rank_order(blocks):
    rank = lax.axis_index("seq")
    stacked = jnp.zeros((len(blocks),) + blocks[0].shape, blocks[0].dtype)
    for offset, block in enumerate(blocks):
        stacked = lax.dynamic_update_index_in_dim(stacked, block, rank ^ offset, 0)
    return stacked


def by_offset(array, axis):
    rank = lax.axis_index("seq")
    ranks = array.shape[axis]
    return [
        lax.dynamic_index_in_dim(array, rank ^ offset, axis, keepdims=False)
        for offset in range(ranks)
    ]


def row_stats(values):
    average = jnp.mean(values, axis=-1, keepdims=True)
    centered = values - average
    variance = jnp.mean(centered * centered, axis=-1, keepdims=True)
    inverse = lax.rsqrt(variance + EPSILON)
    return centered * inverse, inverse


def norm_back(incoming, gain, unit, inverse):
    scaled = incoming * gain
    first = jnp.mean(scaled, axis=-1, keepdims=True)
    second = jnp.mean(scaled * unit, axis=-1, keepdims=True)
    return inverse * (scaled - first - unit * second)


def pad_rows(array, multiple):
    rows = array.shape[0]
    return jnp.pad(array, ((0, -rows % multiple), (0, 0)))


def vector_rows(vectors, parts, columns):
    flat = jnp.concatenate([item.reshape(parts, -1) for item in vectors], axis=1)
    size = flat.shape[1]
    rows = -(-size // columns)
    rows = -(-rows // 16) * 16
    flat = jnp.pad(flat, ((0, 0), (0, rows * columns - size)))
    return flat.reshape(parts, rows, columns)


def per_device(
    tokens,
    cotangent,
    w_qkv,
    w_attn,
    w_fc,
    w_proj,
    bias_query,
    bias_value,
    bias_attn,
    gain_one,
    shift_one,
    gain_two,
    shift_two,
    bias_fc,
    bias_proj,
):
    ranks = lax.axis_size("seq")
    shards = lax.axis_size("dp")
    rank = lax.axis_index("seq")
    seqs, rows, model = tokens.shape
    length = rows * ranks
    width = model // ranks
    part = w_qkv.shape[0]
    hidden_part = w_proj.shape[0]
    units = hidden_part // ranks
    hidden_width = w_fc.shape[1] // ranks
    tokens_own = tokens.reshape(seqs * rows, model)
    cot_own = cotangent.reshape(seqs * rows, model)

    qkv_share = lax.dynamic_index_in_dim(
        w_qkv.reshape(part, 3, ranks, width), rank, 2, keepdims=False
    ).reshape(part, 3 * width)
    vectors = (
        bias_query,
        bias_value,
        bias_attn,
        gain_one,
        shift_one,
        gain_two,
        shift_two,
        bias_proj,
        bias_fc,
    )
    packed = jnp.concatenate([qkv_share, vector_rows(vectors, 1, 3 * width)[0]], axis=0)
    first_gather = lax.all_gather(packed, "dp", axis=0)
    full_qkv = first_gather[:, :part].reshape(model, 3 * width)
    flat_vectors = first_gather[:, part:].reshape(shards, -1).astype(F32)

    def vector(index):
        return flat_vectors[:, index * part : (index + 1) * part].reshape(model)

    query_bias = lax.dynamic_slice_in_dim(vector(0), rank * width, width)
    value_bias = lax.dynamic_slice_in_dim(vector(1), rank * width, width)
    attn_bias = vector(2)
    gain_first, shift_first, gain_second, shift_second, proj_bias = (
        vector(3),
        vector(4),
        vector(5),
        vector(6),
        vector(7),
    )
    fc_bias = lax.dynamic_index_in_dim(
        flat_vectors[:, 8 * part : 8 * part + hidden_part].reshape(shards, ranks, units),
        rank,
        1,
        keepdims=False,
    ).reshape(hidden_width)

    fc_share = lax.dynamic_index_in_dim(
        w_fc.reshape(part, shards, ranks, units), rank, 2, keepdims=False
    ).reshape(part, hidden_width)
    proj_share = lax.dynamic_index_in_dim(
        w_proj.reshape(ranks, units, model), rank, 0, keepdims=False
    ).reshape(part, units * model // part)
    attn_share = lax.dynamic_slice_in_dim(w_attn, rank * width, width, 1)
    second_gather = lax.all_gather(
        jnp.concatenate([attn_share, fc_share, proj_share], axis=1), "dp", axis=0
    )
    attn_columns = second_gather[:, :, :width].reshape(model, width)
    share_fc = second_gather[:, :, width : width + hidden_width].reshape(model, hidden_width)
    share_proj = second_gather[:, :, width + hidden_width :].reshape(hidden_width, model)

    all_tokens = in_rank_order(gather_offsets(tokens)).transpose(1, 0, 2, 3)
    all_tokens = all_tokens.reshape(seqs * length, model)
    cot_blocks = gather_offsets(cot_own)

    unit_all, _ = row_stats(all_tokens.astype(F32))
    normed = (unit_all * gain_first + shift_first).astype(BF16)
    joint_bias = jnp.concatenate([query_bias, jnp.zeros_like(query_bias), value_bias])
    mixed = (dot_nn(normed, full_qkv) + joint_bias).astype(BF16)
    mixed = mixed.reshape(seqs, length, 3 * width)
    attended, logs = attend(mixed, width)

    sent = by_offset(attended.reshape(seqs, ranks, rows, width), 1)
    arrived = [sent[0]] + [swap(sent[offset], offset) for offset in range(1, ranks)]
    joined = in_rank_order(arrived).transpose(1, 2, 0, 3).reshape(seqs * rows, model)
    full_attn = in_rank_order(gather_offsets(attn_columns)).transpose(1, 0, 2)
    full_attn = full_attn.reshape(model, model)

    inputs = tokens_own.astype(F32)
    middle = inputs + (dot_nn(joined, full_attn) + attn_bias)
    unit_two, inverse_two = row_stats(middle)
    normed_two = (unit_two * gain_second + shift_second).astype(BF16)
    all_two = jnp.concatenate(gather_offsets(normed_two), axis=0)
    all_cot = jnp.concatenate(cot_blocks, axis=0)

    hidden = dot_nn(all_two, share_fc) + fc_bias
    active, gelu_pull = jax.vjp(gelu_tanh, hidden)
    active = active.astype(BF16)
    grad_active = dot_nt(all_cot, share_proj)
    grad_hidden = gelu_pull(grad_active)[0].astype(BF16)
    back_two = dot_nt(grad_hidden, share_fc).astype(BF16).reshape(ranks, seqs * rows, model)
    grad_normed_two = reduce_offsets([back_two[offset] for offset in range(ranks)])
    forward_two = dot_nn(active, share_proj).astype(BF16).reshape(ranks, seqs * rows, model)
    projected = reduce_offsets([forward_two[offset] for offset in range(ranks)])
    output = (middle + projected + proj_bias).astype(BF16)

    upstream = cot_own.astype(F32)
    grad_gain_two = jnp.sum(grad_normed_two * unit_two, axis=0)
    grad_shift_two = jnp.sum(grad_normed_two, axis=0)
    grad_middle = upstream + norm_back(grad_normed_two, gain_second, unit_two, inverse_two)
    grad_branch = grad_middle.astype(BF16)
    grad_joined = dot_nt(grad_branch, full_attn).astype(BF16)
    grad_sent = by_offset(grad_joined.reshape(seqs, rows, ranks, width), 2)
    grad_arrived = [grad_sent[0]] + [
        swap(grad_sent[offset], offset) for offset in range(1, ranks)
    ]
    grad_attended = in_rank_order(grad_arrived).transpose(1, 0, 2, 3)
    grad_attended = grad_attended.reshape(seqs, length, width)

    grad_w_proj = dot_tn(active, all_cot).astype(BF16).reshape(shards, units, model)
    grad_w_fc = dot_tn(all_two, grad_hidden).astype(BF16).reshape(shards, part, hidden_width)
    grad_bias_fc = jnp.sum(grad_hidden, axis=0, dtype=F32)
    grad_bias_proj = jnp.sum(upstream, axis=0)
    first_scatter = lax.psum_scatter(
        jnp.concatenate(
            [
                grad_w_fc,
                grad_w_proj.reshape(shards, part, units * model // part),
            ],
            axis=2,
        ),
        "dp",
        scatter_dimension=0,
    )

    grad_attn_part = dot_tn(joined, grad_branch).reshape(model, ranks, width)
    grad_w_attn = reduce_offsets(by_offset(grad_attn_part, 1)).astype(BF16)
    grad_bias_attn = jnp.sum(grad_branch, axis=0, dtype=F32)

    grad_mixed = attend_back(mixed, attended, grad_attended, logs, width)
    grad_mixed = grad_mixed.reshape(seqs * length, 3 * width)
    back_one = dot_nt(grad_mixed, full_qkv).astype(BF16)
    blocks_one = by_offset(back_one.reshape(seqs, ranks, rows, model), 1)
    grad_normed = reduce_offsets(blocks_one).reshape(seqs * rows, model)
    grad_w_qkv = dot_tn(normed, grad_mixed).astype(BF16)
    column_sums = jnp.sum(grad_mixed, axis=0, dtype=F32)
    grad_gain_one = jnp.sum(back_one.astype(F32) * unit_all, axis=0)
    grad_shift_one = jnp.sum(back_one, axis=0, dtype=F32)

    def spread(values):
        return lax.dynamic_update_slice_in_dim(
            jnp.zeros((model,), F32), values, rank * width, 0
        )

    grad_vectors = (
        spread(column_sums[:width]),
        spread(column_sums[2 * width :]),
        grad_bias_attn,
        grad_gain_one,
        grad_shift_one,
        grad_gain_two,
        grad_shift_two,
        grad_bias_proj,
        grad_bias_fc,
    )
    last_columns = 4 * width
    vector_part = vector_rows(grad_vectors, shards, last_columns).astype(BF16)
    last_scatter = lax.psum_scatter(
        jnp.concatenate(
            [
                jnp.concatenate(
                    [
                        grad_w_qkv.reshape(shards, part, 3 * width),
                        grad_w_attn.reshape(shards, part, width),
                    ],
                    axis=2,
                ),
                vector_part,
            ],
            axis=1,
        ),
        "dp",
        scatter_dimension=0,
    )

    unit_one, inverse_one = row_stats(inputs)
    grad_tokens = grad_middle + norm_back(grad_normed, gain_first, unit_one, inverse_one)

    feed = in_rank_order(gather_offsets(first_scatter))
    out_fc = feed[:, :, :hidden_width].reshape(ranks, part, shards, units)
    out_fc = out_fc.transpose(1, 2, 0, 3).reshape(part, w_fc.shape[1]).astype(F32)
    out_proj = feed[:, :, hidden_width:].reshape(hidden_part, model).astype(F32)
    rest = in_rank_order(gather_offsets(last_scatter))
    out_qkv = rest[:, :part, : 3 * width].reshape(ranks, part, 3, width)
    out_qkv = out_qkv.transpose(1, 2, 0, 3).reshape(part, 3 * model).astype(F32)
    out_attn = rest[:, :part, 3 * width :].transpose(1, 0, 2).reshape(part, model).astype(F32)
    out_vectors = rest[:, part:].reshape(ranks, -1).astype(F32)
    summed = jnp.sum(out_vectors[:, : 8 * part], axis=0)
    out_bias_fc = out_vectors[:, 8 * part : 8 * part + units].reshape(hidden_part)

    def out_vector(index):
        return summed[index * part : (index + 1) * part]

    return (
        output.reshape(seqs, rows, model),
        grad_tokens.reshape(seqs, rows, model),
        out_qkv,
        out_attn,
        out_fc,
        out_proj,
        out_vector(0),
        out_vector(1),
        out_vector(2),
        out_vector(3),
        out_vector(4),
        out_vector(5),
        out_vector(6),
        out_bias_fc,
        out_vector(7),
    )


def solution(mesh):
    token_spec = P("dp", "seq", None)
    in_specs = (token_spec,) * 2 + (P("dp", None),) * 4 + (P("dp"),) * 9
    out_specs = (token_spec,) * 2 + (P("dp", None),) * 4 + (P("dp"),) * 9
    return jax.shard_map(
        per_device, mesh=mesh, in_specs=in_specs, out_specs=out_specs, check_vma=False
    )
```

time: 1170 us -> 615 us (0.53)
  blocking collectives: 264 us -> 0 us
  waiting for transfers between devices: 475 us -> 303 us
  matrix products: 212 us -> 73.8 us
  Pallas kernels: 0 us -> 79.4 us
  other arithmetic: 113 us -> 44.3 us
    reduce_scatter x4 -> x2, waiting for transfers between devices: 358 us -> 95.9 us  [the longest x1 79.9 us: per_device(): lax.psum_scatter(jnp.concatenate([grad_w_fc, grad_w_proj.reshape(shards,...]
    all_gather x9 -> x0, blocking collectives: 172 us -> none  [the longest x1 26.3 us: per_device(): lax.all_gather(bias_fc, 'dp', axis=0, tiled=True)]
    ppermute x0 -> x36, waiting for transfers between devices: none -> 154 us  [swap(): lax.ppermute(array, 'seq', [(rank, rank ^ offset) for rank in range(ranks)])]
    dot_general x36 -> x12, matrix products: 212 us -> 73.8 us  [the longest x4 31.6 us: dot_nt(): lax.dot_general(left_side, right_side, (((1,), (1,)), ((), ())), preferre...]
    pallas_call x0 -> x2, Pallas kernels: none -> 79.4 us  [the longest x1 53.6 us: attend_back(): pl.pallas_call(functools.partial(attend_back_kernel, block=block, width=w...]
    all_to_all x1 -> x0, blocking collectives: 50.7 us -> none  [per_device(): lax.all_to_all(grad_packed, 'seq', split_axis=1, concat_axis=3, tiled=True)]
    all_to_all x3 -> x0, waiting for transfers between devices: 43.8 us -> none  [the longest x1 32.1 us: per_device(): lax.all_to_all(packed, 'seq', split_axis=3, concat_axis=1, tiled=True)]
    unnamed x1 -> x0, blocking collectives: 35.2 us -> none
  transfers between devices with their start and end apart: 12 -> 40, of which waited for: 8 -> 18; matrix products, arithmetic and copies ran while one was open for 30% -> 21% of each run, Pallas kernels for 0% -> 13%
where the time goes in v1:
time: 615 us; the launch traced here: 610 us
  waiting for transfers between devices  303 us (49%)
  Pallas kernels  79.4 us (13%)
  matrix products  73.8 us (12%)
  local copies, waits for them, and re-layouts  70.1 us (11%)
  other arithmetic  44.3 us (7%)
  starting transfers between devices  24.6 us (4%)
  between operations  15.3 us (2%)
    ppermute x36, waiting for transfers between devices, swap(): lax.ppermute(array, 'seq', [(rank, rank ^ offset) for rank in range(ranks)])  154 us
    reduce_scatter x1, waiting for transfers between devices, per_device(): lax.psum_scatter(jnp.concatenate([grad_w_fc, grad_w_proj.reshape(shards,...  79.9 us
    pallas_call x1, Pallas kernels, attend_back(): pl.pallas_call(functools.partial(attend_back_kernel, block=block, width=w...  53.6 us
    all_gather x1, waiting for transfers between devices, per_device(): lax.all_gather(jnp.concatenate([attn_share, fc_share, proj_share], axis=1...  39.5 us
    dot_general x4, matrix products, dot_nt(): lax.dot_general(left_side, right_side, (((1,), (1,)), ((), ())), preferre...  31.6 us
    pallas_call x1, Pallas kernels, attend(): pl.pallas_call(functools.partial(attend_kernel, block=block, width=width)...  25.8 us
    dot_general x4, matrix products, dot_tn(): lax.dot_general(left_side, right_side, (((0,), (0,)), ((), ())), preferre...  25.6 us
    ppermute x36, starting transfers between devices, swap(): lax.ppermute(array, 'seq', [(rank, rank ^ offset) for rank in range(ranks)])  24 us
  transfers between devices with their start and end apart: 40, of which 18 were waited for; matrix products, arithmetic and copies ran while one was open for 21% of the time, Pallas kernels for 13%

profile of v1, /device:TPU:0, one launch (start us, length us, event | category | flops | bytes accessed | tf_op | source)
XLA Modules:
  0.0 610.4 jit_solution(836127534637277702)
XLA Ops:
  19.9 3.0 collective-permute-start.1
  23.0 23.2 %collective-permute-done.1 = bf16[1,512,1024]{2,1,0:T(8,128)(2,1)S(1)} collective-permute-done((bf16[1,512,1024]{2,1,0:T(8,128)(2,1)S(1)}, bf16[1,512,1024]{2,1,0:T(8,128)(2,1)S(1)}, u32[]{:S(2)}, u32[]{:S(2)}) %collective-permute-start.1) | collective-permute-done | bytes 1048608 | tf_op jit(solution)/shard_map/ppermute | solution.py:255
  51.7 13.1 %all-gather.5.cloned.1.call-done = bf16[1152,768]{1,0:T(8,128)(2,1)} async-done(((bf16[144,768]{1,0:T(8,128)(2,1)}), bf16[1152,768]{1,0:T(8,128)(2,1)}) %all-gather.5.cloned.1.call-update) | async-done | bytes 1769488 | tf_op jit(solution)/shard_map/all_gather | solution.py:375
  72.6 4.7 fusion.12.mixed_ref
  77.3 25.8 %shard_map.262 = (bf16[1,2048,256]{2,1,0:T(8,128)(2,1)}, f32[1,8,2048]{2,1,0:T(8,128)}) custom-call(bf16[1,2048,768]{2,1,0:T(8,128)(2,1)} %fusion.12.mixed_ref), custom_call_target="tpu_custom_call" | custom-call | flops 4294967296 | bytes 4194304 | tf_op jit(solution)/shard_map/pallas_call | solution.py:104
  108.1 39.5 %all-gather.7.cloned.1.call-done = bf16[1024,2304]{0,1:T(8,128)(2,1)} async-done(((bf16[128,2304]{0,1:T(8,128)(2,1)}), bf16[1024,2304]{0,1:T(8,128)(2,1)}) %all-gather.7.cloned.1.call-update) | async-done | bytes 4718608 | tf_op jit(solution)/shard_map/all_gather | solution.py:406
  147.5 3.6 copy.189
  159.6 7.2 %collective-permute-done.7 = bf16[1024,256]{0,1:T(8,128)(2,1)} collective-permute-done((bf16[1024,256]{0,1:T(8,128)(2,1)S(1)}, bf16[1024,256]{0,1:T(8,128)(2,1)}, u32[]{:S(2)}, u32[]{:S(2)}) %collective-permute-start.7) | collective-permute-done | bytes 524320 | tf_op jit(solution)/shard_map/ppermute | solution.py:255
  174.9 22.8 %collective-permute-done.10 = bf16[512,1024]{1,0:T(8,128)(2,1)S(1)} collective-permute-done((bf16[512,1024]{1,0:T(8,128)(2,1)S(1)}, bf16[512,1024]{1,0:T(8,128)(2,1)S(1)}, u32[]{:S(2)}, u32[]{:S(2)}) %collective-permute-start.10) | collective-permute-done | bytes 1048608 | tf_op jit(solution)/shard_map/ppermute | solution.py:255
  198.2 21.6 %collective-permute-done.16 = bf16[512,1024]{1,0:T(8,128)(2,1)S(1)} collective-permute-done((bf16[512,1024]{1,0:T(8,128)(2,1)S(1)}, bf16[512,1024]{1,0:T(8,128)(2,1)S(1)}, u32[]{:S(2)}, u32[]{:S(2)}) %collective-permute-start.16) | collective-permute-done | bytes 1048608 | tf_op jit(solution)/shard_map/ppermute | solution.py:255
  220.2 4.6 fusion.31
  224.8 16.7 %fusion.67 = (bf16[1024]{0:T(1024)(128)(2,1)S(1)}, bf16[2048,1024]{1,0:T(8,128)(2,1)}) fusion(bf16[128,8,8,128]{3,2,1,0:T(8,128)(2,1)S(1)} %bitcast.355, bf16[512,1024]{1,0:T(8,128)(2,1)S(1)} %collective-permute-done.17, bf16[512,1024]{1,0:T(8,128)(2,1)S(1)} %collective-permute-done.16, bf16[512,1024]{1,0:T(8,128)(2,1)S(1)} %collective-permute-done.15, ...), kind=kOutput, calls=%fused_computation.200 | convolution fusion | flops 4366269440 | bytes 18880512 | tf_op jit(solution)/shard_map/dot_general | solution.py:33
  241.5 7.0 %convolution_convert_fusion.1 = bf16[2048,1024]{1,0:T(8,128)(2,1)S(1)} fusion(bf16[2048,1024]{1,0:T(8,128)(2,1)} %get-tuple-element.147, bf16[128,8,8,128]{3,2,1,0:T(8,128)(2,1)S(1)} %bitcast.358), kind=kOutput, calls=%fused_computation.24 | convolution fusion | flops 4297064448 | bytes 10485760 | tf_op jit(solution)/shard_map/dot_general | solution.py:33
  250.3 5.9 convolution_convert_fusion.2
  265.7 20.0 %collective-permute-done.20 = bf16[512,1024]{1,0:T(8,128)(2,1)} collective-permute-done((bf16[512,1024]{1,0:T(8,128)(2,1)}, bf16[512,1024]{1,0:T(8,128)(2,1)}, u32[]{:S(2)}, u32[]{:S(2)}) %collective-permute-start.20) | collective-permute-done | bytes 1048608 | tf_op jit(solution)/shard_map/ppermute | solution.py:255
  288.5 18.8 %collective-permute-done.14 = bf16[512,1024]{1,0:T(8,128)(2,1)} collective-permute-done((bf16[512,1024]{1,0:T(8,128)(2,1)}, bf16[512,1024]{1,0:T(8,128)(2,1)}, u32[]{:S(2)}, u32[]{:S(2)}) %collective-permute-start.14) | collective-permute-done | bytes 1048608 | tf_op jit(solution)/shard_map/ppermute | solution.py:255
  307.3 4.4 convert_bitcast_fusion.4
  326.6 3.8 collective-permute-done.23
  332.4 53.6 %shard_map.263 = bf16[1,2048,768]{2,1,0:T(8,128)(2,1)} custom-call(bf16[1,2048,768]{2,1,0:T(8,128)(2,1)} %fusion.12.mixed_ref, bf16[1,2048,256]{2,1,0:T(8,128)(2,1)} %get-tuple-element.17.out_ref, bf16[1,2048,256]{2,1,0:T(8,128)(2,1)} %bitcast.374, f32[1,8,2048]{2,1,0:T(8,128)} %get-tuple-element.18.log_ref), custom_call_target="tpu_custom_call" | custom-call | flops 10737418240 | bytes 8388608 | tf_op jit(solution)/shard_map/pallas_call | solution.py:224
  388.8 6.6 %fusion.8 = (bf16[1024]{0:T(1024)(128)(2,1)S(1)}, bf16[2048,1024]{1,0:T(8,128)(2,1)}) fusion(bf16[4,1,512,1024]{3,2,0,1:T(8,128)(2,1)S(1)} %copy-done.4, f32[2048]{0:T(1024)S(1)} %bitcast.392, f32[2048]{0:T(1024)S(1)} %bitcast.393, bf16[1024,768]{1,0:T(8,128)(2,1)} %bitcast.365, bf16[1,2048,768]{2,1,0:T(8,128)(2,1)S(1)} %copy-done.20), kind=kOutput, calls=%fused_computation.13 | convolution fusion | flops 3235904512 | bytes 13125632 | tf_op jit(solution)/shard_map/dot_general | solution.py:33
  395.5 2.9 reduce.6
  401.7 5.7 fusion.41
  407.4 6.8 %collective-permute-done.29 = bf16[1024,256]{1,0:T(8,128)(2,1)S(1)} collective-permute-done((bf16[1024,256]{1,0:T(8,128)(2,1)S(1)}, bf16[1024,256]{1,0:T(8,128)(2,1)S(1)}, u32[]{:S(2)}, u32[]{:S(2)}) %collective-permute-start.29) | collective-permute-done | bytes 524320 | tf_op jit(solution)/shard_map/ppermute | solution.py:255
  418.1 7.9 %convolution_convert_fusion.4 = bf16[1024,1024]{1,0:T(8,128)(2,1)S(1)} fusion(bf16[2048,1024]{1,0:T(8,128)(2,1)} %get-tuple-element.147, bf16[512,1024]{1,0:T(8,128)(2,1)} %copy-done.44, bf16[512,1024]{1,0:T(8,128)(2,1)} %copy-done.42, bf16[512,1024]{1,0:T(8,128)(2,1)} %copy-done.43, bf16[512,1024]{1,0:T(8,128)(2,1)S(1)} %copy-done.27), kind=kOutput, calls=%fused_computation.69 | convolution fusion | flops 4312793088 | bytes 10485760 | tf_op jit(solution)/shard_map/dot_general | solution.py:39
  426.0 9.5 %convolution_convert_fusion.3 = bf16[1024,1024]{1,0:T(8,128)(2,1)S(1)} fusion(bf16[512,1024]{1,0:T(8,128)(2,1)S(1)} %copy-done.48, bf16[512,1024]{1,0:T(8,128)(2,1)S(1)} %copy-done.41, bf16[512,1024]{1,0:T(8,128)(2,1)S(1)} %copy-done.46, bf16[512,1024]{1,0:T(8,128)(2,1)S(1)} %bitcast.350, f32[2048,1024]{1,0:T(8,128)} %copy-done.49, f32[1024]{0:T(1024)S(1)} %fusion.52), kind=kOutput, calls=%fused_computation.68 | convolution fusion | flops 4333764608 | bytes 14684160 | tf_op jit(solution)/shard_map/dot_general | solution.py:39
  445.3 22.9 %collective-permute-done.26 = bf16[1,512,1024]{2,1,0:T(8,128)(2,1)S(1)} collective-permute-done((bf16[1,512,1024]{2,1,0:T(8,128)(2,1)S(1)}, bf16[1,512,1024]{2,1,0:T(8,128)(2,1)S(1)}, u32[]{:S(2)}, u32[]{:S(2)}) %collective-permute-start.26) | collective-permute-done | bytes 1048608 | tf_op jit(solution)/shard_map/ppermute | solution.py:255
  469.4 16.1 %reduce-scatter.3.cloned.1.call-done = bf16[1,144,1024]{2,1,0:T(8,128)(2,1)} async-done(((bf16[8,144,1024]{2,1,0:T(8,128)(2,1)}), bf16[1,144,1024]{2,1,0:T(8,128)(2,1)}) %reduce-scatter.3.cloned.1.call-update) | async-done | bytes 294928 | tf_op jit(solution)/shard_map/reduce_scatter | solution.py:509
  487.0 4.2 fusion.23
  491.3 3.9 collective-permute-done.31
  496.3 79.9 %reduce-scatter.5.cloned.1.call-done = bf16[1,128,2048]{2,1,0:T(8,128)(2,1)} async-done(((bf16[8,128,2048]{2,1,0:T(8,128)(2,1)}), bf16[1,128,2048]{2,1,0:T(8,128)(2,1)}) %reduce-scatter.5.cloned.1.call-update) | async-done | bytes 524304 | tf_op jit(solution)/shard_map/reduce_scatter | solution.py:465
  582.1 3.0 copy.174
  587.8 3.0 copy.178
  (316 shorter events, 123.5 us)
Async XLA Ops:
  7.2 57.7 %all-gather.5.cloned.1.call-start = ((), (), s32[]{:S(2)}) async-start(), calls=%async_computation.4 | async-start | bytes 1990656 | tf_op jit(solution)/shard_map/all_gather | solution.py:375
  16.1 131.4 %all-gather.7.cloned.1.call-start = ((), (), s32[]{:S(2)}) async-start(), calls=%async_computation.5 | async-start | bytes 5308416 | tf_op jit(solution)/shard_map/all_gather | solution.py:406
  19.9 465.6 %reduce-scatter.3.cloned.1.call-start = ((), (), s32[]{:S(2)}) async-start(), calls=%async_computation.2 | async-start | bytes 2654208 | tf_op jit(solution)/shard_map/reduce_scatter | solution.py:509
  19.9 26.2 %collective-permute-start.1 = (bf16[1,512,1024]{2,1,0:T(8,128)(2,1)S(1)}, bf16[1,512,1024]{2,1,0:T(8,128)(2,1)S(1)}, u32[]{:S(2)}, u32[]{:S(2)}) collective-permute-start(bf16[1,512,1024]{2,1,0:T(8,128)(2,1)S(1)} %copy-done.5), channel_id=1, source_target_pairs={{0,2},{1,3},{2,0},{3,1},{4,6},{5,7},{6,4},{7,5},{8,10},{9,11},{10,... | collective-permute-start | bytes 3145736 | tf_op jit(solution)/shard_map/ppermute | solution.py:255
  22.9 23.8 %collective-permute-start = (bf16[1,512,1024]{2,1,0:T(8,128)(2,1)S(1)}, bf16[1,512,1024]{2,1,0:T(8,128)(2,1)}, u32[]{:S(2)}, u32[]{:S(2)}) collective-permute-start(bf16[1,512,1024]{2,1,0:T(8,128)(2,1)S(1)} %copy-done.5), channel_id=1, source_target_pairs={{0,1},{1,0},{2,3},{3,2},{4,5},{5,4},{6,7},{7,6},{8,9},{9,8},{10,11... | collective-permute-start | bytes 3145736 | tf_op jit(solution)/shard_map/ppermute | solution.py:255
  105.1 49.8 %collective-permute-start.3 = (bf16[1,512,256]{2,1,0:T(8,128)(2,1)}, bf16[1,512,256]{2,1,0:T(8,128)(2,1)}, u32[]{:S(2)}, u32[]{:S(2)}) collective-permute-start(bf16[1,512,256]{2,1,0:T(8,128)(2,1)} %get-tuple-element.121), channel_id=1, source_target_pairs={{0,1},{1,0},{2,3},{3,2},{4,5},{5,4},{6,7},{7,6},{8,9},{9,8},{10,11... | collective-permute-start | bytes 786440 | tf_op jit(solution)/shard_map/ppermute | solution.py:255
  105.1 50.9 %collective-permute-start.4 = (bf16[1,512,256]{2,1,0:T(8,128)(2,1)}, bf16[1,512,256]{2,1,0:T(8,128)(2,1)}, u32[]{:S(2)}, u32[]{:S(2)}) collective-permute-start(bf16[1,512,256]{2,1,0:T(8,128)(2,1)} %get-tuple-element.120), channel_id=1, source_target_pairs={{0,2},{1,3},{2,0},{3,1},{4,6},{5,7},{6,4},{7,5},{8,10},{9,11},{10,... | collective-permute-start | bytes 786440 | tf_op jit(solution)/shard_map/ppermute | solution.py:255
  106.6 50.4 %collective-permute-start.5 = (bf16[1,512,256]{2,1,0:T(8,128)(2,1)}, bf16[1,512,256]{2,1,0:T(8,128)(2,1)}, u32[]{:S(2)}, u32[]{:S(2)}) collective-permute-start(bf16[1,512,256]{2,1,0:T(8,128)(2,1)} %get-tuple-element.119), channel_id=1, source_target_pairs={{0,3},{1,2},{2,1},{3,0},{4,7},{5,6},{6,5},{7,4},{8,11},{9,10},{10,... | collective-permute-start | bytes 786440 | tf_op jit(solution)/shard_map/ppermute | solution.py:255
  153.4 13.4 %collective-permute-start.7 = (bf16[1024,256]{0,1:T(8,128)(2,1)S(1)}, bf16[1024,256]{0,1:T(8,128)(2,1)}, u32[]{:S(2)}, u32[]{:S(2)}) collective-permute-start(bf16[1024,256]{0,1:T(8,128)(2,1)S(1)} %bitcast.379), channel_id=1, source_target_pairs={{0,2},{1,3},{2,0},{3,1},{4,6},{5,7},{6,4},{7,5},{8,10},{9,11},{10,... | collective-permute-start | bytes 1572872 | tf_op jit(solution)/shard_map/ppermute | solution.py:255
  156.0 11.2 %collective-permute-start.6 = (bf16[1024,256]{0,1:T(8,128)(2,1)S(1)}, bf16[1024,256]{0,1:T(8,128)(2,1)}, u32[]{:S(2)}, u32[]{:S(2)}) collective-permute-start(bf16[1024,256]{0,1:T(8,128)(2,1)S(1)} %bitcast.380), channel_id=1, source_target_pairs={{0,1},{1,0},{2,3},{3,2},{4,5},{5,4},{6,7},{7,6},{8,9},{9,8},{10,11... | collective-permute-start | bytes 1572872 | tf_op jit(solution)/shard_map/ppermute | solution.py:255
  171.7 26.0 %collective-permute-start.10 = (bf16[512,1024]{1,0:T(8,128)(2,1)S(1)}, bf16[512,1024]{1,0:T(8,128)(2,1)S(1)}, u32[]{:S(2)}, u32[]{:S(2)}) collective-permute-start(bf16[512,1024]{1,0:T(8,128)(2,1)S(1)} %add_convert_fusion.5), channel_id=1, source_target_pairs={{0,2},{1,3},{2,0},{3,1},{4,6},{5,7},{6,4},{7,5},{8,10},{9,11},{10,... | collective-permute-start | bytes 3145736 | tf_op jit(solution)/shard_map/ppermute | solution.py:255
  173.3 46.5 %collective-permute-start.16 = (bf16[512,1024]{1,0:T(8,128)(2,1)S(1)}, bf16[512,1024]{1,0:T(8,128)(2,1)S(1)}, u32[]{:S(2)}, u32[]{:S(2)}) collective-permute-start(bf16[512,1024]{1,0:T(8,128)(2,1)S(1)} %bitcast.347), channel_id=1, source_target_pairs={{0,2},{1,3},{2,0},{3,1},{4,6},{5,7},{6,4},{7,5},{8,10},{9,11},{10,... | collective-permute-start | bytes 3145736 | tf_op jit(solution)/shard_map/ppermute | solution.py:255
  174.7 45.4 %collective-permute-start.9 = (bf16[512,1024]{1,0:T(8,128)(2,1)S(1)}, bf16[512,1024]{1,0:T(8,128)(2,1)S(1)}, u32[]{:S(2)}, u32[]{:S(2)}) collective-permute-start(bf16[512,1024]{1,0:T(8,128)(2,1)S(1)} %add_convert_fusion.5), channel_id=1, source_target_pairs={{0,1},{1,0},{2,3},{3,2},{4,5},{5,4},{6,7},{7,6},{8,9},{9,8},{10,11... | collective-permute-start | bytes 3145736 | tf_op jit(solution)/shard_map/ppermute | solution.py:255
  197.7 22.4 %collective-permute-start.11 = (bf16[512,1024]{1,0:T(8,128)(2,1)S(1)}, bf16[512,1024]{1,0:T(8,128)(2,1)S(1)}, u32[]{:S(2)}, u32[]{:S(2)}) collective-permute-start(bf16[512,1024]{1,0:T(8,128)(2,1)S(1)} %collective-permute-done.10), channel_id=1, source_target_pairs={{0,1},{1,0},{2,3},{3,2},{4,5},{5,4},{6,7},{7,6},{8,9},{9,8},{10,11... | collective-permute-start | bytes 3145736 | tf_op jit(solution)/shard_map/ppermute | solution.py:255
  197.7 27.1 %collective-permute-start.15 = (bf16[512,1024]{1,0:T(8,128)(2,1)S(1)}, bf16[512,1024]{1,0:T(8,128)(2,1)S(1)}, u32[]{:S(2)}, u32[]{:S(2)}) collective-permute-start(bf16[512,1024]{1,0:T(8,128)(2,1)S(1)} %bitcast.348), channel_id=1, source_target_pairs={{0,1},{1,0},{2,3},{3,2},{4,5},{5,4},{6,7},{7,6},{8,9},{9,8},{10,11... | collective-permute-start | bytes 3145736 | tf_op jit(solution)/shard_map/ppermute | solution.py:255
  249.9 8.2 %collective-permute-start.19 = (bf16[512,1024]{1,0:T(8,128)(2,1)S(1)}, bf16[512,1024]{1,0:T(8,128)(2,1)S(1)}, u32[]{:S(2)}, u32[]{:S(2)}) collective-permute-start(bf16[512,1024]{1,0:T(8,128)(2,1)S(1)} %get-tuple-element.109), channel_id=1, source_target_pairs={{0,1},{1,0},{2,3},{3,2},{4,5},{5,4},{6,7},{7,6},{8,9},{9,8},{10,11... | collective-permute-start | bytes 3145736 | tf_op jit(solution)/shard_map/ppermute | solution.py:255
  257.5 8.2 %collective-permute-start.18 = (bf16[512,1024]{1,0:T(8,128)(2,1)}, bf16[512,1024]{1,0:T(8,128)(2,1)S(1)}, u32[]{:S(2)}, u32[]{:S(2)}) collective-permute-start(bf16[512,1024]{1,0:T(8,128)(2,1)} %get-tuple-element.108), channel_id=1, source_target_pairs={{0,1},{1,0},{2,3},{3,2},{4,5},{5,4},{6,7},{7,6},{8,9},{9,8},{10,11... | collective-permute-start | bytes 3145736 | tf_op jit(solution)/shard_map/ppermute | solution.py:255
  259.4 26.3 %collective-permute-start.20 = (bf16[512,1024]{1,0:T(8,128)(2,1)}, bf16[512,1024]{1,0:T(8,128)(2,1)}, u32[]{:S(2)}, u32[]{:S(2)}) collective-permute-start(bf16[512,1024]{1,0:T(8,128)(2,1)} %add_convert_fusion.2), channel_id=1, source_target_pairs={{0,2},{1,3},{2,0},{3,1},{4,6},{5,7},{6,4},{7,5},{8,10},{9,11},{10,... | collective-permute-start | bytes 3145736 | tf_op jit(solution)/shard_map/ppermute | solution.py:255
  261.0 27.5 %collective-permute-start.12 = (bf16[512,1024]{1,0:T(8,128)(2,1)}, bf16[512,1024]{1,0:T(8,128)(2,1)}, u32[]{:S(2)}, u32[]{:S(2)}) collective-permute-start(bf16[512,1024]{1,0:T(8,128)(2,1)} %get-tuple-element.110), channel_id=1, source_target_pairs={{0,1},{1,0},{2,3},{3,2},{4,5},{5,4},{6,7},{7,6},{8,9},{9,8},{10,11... | collective-permute-start | bytes 3145736 | tf_op jit(solution)/shard_map/ppermute | solution.py:255
  262.7 44.5 %collective-permute-start.14 = (bf16[512,1024]{1,0:T(8,128)(2,1)}, bf16[512,1024]{1,0:T(8,128)(2,1)}, u32[]{:S(2)}, u32[]{:S(2)}) collective-permute-start(bf16[512,1024]{1,0:T(8,128)(2,1)} %add_convert_fusion.4), channel_id=1, source_target_pairs={{0,2},{1,3},{2,0},{3,1},{4,6},{5,7},{6,4},{7,5},{8,10},{9,11},{10,... | collective-permute-start | bytes 3145736 | tf_op jit(solution)/shard_map/ppermute | solution.py:255
  316.4 9.3 %collective-permute-start.22 = (bf16[1,512,256]{2,1,0:T(8,128)(2,1)S(1)}, bf16[1,512,256]{2,1,0:T(8,128)(2,1)}, u32[]{:S(2)}, u32[]{:S(2)}) collective-permute-start(bf16[1,512,256]{2,1,0:T(8,128)(2,1)S(1)} %bitcast.390), channel_id=1, source_target_pairs={{0,2},{1,3},{2,0},{3,1},{4,6},{5,7},{6,4},{7,5},{8,10},{9,11},{10,... | collective-permute-start | bytes 786440 | tf_op jit(solution)/shard_map/ppermute | solution.py:255
  318.0 12.4 %collective-permute-start.23 = (bf16[1,512,256]{2,1,0:T(8,128)(2,1)S(1)}, bf16[1,512,256]{2,1,0:T(8,128)(2,1)}, u32[]{:S(2)}, u32[]{:S(2)}) collective-permute-start(bf16[1,512,256]{2,1,0:T(8,128)(2,1)S(1)} %bitcast.389), channel_id=1, source_target_pairs={{0,3},{1,2},{2,1},{3,0},{4,7},{5,6},{6,5},{7,4},{8,11},{9,10},{10,... | collective-permute-start | bytes 786440 | tf_op jit(solution)/shard_map/ppermute | solution.py:255
  323.7 74.9 %collective-permute-start.28 = (bf16[1024,256]{1,0:T(8,128)(2,1)}, bf16[1024,256]{1,0:T(8,128)(2,1)}, u32[]{:S(2)}, u32[]{:S(2)}) collective-permute-start(bf16[1024,256]{1,0:T(8,128)(2,1)} %get-tuple-element.105), channel_id=1, source_target_pairs={{0,1},{1,0},{2,3},{3,2},{4,5},{5,4},{6,7},{7,6},{8,9},{9,8},{10,11... | collective-permute-start | bytes 1572872 | tf_op jit(solution)/shard_map/ppermute | solution.py:255
  324.0 83.4 %collective-permute-start.27 = (bf16[1024,256]{1,0:T(8,128)(2,1)}, bf16[1024,256]{1,0:T(8,128)(2,1)}, u32[]{:S(2)}, u32[]{:S(2)}) collective-permute-start(bf16[1024,256]{1,0:T(8,128)(2,1)} %get-tuple-element.104), channel_id=1, source_target_pairs={{0,1},{1,0},{2,3},{3,2},{4,5},{5,4},{6,7},{7,6},{8,9},{9,8},{10,11... | collective-permute-start | bytes 1572872 | tf_op jit(solution)/shard_map/ppermute | solution.py:255
  400.1 14.1 %collective-permute-start.29 = (bf16[1024,256]{1,0:T(8,128)(2,1)S(1)}, bf16[1024,256]{1,0:T(8,128)(2,1)S(1)}, u32[]{:S(2)}, u32[]{:S(2)}) collective-permute-start(bf16[1024,256]{1,0:T(8,128)(2,1)S(1)} %fusion.45), channel_id=1, source_target_pairs={{0,2},{1,3},{2,0},{3,1},{4,6},{5,7},{6,4},{7,5},{8,10},{9,11},{10,... | collective-permute-start | bytes 1572872 | tf_op jit(solution)/shard_map/ppermute | solution.py:255
  417.6 158.6 %reduce-scatter.5.cloned.1.call-start = ((), (), s32[]{:S(2)}) async-start(), calls=%async_computation.3 | async-start | bytes 4718592 | tf_op jit(solution)/shard_map/reduce_scatter | solution.py:465
  443.0 25.3 %collective-permute-start.26 = (bf16[1,512,1024]{2,1,0:T(8,128)(2,1)S(1)}, bf16[1,512,1024]{2,1,0:T(8,128)(2,1)S(1)}, u32[]{:S(2)}, u32[]{:S(2)}) collective-permute-start(bf16[1,512,1024]{2,1,0:T(8,128)(2,1)S(1)} %fusion.33), channel_id=1, source_target_pairs={{0,2},{1,3},{2,0},{3,1},{4,6},{5,7},{6,4},{7,5},{8,10},{9,11},{10,... | collective-permute-start | bytes 3145736 | tf_op jit(solution)/shard_map/ppermute | solution.py:255
  485.5 9.7 %collective-permute-start.30 = (bf16[144,1024]{1,0:T(8,128)(2,1)}, bf16[144,1024]{1,0:T(8,128)(2,1)S(1)}, u32[]{:S(2)}, u32[]{:S(2)}) collective-permute-start(bf16[144,1024]{1,0:T(8,128)(2,1)} %bitcast.387), channel_id=1, source_target_pairs={{0,1},{1,0},{2,3},{3,2},{4,5},{5,4},{6,7},{7,6},{8,9},{9,8},{10,11... | collective-permute-start | bytes 884744 | tf_op jit(solution)/shard_map/ppermute | solution.py:255
  485.5 9.7 %collective-permute-start.31 = (bf16[144,1024]{1,0:T(8,128)(2,1)}, bf16[144,1024]{1,0:T(8,128)(2,1)}, u32[]{:S(2)}, u32[]{:S(2)}) collective-permute-start(bf16[144,1024]{1,0:T(8,128)(2,1)} %bitcast.388), channel_id=1, source_target_pairs={{0,2},{1,3},{2,0},{3,1},{4,6},{5,7},{6,4},{7,5},{8,10},{9,11},{10,... | collective-permute-start | bytes 884744 | tf_op jit(solution)/shard_map/ppermute | solution.py:255
  495.2 83.7 %collective-permute-start.32 = (bf16[144,1024]{1,0:T(8,128)(2,1)}, bf16[144,1024]{1,0:T(8,128)(2,1)}, u32[]{:S(2)}, u32[]{:S(2)}) collective-permute-start(bf16[144,1024]{1,0:T(8,128)(2,1)} %collective-permute-done.31), channel_id=1, source_target_pairs={{0,1},{1,0},{2,3},{3,2},{4,5},{5,4},{6,7},{7,6},{8,9},{9,8},{10,11... | collective-permute-start | bytes 884744 | tf_op jit(solution)/shard_map/ppermute | solution.py:255
  576.1 17.5 %collective-permute-start.33 = (bf16[128,2048]{1,0:T(8,128)(2,1)}, bf16[128,2048]{1,0:T(8,128)(2,1)}, u32[]{:S(2)}, u32[]{:S(2)}) collective-permute-start(bf16[128,2048]{1,0:T(8,128)(2,1)} %bitcast.381), channel_id=1, source_target_pairs={{0,1},{1,0},{2,3},{3,2},{4,5},{5,4},{6,7},{7,6},{8,9},{9,8},{10,11... | collective-permute-start | bytes 1572872 | tf_op jit(solution)/shard_map/ppermute | solution.py:255
  576.1 17.2 %collective-permute-start.34 = (bf16[128,2048]{1,0:T(8,128)(2,1)}, bf16[128,2048]{1,0:T(8,128)(2,1)}, u32[]{:S(2)}, u32[]{:S(2)}) collective-permute-start(bf16[128,2048]{1,0:T(8,128)(2,1)} %bitcast.382), channel_id=1, source_target_pairs={{0,2},{1,3},{2,0},{3,1},{4,6},{5,7},{6,4},{7,5},{8,10},{9,11},{10,... | collective-permute-start | bytes 1572872 | tf_op jit(solution)/shard_map/ppermute | solution.py:255
  (60 other events, 763.9 us)
Sparse Core Ops, SparseCore 0:
  16.2 48.6 all-gather.4
  67.5 80.0 all-gather.6
  417.7 67.7 reduce-scatter.2
  489.0 87.1 reduce-scatter.4

commit v2 on v1

--- a/solution.py
+++ b/solution.py
@@ -50,7 +50,7 @@
 def attend_kernel(mixed_ref, out_ref, log_ref, *, block, width):
     length = mixed_ref.shape[1]
     heads = width // HEAD_DIM
-    step = 2 if heads % 2 == 0 else 1
+    step = 4 if heads % 4 == 0 else 1
     for index in range(length // block):
         first, stop = index * block, (index + 1) * block
         query = mixed_ref[0, first:stop, 0:width]
@@ -115,7 +115,7 @@
         ],
         compiler_params=pltpu.CompilerParams(vmem_limit_bytes=VMEM_BYTES),
         cost_estimate=pl.CostEstimate(
-            flops=4 * seqs * length * length * width,
+            flops=28 * seqs * length * length * width,
             bytes_accessed=8 * seqs * length * width,
             transcendentals=seqs * length * length * width // HEAD_DIM // 2,
         ),
@@ -220,7 +220,7 @@
 def attend_back(mixed, attended, grad_attended, logs, width):
     seqs, length, _ = mixed.shape
     heads = width // HEAD_DIM
-    block = min(256, length)
+    block = min(512, length)
     return pl.pallas_call(
         functools.partial(attend_back_kernel, block=block, width=width),
         grid=(seqs,),
@@ -243,11 +243,157 @@
         ],
         compiler_params=pltpu.CompilerParams(vmem_limit_bytes=VMEM_BYTES),
         cost_estimate=pl.CostEstimate(
-            flops=10 * seqs * length * length * width,
+            flops=56 * seqs * length * length * width,
             bytes_accessed=16 * seqs * length * width,
             transcendentals=seqs * length * length * width // HEAD_DIM // 2,
         ),
     )(mixed, attended, grad_attended, logs)
+
+
+def feed_kernel(
+    normed_ref,
+    cot_ref,
+    fc_ref,
+    proj_ref,
+    bias_ref,
+    active_ref,
+    grad_ref,
+    back_ref,
+    ahead_ref,
+    sum_ref,
+):
+    hidden = dot_nn(normed_ref[...], fc_ref[...]) + bias_ref[...]
+    grad_active = dot_nt(cot_ref[...], proj_ref[...])
+    square = hidden * hidden
+    curve = jnp.tanh(ROOT_COEF * hidden * (1.0 + 0.044715 * square))
+    half = 0.5 + 0.5 * curve
+    active = (hidden * half).astype(BF16)
+    slope = half + hidden * (0.5 - 0.5 * curve * curve) * (
+        ROOT_COEF + (3.0 * 0.044715 * ROOT_COEF) * square
+    )
+    grad = (grad_active * slope).astype(BF16)
+    active_ref[...] = active
+    grad_ref[...] = grad
+    back_ref[...] = dot_nt(grad, fc_ref[...]).astype(BF16)
+    ahead_ref[...] = dot_nn(active, proj_ref[...]).astype(BF16)
+    sums = jnp.sum(grad.astype(F32), axis=0, keepdims=True)
+
+    @pl.when(pl.program_id(0) == 0)
+    def _():
+        sum_ref[...] = jnp.zeros_like(sum_ref)
+
+    sum_ref[...] += sums
+
+
+def feed(normed, cotangent, share_fc, share_proj, bias):
+    rows, model = normed.shape
+    width = share_fc.shape[1]
+    block = min(256, rows)
+    row_spec = pl.BlockSpec((block, model), lambda i: (i, 0))
+    wide_spec = pl.BlockSpec((block, width), lambda i: (i, 0))
+    return pl.pallas_call(
+        feed_kernel,
+        grid=(rows // block,),
+        in_specs=[
+            row_spec,
+            row_spec,
+            pl.BlockSpec((model, width), lambda i: (0, 0)),
+            pl.BlockSpec((width, model), lambda i: (0, 0)),
+            pl.BlockSpec((1, width), lambda i: (0, 0)),
+        ],
+        out_specs=[
+            wide_spec,
+            wide_spec,
+            row_spec,
+            row_spec,
+            pl.BlockSpec((1, width), lambda i: (0, 0)),
+        ],
+        out_shape=[
+            jax.ShapeDtypeStruct((rows, width), BF16),
+            jax.ShapeDtypeStruct((rows, width), BF16),
+            jax.ShapeDtypeStruct((rows, model), BF16),
+            jax.ShapeDtypeStruct((rows, model), BF16),
+            jax.ShapeDtypeStruct((1, width), F32),
+        ],
+        compiler_params=pltpu.CompilerParams(vmem_limit_bytes=VMEM_BYTES),
+        cost_estimate=pl.CostEstimate(
+            flops=14 * rows * model * width,
+            bytes_accessed=8 * rows * model + 4 * rows * width + 4 * model * width,
+            transcendentals=rows * width,
+        ),
+    )(normed, cotangent, share_fc, share_proj, bias)
+
+
+def ring_order(shards):
+    fast = 1
+    while fast * fast * 4 <= shards:
+        fast *= 2
+    slow = shards // fast
+    if fast == 1:
+        return list(range(shards))
+    path = [row * fast for row in range(slow)]
+    for row in reversed(range(slow)):
+        line = range(1, fast) if (slow - 1 - row) % 2 == 0 else reversed(range(1, fast))
+        path += [row * fast + place for place in line]
+    return path
+
+
+def ring_move(array, towards):
+    order = ring_order(lax.axis_size("dp"))
+    shards = len(order)
+    pairs = [(order[i], order[(i + towards) % shards]) for i in range(shards)]
+    return lax.ppermute(array, "dp", pairs)
+
+
+def ring_lookup(distance):
+    order = ring_order(lax.axis_size("dp"))
+    shards = len(order)
+    table = [0] * shards
+    for place, device in enumerate(order):
+        table[device] = order[(place + distance) % shards]
+    return jnp.array(table, jnp.int32)[lax.axis_index("dp")]
+
+
+def ring_gather(share, ties):
+    shards = lax.axis_size("dp")
+    full = jnp.zeros((shards,) + share.shape, share.dtype)
+    full = lax.dynamic_update_index_in_dim(full, share, lax.axis_index("dp"), 0)
+    upward = downward = share
+    tied = {}
+    for step in range(1, shards // 2 + 1):
+        upward = ring_move(upward, 1)
+        if 2 * step < shards:
+            downward = ring_move(downward, -1)
+        full = lax.dynamic_update_index_in_dim(full, upward, ring_lookup(-step), 0)
+        if 2 * step < shards:
+            full = lax.dynamic_update_index_in_dim(full, downward, ring_lookup(step), 0)
+        if step in ties:
+            upward, tied[step] = lax.optimization_barrier((upward, ties[step]))
+    return full, tied
+
+
+def ring_scatter(parts, tie):
+    shards = parts.shape[0]
+    half = shards // 2
+
+    def own(distance):
+        return lax.dynamic_index_in_dim(parts, ring_lookup(distance), 0, keepdims=False)
+
+    downward = upward = None
+    for distance in range(half, 0, -1):
+        held = own(-distance)
+        if downward is not None:
+            held = (held.astype(F32) + downward.astype(F32)).astype(BF16)
+        if distance == 1:
+            held, tie = lax.optimization_barrier((held, tie))
+        downward = ring_move(held, -1)
+        if distance < half or 2 * half < shards:
+            held = own(distance)
+            if upward is not None:
+                held = (held.astype(F32) + upward.astype(F32)).astype(BF16)
+            upward = ring_move(held, 1)
+    total = own(0).astype(F32) + downward.astype(F32)
+    return (total if upward is None else total + upward.astype(F32)), tie
 
 
 def swap(array, offset):
@@ -263,17 +409,17 @@
     return bits
 
 
-def gather_offsets(array):
+def gather_offsets(array, bits=None):
     found = {0: array}
-    for bit in reversed(bits_up()):
+    for bit in reversed(bits_up() if bits is None else bits):
         for offset in sorted(found):
             found[offset | bit] = swap(found[offset], bit)
     return [found[offset] for offset in range(len(found))]
 
 
-def reduce_offsets(blocks):
+def reduce_offsets(blocks, bits=None):
     left = dict(enumerate(blocks))
-    for bit in bits_up():
+    for bit in bits_up() if bits is None else bits:
         for offset in sorted(left, reverse=True):
             if offset & bit:
                 arrived = swap(left.pop(offset).astype(BF16), bit)
@@ -281,21 +427,55 @@
     return left[0]
 
 
-def in_rank_order(blocks):
+def placed(blocks, axis):
     rank = lax.axis_index("seq")
-    stacked = jnp.zeros((len(blocks),) + blocks[0].shape, blocks[0].dtype)
+    size = blocks[0].shape[axis]
+    shape = list(blocks[0].shape)
+    shape[axis] = size * len(blocks)
+    full = jnp.zeros(shape, blocks[0].dtype)
     for offset, block in enumerate(blocks):
-        stacked = lax.dynamic_update_index_in_dim(stacked, block, rank ^ offset, 0)
-    return stacked
-
-
-def by_offset(array, axis):
-    rank = lax.axis_index("seq")
-    ranks = array.shape[axis]
+        full = lax.dynamic_update_slice_in_dim(full, block, (rank ^ offset) * size, axis)
+    return full
+
+
+def picked(array, axis):
+    rank, ranks = (lax.axis_index("seq"), lax.axis_size("seq"))
+    size = array.shape[axis] // ranks
     return [
-        lax.dynamic_index_in_dim(array, rank ^ offset, axis, keepdims=False)
+        lax.dynamic_slice_in_dim(array, (rank ^ offset) * size, size, axis)
         for offset in range(ranks)
     ]
+
+
+def columns_kernel(rank_ref, *refs, groups, size):
+    blocks, full_ref = (refs[:-1], refs[-1])
+    ranks = len(blocks)
+    for offset, block_ref in enumerate(blocks):
+        owner = lax.bitwise_xor(rank_ref[0, 0], offset)
+        for group in range(groups):
+            start = pl.multiple_of((owner + group * ranks) * size, size)
+            piece = block_ref[:, group * size : (group + 1) * size]
+            full_ref[:, pl.ds(start, size)] = piece.astype(full_ref.dtype)
+
+
+def columns(blocks, groups, dtype):
+    rows, wide = blocks[0].shape
+    ranks, size = (len(blocks), wide // groups)
+    rank = lax.axis_index("seq")
+    if size % 128:
+        shaped = [block.reshape(rows, groups, 1, size) for block in blocks]
+        return placed(shaped, 2).reshape(rows, ranks * wide).astype(dtype)
+    return pl.pallas_call(
+        functools.partial(columns_kernel, groups=groups, size=size),
+        in_specs=[pl.BlockSpec(memory_space=pltpu.SMEM)]
+        + [pl.BlockSpec(memory_space=pltpu.VMEM)] * ranks,
+        out_specs=pl.BlockSpec(memory_space=pltpu.VMEM),
+        out_shape=jax.ShapeDtypeStruct((rows, ranks * wide), dtype),
+        compiler_params=pltpu.CompilerParams(vmem_limit_bytes=VMEM_BYTES),
+        cost_estimate=pl.CostEstimate(
+            flops=rows * wide * ranks, bytes_accessed=6 * rows * wide * ranks, transcendentals=0
+        ),
+    )(rank.astype(jnp.int32).reshape(1, 1), *blocks)
 
 
 def row_stats(values):
@@ -313,18 +493,12 @@
     return inverse * (scaled - first - unit * second)
 
 
-def pad_rows(array, multiple):
-    rows = array.shape[0]
-    return jnp.pad(array, ((0, -rows % multiple), (0, 0)))
-
-
-def vector_rows(vectors, parts, columns):
-    flat = jnp.concatenate([item.reshape(parts, -1) for item in vectors], axis=1)
-    size = flat.shape[1]
-    rows = -(-size // columns)
-    rows = -(-rows // 16) * 16
-    flat = jnp.pad(flat, ((0, 0), (0, rows * columns - size)))
-    return flat.reshape(parts, rows, columns)
+def vector_rows(vectors, columns_count):
+    padded = [
+        jnp.pad(item, ((0, 0), (0, columns_count - item.shape[1])))[:, None] for item in vectors
+    ]
+    stacked = jnp.concatenate(padded, axis=1)
+    return jnp.pad(stacked, ((0, 0), (0, -stacked.shape[1] % 16), (0, 0)))
 
 
 def per_device(
@@ -356,28 +530,63 @@
     hidden_width = w_fc.shape[1] // ranks
     tokens_own = tokens.reshape(seqs * rows, model)
     cot_own = cotangent.reshape(seqs * rows, model)
-
-    qkv_share = lax.dynamic_index_in_dim(
-        w_qkv.reshape(part, 3, ranks, width), rank, 2, keepdims=False
-    ).reshape(part, 3 * width)
-    vectors = (
-        bias_query,
-        bias_value,
-        bias_attn,
-        gain_one,
-        shift_one,
-        gain_two,
-        shift_two,
-        bias_proj,
-        bias_fc,
-    )
-    packed = jnp.concatenate([qkv_share, vector_rows(vectors, 1, 3 * width)[0]], axis=0)
-    first_gather = lax.all_gather(packed, "dp", axis=0)
-    full_qkv = first_gather[:, :part].reshape(model, 3 * width)
-    flat_vectors = first_gather[:, part:].reshape(shards, -1).astype(F32)
+    gather_columns = 4 * width
+
+    def share_of(array, groups):
+        size = array.shape[1] // (groups * ranks)
+        return [
+            lax.dynamic_slice_in_dim(array, (group * ranks + rank) * size, size, 1)
+            for group in range(groups)
+        ]
+
+    vectors = [
+        item.reshape(1, part)
+        for item in (
+            bias_query,
+            bias_value,
+            bias_attn,
+            gain_one,
+            shift_one,
+            gain_two,
+            shift_two,
+            bias_proj,
+        )
+    ] + [item.reshape(1, units) for item in jnp.split(bias_fc, ranks)]
+    packed = jnp.concatenate(
+        [
+            jnp.concatenate(share_of(w_qkv, 3) + share_of(w_attn, 1), axis=1),
+            vector_rows(vectors, gather_columns)[0],
+        ],
+        axis=0,
+    )
+    proj_share = lax.dynamic_slice_in_dim(w_proj, rank * units, units, 0)
+    feed_share = jnp.concatenate(
+        share_of(w_fc, shards) + [proj_share.reshape(part, units * model // part)], axis=1
+    )
+
+    all_tokens = placed(gather_offsets(tokens), 1).reshape(seqs * length, model)
+    token_values = all_tokens.astype(F32)
+    average = jnp.mean(token_values, axis=-1, keepdims=True)
+    centered = token_values - average
+    inverse_all = lax.rsqrt(jnp.mean(centered * centered, axis=-1, keepdims=True) + EPSILON)
+
+    steps = shards // 2
+    middle_step = max(1, steps // 2)
+    first_gather, tied = ring_gather(
+        packed,
+        {middle_step: (feed_share,), steps - 1: (average, inverse_all, all_tokens)},
+    )
+    (feed_share,) = tied[middle_step]
+    average, inverse_all, all_tokens = tied[steps - 1]
+    second_gather = lax.all_gather(feed_share, "dp", axis=0)
+    share_fc = second_gather[:, :, :hidden_width].reshape(model, hidden_width)
+    share_proj = second_gather[:, :, hidden_width:].reshape(hidden_width, model)
+    full_qkv = first_gather[:, :part, : 3 * width].reshape(model, 3 * width)
+    attn_columns = first_gather[:, :part, 3 * width :].reshape(model, width)
+    vector_block = first_gather[:, part:].astype(F32)
 
     def vector(index):
-        return flat_vectors[:, index * part : (index + 1) * part].reshape(model)
+        return vector_block[:, index, :part].reshape(model)
 
     query_bias = lax.dynamic_slice_in_dim(vector(0), rank * width, width)
     value_bias = lax.dynamic_slice_in_dim(vector(1), rank * width, width)
@@ -389,61 +598,49 @@
         vector(6),
         vector(7),
     )
-    fc_bias = lax.dynamic_index_in_dim(
-        flat_vectors[:, 8 * part : 8 * part + hidden_part].reshape(shards, ranks, units),
-        rank,
-        1,
-        keepdims=False,
-    ).reshape(hidden_width)
-
-    fc_share = lax.dynamic_index_in_dim(
-        w_fc.reshape(part, shards, ranks, units), rank, 2, keepdims=False
-    ).reshape(part, hidden_width)
-    proj_share = lax.dynamic_index_in_dim(
-        w_proj.reshape(ranks, units, model), rank, 0, keepdims=False
-    ).reshape(part, units * model // part)
-    attn_share = lax.dynamic_slice_in_dim(w_attn, rank * width, width, 1)
-    second_gather = lax.all_gather(
-        jnp.concatenate([attn_share, fc_share, proj_share], axis=1), "dp", axis=0
-    )
-    attn_columns = second_gather[:, :, :width].reshape(model, width)
-    share_fc = second_gather[:, :, width : width + hidden_width].reshape(model, hidden_width)
-    share_proj = second_gather[:, :, width + hidden_width :].reshape(hidden_width, model)
-
-    all_tokens = in_rank_order(gather_offsets(tokens)).transpose(1, 0, 2, 3)
-    all_tokens = all_tokens.reshape(seqs * length, model)
+    fc_bias = lax.dynamic_index_in_dim(vector_block, 8 + rank, 1, keepdims=False)
+    fc_bias = fc_bias[:, :units].reshape(hidden_width)
     cot_blocks = gather_offsets(cot_own)
-
-    unit_all, _ = row_stats(all_tokens.astype(F32))
+    half = ranks // 2
+    near_cot = jnp.concatenate(cot_blocks[:half], axis=0)
+    far_cot = jnp.concatenate(cot_blocks[half:], axis=0)
+
+    unit_all = (all_tokens.astype(F32) - average) * inverse_all
     normed = (unit_all * gain_first + shift_first).astype(BF16)
     joint_bias = jnp.concatenate([query_bias, jnp.zeros_like(query_bias), value_bias])
     mixed = (dot_nn(normed, full_qkv) + joint_bias).astype(BF16)
     mixed = mixed.reshape(seqs, length, 3 * width)
+    mixed, near_cot, far_cot = lax.optimization_barrier((mixed, near_cot, far_cot))
     attended, logs = attend(mixed, width)
 
-    sent = by_offset(attended.reshape(seqs, ranks, rows, width), 1)
+    sent = picked(attended, 1)
     arrived = [sent[0]] + [swap(sent[offset], offset) for offset in range(1, ranks)]
-    joined = in_rank_order(arrived).transpose(1, 2, 0, 3).reshape(seqs * rows, model)
-    full_attn = in_rank_order(gather_offsets(attn_columns)).transpose(1, 0, 2)
-    full_attn = full_attn.reshape(model, model)
+    joined = columns([item.reshape(seqs * rows, width) for item in arrived], 1, BF16)
+    full_attn = columns(gather_offsets(attn_columns), 1, BF16)
 
     inputs = tokens_own.astype(F32)
     middle = inputs + (dot_nn(joined, full_attn) + attn_bias)
     unit_two, inverse_two = row_stats(middle)
     normed_two = (unit_two * gain_second + shift_second).astype(BF16)
-    all_two = jnp.concatenate(gather_offsets(normed_two), axis=0)
-    all_cot = jnp.concatenate(cot_blocks, axis=0)
-
-    hidden = dot_nn(all_two, share_fc) + fc_bias
-    active, gelu_pull = jax.vjp(gelu_tanh, hidden)
-    active = active.astype(BF16)
-    grad_active = dot_nt(all_cot, share_proj)
-    grad_hidden = gelu_pull(grad_active)[0].astype(BF16)
-    back_two = dot_nt(grad_hidden, share_fc).astype(BF16).reshape(ranks, seqs * rows, model)
-    grad_normed_two = reduce_offsets([back_two[offset] for offset in range(ranks)])
-    forward_two = dot_nn(active, share_proj).astype(BF16).reshape(ranks, seqs * rows, model)
-    projected = reduce_offsets([forward_two[offset] for offset in range(ranks)])
-    output = (middle + projected + proj_bias).astype(BF16)
+    *low_bits, top_bit = bits_up()
+    near_two = jnp.concatenate(gather_offsets(normed_two, low_bits), axis=0)
+    far_two = jnp.concatenate(gather_offsets(swap(normed_two, top_bit), low_bits), axis=0)
+    feed_bias = fc_bias.reshape(1, hidden_width)
+    near_active, near_grad, near_back, near_ahead, near_sum = feed(
+        near_two, near_cot, share_fc, share_proj, feed_bias
+    )
+    far_active, far_grad, far_back, far_ahead, far_sum = feed(
+        far_two, far_cot, share_fc, share_proj, feed_bias
+    )
+
+    def reduce_halves(near, far):
+        blocks = (half, seqs * rows, model)
+        far_part = reduce_offsets(list(far.reshape(blocks)), low_bits).astype(BF16)
+        near_part = reduce_offsets(list(near.reshape(blocks)), low_bits)
+        return near_part.astype(F32), swap(far_part, top_bit)
+
+    near_part, far_part = reduce_halves(near_back, far_back)
+    grad_normed_two = near_part + far_part.astype(F32)
 
     upstream = cot_own.astype(F32)
     grad_gain_two = jnp.sum(grad_normed_two * unit_two, axis=0)
@@ -451,96 +648,100 @@
     grad_middle = upstream + norm_back(grad_normed_two, gain_second, unit_two, inverse_two)
     grad_branch = grad_middle.astype(BF16)
     grad_joined = dot_nt(grad_branch, full_attn).astype(BF16)
-    grad_sent = by_offset(grad_joined.reshape(seqs, rows, ranks, width), 2)
+    grad_sent = picked(grad_joined.reshape(seqs, rows, model), 2)
     grad_arrived = [grad_sent[0]] + [
         swap(grad_sent[offset], offset) for offset in range(1, ranks)
     ]
-    grad_attended = in_rank_order(grad_arrived).transpose(1, 0, 2, 3)
-    grad_attended = grad_attended.reshape(seqs, length, width)
-
-    grad_w_proj = dot_tn(active, all_cot).astype(BF16).reshape(shards, units, model)
-    grad_w_fc = dot_tn(all_two, grad_hidden).astype(BF16).reshape(shards, part, hidden_width)
-    grad_bias_fc = jnp.sum(grad_hidden, axis=0, dtype=F32)
+    grad_attended = placed(grad_arrived, 1)
+
+    grad_w_proj = dot_tn(near_active, near_cot) + dot_tn(far_active, far_cot)
+    grad_w_proj = grad_w_proj.astype(BF16).reshape(shards, part, units * model // part)
+    grad_w_fc = dot_tn(near_two, near_grad) + dot_tn(far_two, far_grad)
+    grad_w_fc = grad_w_fc.astype(BF16).reshape(shards, part, hidden_width)
+    grad_bias_fc = (near_sum + far_sum).reshape(hidden_width)
     grad_bias_proj = jnp.sum(upstream, axis=0)
-    first_scatter = lax.psum_scatter(
-        jnp.concatenate(
-            [
-                grad_w_fc,
-                grad_w_proj.reshape(shards, part, units * model // part),
-            ],
-            axis=2,
-        ),
-        "dp",
-        scatter_dimension=0,
-    )
-
-    grad_attn_part = dot_tn(joined, grad_branch).reshape(model, ranks, width)
-    grad_w_attn = reduce_offsets(by_offset(grad_attn_part, 1)).astype(BF16)
+    first_parts = jnp.concatenate([grad_w_fc, grad_w_proj], axis=2)
+    near_ahead, far_ahead, _ = lax.optimization_barrier((near_ahead, far_ahead, grad_branch))
+    ahead_far = reduce_offsets(
+        list(far_ahead.reshape(half, seqs * rows, model)), low_bits
+    ).astype(BF16)
+    grad_attn_part = dot_tn(joined, grad_branch).astype(BF16)
+    grad_attended, first_parts, ahead_far, grad_attn_part = lax.optimization_barrier(
+        (grad_attended, first_parts, ahead_far, grad_attn_part)
+    )
+    first_scatter = lax.psum_scatter(first_parts, "dp", scatter_dimension=0)
+    ahead_far = swap(ahead_far, top_bit)
+    ahead_part = reduce_offsets(list(near_ahead.reshape(half, seqs * rows, model)), low_bits)
+    grad_w_attn = reduce_offsets(picked(grad_attn_part, 1)).astype(BF16)
     grad_bias_attn = jnp.sum(grad_branch, axis=0, dtype=F32)
 
     grad_mixed = attend_back(mixed, attended, grad_attended, logs, width)
     grad_mixed = grad_mixed.reshape(seqs * length, 3 * width)
-    back_one = dot_nt(grad_mixed, full_qkv).astype(BF16)
-    blocks_one = by_offset(back_one.reshape(seqs, ranks, rows, model), 1)
-    grad_normed = reduce_offsets(blocks_one).reshape(seqs * rows, model)
-    grad_w_qkv = dot_tn(normed, grad_mixed).astype(BF16)
+    grad_w_qkv = dot_tn(normed, grad_mixed)
     column_sums = jnp.sum(grad_mixed, axis=0, dtype=F32)
-    grad_gain_one = jnp.sum(back_one.astype(F32) * unit_all, axis=0)
-    grad_shift_one = jnp.sum(back_one, axis=0, dtype=F32)
+    qkv_values = full_qkv.astype(F32)
+    grad_shift_one = jnp.sum(qkv_values * column_sums, axis=1)
+    grad_gain_one = (
+        jnp.sum(qkv_values * grad_w_qkv, axis=1) - shift_first * grad_shift_one
+    ) / gain_first
 
     def spread(values):
         return lax.dynamic_update_slice_in_dim(
             jnp.zeros((model,), F32), values, rank * width, 0
         )
 
-    grad_vectors = (
-        spread(column_sums[:width]),
-        spread(column_sums[2 * width :]),
-        grad_bias_attn,
-        grad_gain_one,
-        grad_shift_one,
-        grad_gain_two,
-        grad_shift_two,
-        grad_bias_proj,
-        grad_bias_fc,
-    )
-    last_columns = 4 * width
-    vector_part = vector_rows(grad_vectors, shards, last_columns).astype(BF16)
-    last_scatter = lax.psum_scatter(
-        jnp.concatenate(
-            [
-                jnp.concatenate(
-                    [
-                        grad_w_qkv.reshape(shards, part, 3 * width),
-                        grad_w_attn.reshape(shards, part, width),
-                    ],
-                    axis=2,
-                ),
-                vector_part,
-            ],
-            axis=1,
-        ),
-        "dp",
-        scatter_dimension=0,
-    )
-
+    grad_vectors = [
+        item.reshape(shards, -1).astype(BF16)
+        for item in (
+            spread(column_sums[:width]),
+            spread(column_sums[2 * width :]),
+            grad_bias_attn,
+            grad_gain_one,
+            grad_shift_one,
+            grad_gain_two,
+            grad_shift_two,
+            grad_bias_proj,
+            grad_bias_fc,
+        )
+    ]
+    last_parts = jnp.concatenate(
+        [
+            jnp.concatenate(
+                [
+                    grad_w_qkv.astype(BF16).reshape(shards, part, 3 * width),
+                    grad_w_attn.reshape(shards, part, width),
+                ],
+                axis=2,
+            ),
+            vector_rows(grad_vectors, gather_columns),
+        ],
+        axis=1,
+    )
+    back_one = dot_nt(grad_mixed, full_qkv).astype(BF16)
+    blocks_one = [
+        item.reshape(seqs * rows, model) for item in picked(back_one.reshape(seqs, length, model), 1)
+    ]
+    grad_normed = reduce_offsets(blocks_one)
+    fed = gather_offsets(first_scatter)
+    last_scatter, fed = ring_scatter(last_parts, fed)
+    rest = gather_offsets(last_scatter.astype(BF16))
+
+    _, ahead_far = lax.optimization_barrier((grad_mixed, ahead_far))
+    output = (middle + ahead_part.astype(F32) + ahead_far.astype(F32) + proj_bias).astype(BF16)
     unit_one, inverse_one = row_stats(inputs)
     grad_tokens = grad_middle + norm_back(grad_normed, gain_first, unit_one, inverse_one)
 
-    feed = in_rank_order(gather_offsets(first_scatter))
-    out_fc = feed[:, :, :hidden_width].reshape(ranks, part, shards, units)
-    out_fc = out_fc.transpose(1, 2, 0, 3).reshape(part, w_fc.shape[1]).astype(F32)
-    out_proj = feed[:, :, hidden_width:].reshape(hidden_part, model).astype(F32)
-    rest = in_rank_order(gather_offsets(last_scatter))
-    out_qkv = rest[:, :part, : 3 * width].reshape(ranks, part, 3, width)
-    out_qkv = out_qkv.transpose(1, 2, 0, 3).reshape(part, 3 * model).astype(F32)
-    out_attn = rest[:, :part, 3 * width :].transpose(1, 0, 2).reshape(part, model).astype(F32)
-    out_vectors = rest[:, part:].reshape(ranks, -1).astype(F32)
-    summed = jnp.sum(out_vectors[:, : 8 * part], axis=0)
-    out_bias_fc = out_vectors[:, 8 * part : 8 * part + units].reshape(hidden_part)
+    out_fc = columns([item[:, :hidden_width] for item in fed], shards, F32)
+    proj_blocks = [item[:, hidden_width:].reshape(units, model) for item in fed]
+    out_proj = placed(proj_blocks, 0).astype(F32)
+    out_qkv = columns([item[:part, : 3 * width] for item in rest], 3, F32)
+    out_attn = columns([item[:part, 3 * width :] for item in rest], 1, F32)
+    tails = [item[part:].astype(F32) for item in rest]
+    summed = sum(tails)[:, :part]
+    out_bias_fc = placed([item[8, :units] for item in tails], 0)
 
     def out_vector(index):
-        return summed[index * part : (index + 1) * part]
+        return summed[index]
 
     return (
         output.reshape(seqs, rows, model),

time: 615 us -> 478 us (0.78)
  waiting for transfers between devices: 303 us -> 129 us
  matrix products: 73.8 us -> 38.8 us
  Pallas kernels: 79.4 us -> 98.1 us
  other arithmetic: 44.3 us -> 60 us
  between operations: 15.3 us -> 29.1 us
  starting transfers between devices: 24.6 us -> 37.1 us
  local copies, waits for them, and re-layouts: 70.1 us -> 79.3 us
    reduce_scatter x2 -> x1, waiting for transfers between devices: 95.9 us -> 0.01 us  [per_device(): first_scatter = lax.psum_scatter(first_parts, 'dp', scatter_dimension=0)]
    ppermute x36, waiting for transfers between devices: 154 us -> 93.5 us  [swap(): lax.ppermute(array, 'seq', [(rank, rank ^ offset) for rank in range(ranks)])]
    all_gather x2 -> x1, waiting for transfers between devices: 52.6 us -> 0.01 us  [per_device(): second_gather = lax.all_gather(feed_share, 'dp', axis=0)]
    pallas_call x0 -> x7, Pallas kernels: none -> 41.7 us  [the longest x2 29.2 us: feed(): pl.pallas_call(feed_kernel, grid=(rows // block,), in_specs=[row_spec, ro...]
    ppermute x0 -> x14, waiting for transfers between devices: none -> 35.5 us  [ring_move(): return lax.ppermute(array, 'dp', pairs)]
    dot_general x4 -> x2, matrix products: 31.6 us -> 5.11 us  [dot_nt(): lax.dot_general(left_side, right_side, (((1,), (1,)), ((), ())), preferre...]
    ppermute x0 -> x14, starting transfers between devices: none -> 16.4 us  [ring_move(): return lax.ppermute(array, 'dp', pairs)]
    pallas_call x1, Pallas kernels: 53.6 us -> 38.6 us  [attend_back(): pl.pallas_call(functools.partial(attend_back_kernel, block=block, width=w...]
  transfers between devices with their start and end apart: 40 -> 52, of which waited for: 18 -> 18; matrix products, arithmetic and copies ran while one was open for 21% -> 32% of each run, Pallas kernels for 13% -> 17%
where the time goes in v2:
time: 478 us; the launch traced here: 471 us
  waiting for transfers between devices  129 us (27%)
  Pallas kernels  98.1 us (21%)
  local copies, waits for them, and re-layouts  79.3 us (17%)
  other arithmetic  60 us (13%)
  matrix products  38.8 us (8%)
  starting transfers between devices  37.1 us (8%)
  between operations  29.1 us (6%)
    ppermute x36, waiting for transfers between devices, swap(): lax.ppermute(array, 'seq', [(rank, rank ^ offset) for rank in range(ranks)])  93.5 us
    pallas_call x1, Pallas kernels, attend_back(): pl.pallas_call(functools.partial(attend_back_kernel, block=block, width=w...  38.6 us
    ppermute x14, waiting for transfers between devices, ring_move(): return lax.ppermute(array, 'dp', pairs)  35.5 us
    pallas_call x2, Pallas kernels, feed(): pl.pallas_call(feed_kernel, grid=(rows // block,), in_specs=[row_spec, ro...  29.2 us
    dot_general x6, matrix products, dot_tn(): lax.dot_general(left_side, right_side, (((0,), (0,)), ((), ())), preferre...  22.1 us
    ppermute x36, starting transfers between devices, swap(): lax.ppermute(array, 'seq', [(rank, rank ^ offset) for rank in range(ranks)])  20.7 us
    pallas_call x1, Pallas kernels, attend(): pl.pallas_call(functools.partial(attend_kernel, block=block, width=width)...  17.8 us
    ppermute x14, starting transfers between devices, ring_move(): return lax.ppermute(array, 'dp', pairs)  16.4 us
  transfers between devices with their start and end apart: 52, of which 18 were waited for; matrix products, arithmetic and copies ran while one was open for 32% of the time, Pallas kernels for 17%

profile of v2, /device:TPU:0, one launch (start us, length us, event | category | flops | bytes accessed | tf_op | source)
XLA Modules:
  0.0 471.5 jit_solution(16516255305288849638)
XLA Ops:
  53.8 3.4 collective-permute-done.1
  74.5 3.0 fusion.1
  83.6 7.9 %collective-permute-done.9 = bf16[144,1024]{1,0:T(8,128)(2,1)S(1)} collective-permute-done((bf16[144,1024]{1,0:T(8,128)(2,1)S(1)}, bf16[144,1024]{1,0:T(8,128)(2,1)S(1)}, u32[]{:S(2)}, u32[]{:S(2)}) %collective-permute-start.9) | collective-permute-done | bytes 294944 | tf_op jit(solution)/shard_map/ppermute | solution.py:345
  98.8 8.6 %fusion.3.mixed_ref = bf16[1,2048,768]{2,1,0:T(8,128)(2,1)} fusion(f32[768]{0:T(1024)S(1)} %pad_maximum_fusion.5, bf16[1024,768]{1,0:T(8,128)(2,1)S(1)} %bitcast.261, bf16[2048,1024]{1,0:T(8,128)(2,1)} %bitcast_dynamic-update-slice_fusion, f32[1024]{0:T(1024)S(1)} %bitcast.280, f32[1024]{0:T(1024)S(1)} %bitcast.273, f32[2048]{0:T(1024)S(1)} %add_rsqrt_fusion, ...), kind=kOutput, calls=%fused_computation.18 | convolution fusion | flops 3236954112 | bytes 8940544 | tf_op jit(solution)/shard_map/dot_general | solution.py:27
  107.8 17.8 %shard_map.397 = (bf16[1,2048,256]{2,1,0:T(8,128)(2,1)}, f32[1,8,2048]{2,1,0:T(8,128)}) custom-call(bf16[1,2048,768]{2,1,0:T(8,128)(2,1)} %fusion.3.mixed_ref), custom_call_target="tpu_custom_call" | custom-call | flops 30064771072 | bytes 4194304 | tf_op jit(solution)/shard_map/pallas_call | solution.py:104
  129.5 7.4 %collective-permute-done.14 = bf16[1,512,256]{2,1,0:T(8,128)(2,1)S(1)} collective-permute-done((bf16[1,512,256]{2,1,0:T(8,128)(2,1)S(1)}, bf16[1,512,256]{2,1,0:T(8,128)(2,1)S(1)}, u32[]{:S(2)}, u32[]{:S(2)}) %collective-permute-start.14) | collective-permute-done | bytes 262176 | tf_op jit(solution)/shard_map/ppermute | solution.py:401
  136.9 4.5 collective-permute-done.15
  146.1 3.1 shard_map.399
  155.3 24.4 %collective-permute-done.20 = bf16[512,1024]{1,0:T(8,128)(2,1)} collective-permute-done((bf16[512,1024]{1,0:T(8,128)(2,1)}, bf16[512,1024]{1,0:T(8,128)(2,1)}, u32[]{:S(2)}, u32[]{:S(2)}) %collective-permute-start.20) | collective-permute-done | bytes 1048608 | tf_op jit(solution)/shard_map/ppermute | solution.py:401
  186.3 3.0 pad_maximum_fusion.3.normed_ref
  191.6 4.8 %fusion.36 = (bf16[8,128,1024]{2,1,0:T(8,128)(2,1)}, bf16[8,128,1024]{2,1,0:T(8,128)(2,1)}) fusion(bf16[8,128,2048]{2,1,0:T(8,128)(2,1)} %bitcast.250), kind=kLoop, calls=%fused_computation.191 | loop fusion | bytes 8388608 | tf_op jit(solution)/shard_map/slice | solution.py:583
  196.5 14.6 %shard_map.400 = (bf16[1024,1024]{1,0:T(8,128)(2,1)}, bf16[1024,1024]{1,0:T(8,128)(2,1)}, bf16[1024,1024]{1,0:T(8,128)(2,1)}, bf16[1024,1024]{1,0:T(8,128)(2,1)}, f32[1,1024]{1,0:T(1,128)}) custom-call(bf16[1024,1024]{1,0:T(8,128)(2,1)} %pad_maximum_fusion.3.normed_ref, bf16[1024,1024]{1,0:T(8,128)(2,1)} %pad_maximum_fusion.1.cot_ref, ...), custom_call_target="tpu_custom_call" | custom-call | flops 15032385536 | bytes 16777216 | tf_op jit(solution)/shard_map/pallas_call | solution.py:294
  213.9 14.6 %shard_map.401 = (bf16[1024,1024]{1,0:T(8,128)(2,1)}, bf16[1024,1024]{1,0:T(8,128)(2,1)}, bf16[1024,1024]{1,0:T(8,128)(2,1)}, bf16[1024,1024]{1,0:T(8,128)(2,1)}, f32[1,1024]{1,0:T(1,128)}) custom-call(bf16[1024,1024]{1,0:T(8,128)(2,1)} %constant_dynamic-update-slice_fusion.normed_ref, bf16[1024,1024]{1,0:T(8,128)(2,1)} %pad_maximum_fusion.2.cot_ref, ...), custom_call_target="tpu_custom_call" | custom-call | flops 15032385536 | bytes 16777216 | tf_op jit(solution)/shard_map/pallas_call | solution.py:294
  233.0 4.1 fusion.33
  237.1 4.2 add_convert_fusion.3
  249.0 19.2 %collective-permute-done.24 = bf16[512,1024]{1,0:T(8,128)(2,1)} collective-permute-done((bf16[512,1024]{1,0:T(8,128)(2,1)}, bf16[512,1024]{1,0:T(8,128)(2,1)}, u32[]{:S(2)}, u32[]{:S(2)}) %collective-permute-start.24) | collective-permute-done | bytes 1048608 | tf_op jit(solution)/shard_map/ppermute | solution.py:401
  270.9 3.9 fusion.35
  281.1 5.5 %collective-permute-done.27 = bf16[1,512,256]{2,1,0:T(8,128)(2,1)S(1)} collective-permute-done((bf16[1,512,256]{2,1,0:T(8,128)(2,1)S(1)}, bf16[1,512,256]{2,1,0:T(8,128)(2,1)S(1)}, u32[]{:S(2)}, u32[]{:S(2)}) %collective-permute-start.27) | collective-permute-done | bytes 262176 | tf_op jit(solution)/shard_map/ppermute | solution.py:401
  286.6 3.7 collective-permute-done.28
  293.7 38.6 %shard_map.402 = bf16[1,2048,768]{2,1,0:T(8,128)(2,1)} custom-call(bf16[1,2048,768]{2,1,0:T(8,128)(2,1)} %fusion.3.mixed_ref, bf16[1,2048,256]{2,1,0:T(8,128)(2,1)} %get-tuple-element.54.out_ref, bf16[1,2048,256]{2,1,0:T(8,128)(2,1)} %copy-done.23, f32[1,8,2048]{2,1,0:T(8,128)} %get-tuple-element.69.log_ref), custom_call_target="tpu_custom_call" | custom-call | flops 60129542144 | bytes 8388608 | tf_op jit(solution)/shard_map/pallas_call | solution.py:224
  336.9 7.5 %fusion.37 = (bf16[1024,768]{1,0:T(8,128)(2,1)}, f32[1024]{0:T(1024)S(1)}) fusion(bf16[8,128,768]{2,1,0:T(8,128)(2,1)S(1)} %copy-done.19, bf16[1,2048,768]{2,1,0:T(8,128)(2,1)S(1)} %copy-done.8, bf16[2048,1024]{1,0:T(8,128)(2,1)} %bitcast_dynamic-update-slice_fusion, f32[1024]{0:T(1024)S(1)} %bitcast.281, f32[1024]{0:T(1024)S(1)} %bitcast.274, ...), kind=kOutput, calls=%fused_computation.192 | convolution fusion | flops 3236953088 | bytes 10514432 | tf_op jit(solution)/shard_map/dot_general | solution.py:39
  344.6 3.8 convolution_convert_fusion
  358.5 7.4 %collective-permute-done.36 = bf16[1024,256]{1,0:T(8,128)(2,1)S(1)} collective-permute-done((bf16[1024,256]{1,0:T(8,128)(2,1)}, bf16[1024,256]{1,0:T(8,128)(2,1)S(1)}, u32[]{:S(2)}, u32[]{:S(2)}) %collective-permute-start.36) | collective-permute-done | bytes 524320 | tf_op jit(solution)/shard_map/ppermute | solution.py:401
  369.7 3.2 collective-permute-start.37
  374.9 12.9 %collective-permute-done.37 = bf16[144,1024]{1,0:T(8,128)(2,1)S(1)} collective-permute-done((bf16[144,1024]{1,0:T(8,128)(2,1)}, bf16[144,1024]{1,0:T(8,128)(2,1)S(1)}, u32[]{:S(2)}, u32[]{:S(2)}) %collective-permute-start.37) | collective-permute-done | bytes 294944 | tf_op jit(solution)/shard_map/ppermute | solution.py:345
  389.0 3.1 add_convert_fusion.4
  399.4 3.3 fusion.15
  402.7 4.7 collective-permute-done.39
  410.8 7.6 %collective-permute-done.33 = bf16[512,1024]{1,0:T(8,128)(2,1)} collective-permute-done((bf16[512,1024]{1,0:T(8,128)(2,1)}, bf16[512,1024]{1,0:T(8,128)(2,1)}, u32[]{:S(2)}, u32[]{:S(2)}) %collective-permute-start.33) | collective-permute-done | bytes 1048608 | tf_op jit(solution)/shard_map/ppermute | solution.py:401
  421.3 7.4 %collective-permute-done.41 = bf16[128,2048]{1,0:T(8,128)(2,1)S(1)} collective-permute-done((bf16[128,2048]{1,0:T(8,128)(2,1)}, bf16[128,2048]{1,0:T(8,128)(2,1)S(1)}, u32[]{:S(2)}, u32[]{:S(2)}) %collective-permute-start.41) | collective-permute-done | bytes 524320 | tf_op jit(solution)/shard_map/ppermute | solution.py:401
  428.6 4.1 fusion.13
  448.8 6.5 %collective-permute-done.48 = bf16[144,1024]{1,0:T(8,128)(2,1)S(1)} collective-permute-done((bf16[144,1024]{1,0:T(8,128)(2,1)S(1)}, bf16[144,1024]{1,0:T(8,128)(2,1)S(1)}, u32[]{:S(2)}, u32[]{:S(2)}) %collective-permute-start.48) | collective-permute-done | bytes 294944 | tf_op jit(solution)/shard_map/ppermute | solution.py:401
  (371 shorter events, 174.7 us)
Async XLA Ops:
  7.2 184.4 %all-gather.3.cloned.1.call-start = ((), (), s32[]{:S(2)}) async-start(), calls=%async_computation.2 | async-start | bytes 4718592 | tf_op jit(solution)/shard_map/all_gather | solution.py:581
  7.2 59.9 %collective-permute-start.3 = (bf16[1,512,1024]{2,1,0:T(8,128)(2,1)}, bf16[1,512,1024]{2,1,0:T(8,128)(2,1)S(1)}, u32[]{:S(2)}, u32[]{:S(2)}) collective-permute-start(bf16[1,512,1024]{2,1,0:T(8,128)(2,1)} %param.30), channel_id=1, source_target_pairs={{0,1},{1,0},{2,3},{3,2},{4,5},{5,4},{6,7},{7,6},{8,9},{9,8},{10,11... | collective-permute-start | bytes 3145736 | tf_op jit(solution)/shard_map/ppermute | solution.py:401
  7.7 53.3 %collective-permute-start.4 = (bf16[1,512,1024]{2,1,0:T(8,128)(2,1)}, bf16[1,512,1024]{2,1,0:T(8,128)(2,1)}, u32[]{:S(2)}, u32[]{:S(2)}) collective-permute-start(bf16[1,512,1024]{2,1,0:T(8,128)(2,1)} %param.30), channel_id=1, source_target_pairs={{0,2},{1,3},{2,0},{3,1},{4,6},{5,7},{6,4},{7,5},{8,10},{9,11},{10,... | collective-permute-start | bytes 3145736 | tf_op jit(solution)/shard_map/ppermute | solution.py:401
  15.1 33.3 %collective-permute-start = (bf16[144,1024]{1,0:T(8,128)(2,1)S(1)}, bf16[144,1024]{1,0:T(8,128)(2,1)}, u32[]{:S(2)}, u32[]{:S(2)}) collective-permute-start(bf16[144,1024]{1,0:T(8,128)(2,1)S(1)} %pad_maximum_fusion.4), channel_id=1, source_target_pairs={{0,8},{8,16},{16,24},{24,28},{28,20},{20,12},{12,4},{4,0},{1,9},{9... | collective-permute-start | bytes 884744 | tf_op jit(solution)/shard_map/ppermute | solution.py:345
  16.8 33.7 %collective-permute-start.6 = (bf16[144,1024]{1,0:T(8,128)(2,1)S(1)}, bf16[144,1024]{1,0:T(8,128)(2,1)}, u32[]{:S(2)}, u32[]{:S(2)}) collective-permute-start(bf16[144,1024]{1,0:T(8,128)(2,1)S(1)} %pad_maximum_fusion.4), channel_id=1, source_target_pairs={{0,4},{8,0},{16,8},{24,16},{28,24},{20,28},{12,20},{4,12},{1,5},{9... | collective-permute-start | bytes 884744 | tf_op jit(solution)/shard_map/ppermute | solution.py:345
  17.2 49.9 %collective-permute-start.11 = (bf16[512,1024]{1,0:T(8,128)(2,1)}, bf16[512,1024]{1,0:T(8,128)(2,1)}, u32[]{:S(2)}, u32[]{:S(2)}) collective-permute-start(bf16[512,1024]{1,0:T(8,128)(2,1)} %bitcast.247), channel_id=1, source_target_pairs={{0,2},{1,3},{2,0},{3,1},{4,6},{5,7},{6,4},{7,5},{8,10},{9,11},{10,... | collective-permute-start | bytes 3145736 | tf_op jit(solution)/shard_map/ppermute | solution.py:401
  59.0 350.4 %reduce-scatter.2.cloned.1.call-start = ((), (), s32[]{:S(2)}) async-start(), calls=%async_computation.1 | async-start | bytes 4718592 | tf_op jit(solution)/shard_map/reduce_scatter | solution.py:672
  65.0 14.3 %collective-permute-start.10 = (bf16[512,1024]{1,0:T(8,128)(2,1)S(1)}, bf16[512,1024]{1,0:T(8,128)(2,1)S(1)}, u32[]{:S(2)}, u32[]{:S(2)}) collective-permute-start(bf16[512,1024]{1,0:T(8,128)(2,1)S(1)} %bitcast.248), channel_id=1, source_target_pairs={{0,1},{1,0},{2,3},{3,2},{4,5},{5,4},{6,7},{7,6},{8,9},{9,8},{10,11... | collective-permute-start | bytes 3145736 | tf_op jit(solution)/shard_map/ppermute | solution.py:401
  67.1 13.8 %collective-permute-start.12 = (bf16[512,1024]{1,0:T(8,128)(2,1)}, bf16[512,1024]{1,0:T(8,128)(2,1)S(1)}, u32[]{:S(2)}, u32[]{:S(2)}) collective-permute-start(bf16[512,1024]{1,0:T(8,128)(2,1)} %collective-permute-done.11), channel_id=1, source_target_pairs={{0,1},{1,0},{2,3},{3,2},{4,5},{5,4},{6,7},{7,6},{8,9},{9,8},{10,11... | collective-permute-start | bytes 3145736 | tf_op jit(solution)/shard_map/ppermute | solution.py:401
  77.5 14.0 %collective-permute-start.9 = (bf16[144,1024]{1,0:T(8,128)(2,1)S(1)}, bf16[144,1024]{1,0:T(8,128)(2,1)S(1)}, u32[]{:S(2)}, u32[]{:S(2)}) collective-permute-start(bf16[144,1024]{1,0:T(8,128)(2,1)S(1)} %collective-permute-done.2), channel_id=1, source_target_pairs={{0,8},{8,16},{16,24},{24,28},{28,20},{20,12},{12,4},{4,0},{1,9},{9... | collective-permute-start | bytes 884744 | tf_op jit(solution)/shard_map/ppermute | solution.py:345
  93.4 14.0 %collective-permute-start.17 = (bf16[1024,256]{1,0:T(8,128)(2,1)S(1)}, bf16[1024,256]{1,0:T(8,128)(2,1)S(1)}, u32[]{:S(2)}, u32[]{:S(2)}) collective-permute-start(bf16[1024,256]{1,0:T(8,128)(2,1)S(1)} %bitcast.252), channel_id=1, source_target_pairs={{0,2},{1,3},{2,0},{3,1},{4,6},{5,7},{6,4},{7,5},{8,10},{9,11},{10,... | collective-permute-start | bytes 1572872 | tf_op jit(solution)/shard_map/ppermute | solution.py:401
  95.2 49.3 %collective-permute-start.16 = (bf16[1024,256]{1,0:T(8,128)(2,1)S(1)}, bf16[1024,256]{1,0:T(8,128)(2,1)S(1)}, u32[]{:S(2)}, u32[]{:S(2)}) collective-permute-start(bf16[1024,256]{1,0:T(8,128)(2,1)S(1)} %bitcast.253), channel_id=1, source_target_pairs={{0,1},{1,0},{2,3},{3,2},{4,5},{5,4},{6,7},{7,6},{8,9},{9,8},{10,11... | collective-permute-start | bytes 1572872 | tf_op jit(solution)/shard_map/ppermute | solution.py:401
  107.4 37.1 %collective-permute-start.18 = (bf16[1024,256]{1,0:T(8,128)(2,1)S(1)}, bf16[1024,256]{1,0:T(8,128)(2,1)S(1)}, u32[]{:S(2)}, u32[]{:S(2)}) collective-permute-start(bf16[1024,256]{1,0:T(8,128)(2,1)S(1)} %collective-permute-done.17.refs_2_), channel_id=1, source_target_pairs={{0,1},{1,0},{2,3},{3,2},{4,5},{5,4},{6,7},{7,6},{8,9},{9,8},{10,11... | collective-permute-start | bytes 1572872 | tf_op jit(solution)/shard_map/ppermute | solution.py:401
  129.2 12.2 %collective-permute-start.15 = (bf16[1,512,256]{2,1,0:T(8,128)(2,1)S(1)}, bf16[1,512,256]{2,1,0:T(8,128)(2,1)S(1)}, u32[]{:S(2)}, u32[]{:S(2)}) collective-permute-start(bf16[1,512,256]{2,1,0:T(8,128)(2,1)S(1)} %get-tuple-element.105), channel_id=1, source_target_pairs={{0,3},{1,2},{2,1},{3,0},{4,7},{5,6},{6,5},{7,4},{8,11},{9,10},{10,... | collective-permute-start | bytes 786440 | tf_op jit(solution)/shard_map/ppermute | solution.py:401
  153.9 25.8 %collective-permute-start.20 = (bf16[512,1024]{1,0:T(8,128)(2,1)}, bf16[512,1024]{1,0:T(8,128)(2,1)}, u32[]{:S(2)}, u32[]{:S(2)}) collective-permute-start(bf16[512,1024]{1,0:T(8,128)(2,1)} %add_convert_fusion.8), channel_id=1, source_target_pairs={{0,2},{1,3},{2,0},{3,1},{4,6},{5,7},{6,4},{7,5},{8,10},{9,11},{10,... | collective-permute-start | bytes 3145736 | tf_op jit(solution)/shard_map/ppermute | solution.py:401
  155.0 31.4 %collective-permute-start.19 = (bf16[512,1024]{1,0:T(8,128)(2,1)}, bf16[512,1024]{1,0:T(8,128)(2,1)}, u32[]{:S(2)}, u32[]{:S(2)}) collective-permute-start(bf16[512,1024]{1,0:T(8,128)(2,1)} %add_convert_fusion.8), channel_id=1, source_target_pairs={{0,1},{1,0},{2,3},{3,2},{4,5},{5,4},{6,7},{7,6},{8,9},{9,8},{10,11... | collective-permute-start | bytes 3145736 | tf_op jit(solution)/shard_map/ppermute | solution.py:401
  213.4 35.6 %collective-permute-start.22 = (bf16[512,1024]{1,0:T(8,128)(2,1)}, bf16[512,1024]{1,0:T(8,128)(2,1)S(1)}, u32[]{:S(2)}, u32[]{:S(2)}) collective-permute-start(bf16[512,1024]{1,0:T(8,128)(2,1)} %unstack.33), channel_id=1, source_target_pairs={{0,1},{1,0},{2,3},{3,2},{4,5},{5,4},{6,7},{7,6},{8,9},{9,8},{10,11... | collective-permute-start | bytes 3145736 | tf_op jit(solution)/shard_map/ppermute | solution.py:401
  242.7 25.5 %collective-permute-start.24 = (bf16[512,1024]{1,0:T(8,128)(2,1)}, bf16[512,1024]{1,0:T(8,128)(2,1)}, u32[]{:S(2)}, u32[]{:S(2)}) collective-permute-start(bf16[512,1024]{1,0:T(8,128)(2,1)} %add_convert_fusion.7), channel_id=1, source_target_pairs={{0,2},{1,3},{2,0},{3,1},{4,6},{5,7},{6,4},{7,5},{8,10},{9,11},{10,... | collective-permute-start | bytes 3145736 | tf_op jit(solution)/shard_map/ppermute | solution.py:401
  276.5 13.9 %collective-permute-start.29 = (bf16[512,1024]{1,0:T(8,128)(2,1)S(1)}, bf16[512,1024]{1,0:T(8,128)(2,1)S(1)}, u32[]{:S(2)}, u32[]{:S(2)}) collective-permute-start(bf16[512,1024]{1,0:T(8,128)(2,1)S(1)} %unstack.39), channel_id=1, source_target_pairs={{0,1},{1,0},{2,3},{3,2},{4,5},{5,4},{6,7},{7,6},{8,9},{9,8},{10,11... | collective-permute-start | bytes 3145736 | tf_op jit(solution)/shard_map/ppermute | solution.py:401
  278.7 11.7 %collective-permute-start.28 = (bf16[1,512,256]{2,1,0:T(8,128)(2,1)S(1)}, bf16[1,512,256]{2,1,0:T(8,128)(2,1)S(1)}, u32[]{:S(2)}, u32[]{:S(2)}) collective-permute-start(bf16[1,512,256]{2,1,0:T(8,128)(2,1)S(1)} %get-tuple-element.102), channel_id=1, source_target_pairs={{0,3},{1,2},{2,1},{3,0},{4,7},{5,6},{6,5},{7,4},{8,11},{9,10},{10,... | collective-permute-start | bytes 786440 | tf_op jit(solution)/shard_map/ppermute | solution.py:401
  292.9 55.6 %collective-permute-start.35 = (bf16[1024,256]{1,0:T(8,128)(2,1)}, bf16[1024,256]{1,0:T(8,128)(2,1)S(1)}, u32[]{:S(2)}, u32[]{:S(2)}) collective-permute-start(bf16[1024,256]{1,0:T(8,128)(2,1)} %get-tuple-element.101), channel_id=1, source_target_pairs={{0,1},{1,0},{2,3},{3,2},{4,5},{5,4},{6,7},{7,6},{8,9},{9,8},{10,11... | collective-permute-start | bytes 1572872 | tf_op jit(solution)/shard_map/ppermute | solution.py:401
  293.7 64.8 %collective-permute-start.34 = (bf16[1024,256]{1,0:T(8,128)(2,1)}, bf16[1024,256]{1,0:T(8,128)(2,1)S(1)}, u32[]{:S(2)}, u32[]{:S(2)}) collective-permute-start(bf16[1024,256]{1,0:T(8,128)(2,1)} %get-tuple-element.100), channel_id=1, source_target_pairs={{0,1},{1,0},{2,3},{3,2},{4,5},{5,4},{6,7},{7,6},{8,9},{9,8},{10,11... | collective-permute-start | bytes 1572872 | tf_op jit(solution)/shard_map/ppermute | solution.py:401
  350.9 14.9 %collective-permute-start.36 = (bf16[1024,256]{1,0:T(8,128)(2,1)}, bf16[1024,256]{1,0:T(8,128)(2,1)S(1)}, u32[]{:S(2)}, u32[]{:S(2)}) collective-permute-start(bf16[1024,256]{1,0:T(8,128)(2,1)} %add_convert_fusion.10), channel_id=1, source_target_pairs={{0,2},{1,3},{2,0},{3,1},{4,6},{5,7},{6,4},{7,5},{8,10},{9,11},{10,... | collective-permute-start | bytes 1572872 | tf_op jit(solution)/shard_map/ppermute | solution.py:401
  356.2 32.7 %collective-permute-start.32 = (bf16[512,1024]{1,0:T(8,128)(2,1)}, bf16[512,1024]{1,0:T(8,128)(2,1)}, u32[]{:S(2)}, u32[]{:S(2)}) collective-permute-start(bf16[512,1024]{1,0:T(8,128)(2,1)} %get-tuple-element.91), channel_id=1, source_target_pairs={{0,1},{1,0},{2,3},{3,2},{4,5},{5,4},{6,7},{7,6},{8,9},{9,8},{10,11... | collective-permute-start | bytes 3145736 | tf_op jit(solution)/shard_map/ppermute | solution.py:401
  356.4 37.1 %collective-permute-start.30 = (bf16[512,1024]{1,0:T(8,128)(2,1)}, bf16[512,1024]{1,0:T(8,128)(2,1)}, u32[]{:S(2)}, u32[]{:S(2)}) collective-permute-start(bf16[512,1024]{1,0:T(8,128)(2,1)} %add_convert_fusion.6), channel_id=1, source_target_pairs={{0,2},{1,3},{2,0},{3,1},{4,6},{5,7},{6,4},{7,5},{8,10},{9,11},{10,... | collective-permute-start | bytes 3145736 | tf_op jit(solution)/shard_map/ppermute | solution.py:401
  369.7 18.2 %collective-permute-start.37 = (bf16[144,1024]{1,0:T(8,128)(2,1)}, bf16[144,1024]{1,0:T(8,128)(2,1)S(1)}, u32[]{:S(2)}, u32[]{:S(2)}) collective-permute-start(bf16[144,1024]{1,0:T(8,128)(2,1)} %get-tuple-element.98), channel_id=1, source_target_pairs={{0,4},{8,0},{16,8},{24,16},{28,24},{20,28},{12,20},{4,12},{1,5},{9... | collective-permute-start | bytes 884744 | tf_op jit(solution)/shard_map/ppermute | solution.py:345
  373.9 25.4 %collective-permute-start.25 = (bf16[512,1024]{1,0:T(8,128)(2,1)}, bf16[512,1024]{1,0:T(8,128)(2,1)}, u32[]{:S(2)}, u32[]{:S(2)}) collective-permute-start(bf16[512,1024]{1,0:T(8,128)(2,1)} %unstack.37), channel_id=1, source_target_pairs={{0,1},{1,0},{2,3},{3,2},{4,5},{5,4},{6,7},{7,6},{8,9},{9,8},{10,11... | collective-permute-start | bytes 3145736 | tf_op jit(solution)/shard_map/ppermute | solution.py:401
  374.4 36.4 %collective-permute-start.31 = (bf16[512,1024]{1,0:T(8,128)(2,1)}, bf16[512,1024]{1,0:T(8,128)(2,1)}, u32[]{:S(2)}, u32[]{:S(2)}) collective-permute-start(bf16[512,1024]{1,0:T(8,128)(2,1)} %get-tuple-element.90), channel_id=1, source_target_pairs={{0,1},{1,0},{2,3},{3,2},{4,5},{5,4},{6,7},{7,6},{8,9},{9,8},{10,11... | collective-permute-start | bytes 3145736 | tf_op jit(solution)/shard_map/ppermute | solution.py:401
  392.0 26.3 %collective-permute-start.33 = (bf16[512,1024]{1,0:T(8,128)(2,1)}, bf16[512,1024]{1,0:T(8,128)(2,1)}, u32[]{:S(2)}, u32[]{:S(2)}) collective-permute-start(bf16[512,1024]{1,0:T(8,128)(2,1)} %add_convert_fusion.4), channel_id=1, source_target_pairs={{0,2},{1,3},{2,0},{3,1},{4,6},{5,7},{6,4},{7,5},{8,10},{9,11},{10,... | collective-permute-start | bytes 3145736 | tf_op jit(solution)/shard_map/ppermute | solution.py:401
  408.6 24.2 %collective-permute-start.45 = (bf16[144,1024]{1,0:T(8,128)(2,1)S(1)}, bf16[144,1024]{1,0:T(8,128)(2,1)S(1)}, u32[]{:S(2)}, u32[]{:S(2)}) collective-permute-start(bf16[144,1024]{1,0:T(8,128)(2,1)S(1)} %get-tuple-element.97), channel_id=1, source_target_pairs={{0,8},{8,16},{16,24},{24,28},{28,20},{20,12},{12,4},{4,0},{1,9},{9... | collective-permute-start | bytes 884744 | tf_op jit(solution)/shard_map/ppermute | solution.py:345
  409.3 19.3 %collective-permute-start.41 = (bf16[128,2048]{1,0:T(8,128)(2,1)}, bf16[128,2048]{1,0:T(8,128)(2,1)S(1)}, u32[]{:S(2)}, u32[]{:S(2)}) collective-permute-start(bf16[128,2048]{1,0:T(8,128)(2,1)} %bitcast.264), channel_id=1, source_target_pairs={{0,2},{1,3},{2,0},{3,1},{4,6},{5,7},{6,4},{7,5},{8,10},{9,11},{10,... | collective-permute-start | bytes 1572872 | tf_op jit(solution)/shard_map/ppermute | solution.py:401
  421.2 14.3 %collective-permute-start.40 = (bf16[128,2048]{1,0:T(8,128)(2,1)S(1)}, bf16[128,2048]{1,0:T(8,128)(2,1)S(1)}, u32[]{:S(2)}, u32[]{:S(2)}) collective-permute-start(bf16[128,2048]{1,0:T(8,128)(2,1)S(1)} %bitcast.265), channel_id=1, source_target_pairs={{0,1},{1,0},{2,3},{3,2},{4,5},{5,4},{6,7},{7,6},{8,9},{9,8},{10,11... | collective-permute-start | bytes 1572872 | tf_op jit(solution)/shard_map/ppermute | solution.py:401
  (79 other events, 788.6 us)
Sparse Core Ops, SparseCore 0:
  59.1 80.0 all-gather.2
  293.8 93.0 reduce-scatter.1

commit v3 on v2

--- a/solution.py
+++ b/solution.py
@@ -38,6 +38,79 @@
 def dot_tn(left_side, right_side):
     return lax.dot_general(
         left_side, right_side, (((0,), (0,)), ((), ())), preferred_element_type=F32
+    )
+
+
+def project_kernel(rank_ref, *refs, parts):
+    del rank_ref
+    block_refs = refs[:parts]
+    weight_ref, gain_ref, shift_ref, bias_ref, normed_ref, mixed_ref = refs[parts:]
+    place = pl.program_id(0)
+    values = block_refs[0][0]
+    for part in range(1, parts):
+        values = jnp.where(place == part, block_refs[part][0], values)
+    values = values.astype(F32)
+    centered = values - jnp.mean(values, axis=-1, keepdims=True)
+    inverse = lax.rsqrt(jnp.mean(centered * centered, axis=-1, keepdims=True) + EPSILON)
+    normed = (centered * inverse * gain_ref[...] + shift_ref[...]).astype(BF16)
+    normed_ref[0, 0] = normed
+    mixed_ref[0, 0] = (dot_nn(normed, weight_ref[...]) + bias_ref[...]).astype(BF16)
+
+
+def project(blocks, weight, gain, shift, bias):
+    seqs, rows, model = blocks[0].shape
+    parts, wide = (len(blocks), weight.shape[1])
+    block = min(256, rows)
+    steps = rows // block
+
+    def block_spec(part):
+        def index_map(p, s, b, rank_ref):
+            seq = jnp.where(p < part, 0, jnp.where(p > part, seqs - 1, s))
+            row = jnp.where(p < part, 0, jnp.where(p > part, steps - 1, b))
+            return (seq, row, 0)
+
+        return pl.BlockSpec((1, block, model), index_map)
+
+    def whole_spec(*shape):
+        return pl.BlockSpec(shape, lambda p, s, b, rank_ref: (0, 0))
+
+    def out_spec(columns_count):
+        return pl.BlockSpec(
+            (1, 1, block, columns_count),
+            lambda p, s, b, rank_ref: (s, lax.bitwise_xor(rank_ref[0], p), b, 0),
+        )
+
+    return pl.pallas_call(
+        functools.partial(project_kernel, parts=parts),
+        grid_spec=pltpu.PrefetchScalarGridSpec(
+            num_scalar_prefetch=1,
+            grid=(parts, seqs, steps),
+            in_specs=[block_spec(part) for part in range(parts)]
+            + [
+                whole_spec(model, wide),
+                whole_spec(1, model),
+                whole_spec(1, model),
+                whole_spec(1, wide),
+            ],
+            out_specs=[out_spec(model), out_spec(wide)],
+        ),
+        out_shape=[
+            jax.ShapeDtypeStruct((seqs, parts, rows, model), BF16),
+            jax.ShapeDtypeStruct((seqs, parts, rows, wide), BF16),
+        ],
+        compiler_params=pltpu.CompilerParams(vmem_limit_bytes=VMEM_BYTES),
+        cost_estimate=pl.CostEstimate(
+            flops=4 * parts * seqs * rows * model * wide,
+            bytes_accessed=parts * seqs * rows * (4 * model + 2 * wide) + 2 * model * wide,
+            transcendentals=parts * seqs * rows,
+        ),
+    )(
+        lax.axis_index("seq").astype(jnp.int32).reshape(1),
+        *blocks,
+        weight,
+        gain.reshape(1, model),
+        shift.reshape(1, model),
+        bias.reshape(1, wide),
     )
 
 
@@ -128,6 +201,7 @@
     grad_ref,
     log_ref,
     result_ref,
+    sum_ref,
     query_heads,
     key_heads,
     grad_heads,
@@ -209,11 +283,15 @@
 
     def finish(index, carry):
         rows = pl.ds(pl.multiple_of(index * block, block), block)
-        result_ref[0, rows, 0:width] = (grad_query[rows, :] * SCALE).astype(BF16)
-        result_ref[0, rows, width : 2 * width] = grad_key[rows, :].astype(BF16)
-        result_ref[0, rows, 2 * width : 3 * width] = grad_value[rows, :].astype(BF16)
+        pieces = (grad_query[rows, :] * SCALE, grad_key[rows, :], grad_value[rows, :])
+        for place, piece in enumerate(pieces):
+            piece = piece.astype(BF16)
+            columns_here = slice(place * width, (place + 1) * width)
+            result_ref[0, rows, columns_here] = piece
+            sum_ref[0, 0:1, columns_here] += jnp.sum(piece.astype(F32), axis=0, keepdims=True)
         return carry
 
+    sum_ref[...] = jnp.zeros_like(sum_ref)
     lax.fori_loop(0, blocks, finish, 0)
 
 
@@ -230,8 +308,14 @@
             pl.BlockSpec((1, length, width), lambda s: (s, 0, 0)),
             pl.BlockSpec((1, LOG_ROWS, length), lambda s: (s, 0, 0)),
         ],
-        out_specs=pl.BlockSpec((1, length, 3 * width), lambda s: (s, 0, 0)),
-        out_shape=jax.ShapeDtypeStruct((seqs, length, 3 * width), BF16),
+        out_specs=[
+            pl.BlockSpec((1, length, 3 * width), lambda s: (s, 0, 0)),
+            pl.BlockSpec((1, 8, 3 * width), lambda s: (s, 0, 0)),
+        ],
+        out_shape=[
+            jax.ShapeDtypeStruct((seqs, length, 3 * width), BF16),
+            jax.ShapeDtypeStruct((seqs, 8, 3 * width), F32),
+        ],
         scratch_shapes=[
             pltpu.VMEM((heads, length, width), BF16),
             pltpu.VMEM((heads, length, width), BF16),
@@ -250,19 +334,16 @@
     )(mixed, attended, grad_attended, logs)
 
 
-def feed_kernel(
-    normed_ref,
-    cot_ref,
-    fc_ref,
-    proj_ref,
-    bias_ref,
-    active_ref,
-    grad_ref,
-    back_ref,
-    ahead_ref,
-    sum_ref,
-):
-    hidden = dot_nn(normed_ref[...], fc_ref[...]) + bias_ref[...]
+def feed_kernel(*refs, parts, steps):
+    normed_refs, rest = (refs[:parts], refs[parts:])
+    cot_ref, fc_ref, proj_ref, bias_ref, active_ref, grad_ref = rest[:6]
+    back_refs, ahead_refs = (rest[6 : 6 + parts], rest[6 + parts : 6 + 2 * parts])
+    sum_ref = rest[6 + 2 * parts]
+    index = pl.program_id(0)
+    normed = normed_refs[0][...]
+    for place in range(1, parts):
+        normed = jnp.where(index >= place * steps, normed_refs[place][...], normed)
+    hidden = dot_nn(normed, fc_ref[...]) + bias_ref[...]
     grad_active = dot_nt(cot_ref[...], proj_ref[...])
     square = hidden * hidden
     curve = jnp.tanh(ROOT_COEF * hidden * (1.0 + 0.044715 * square))
@@ -274,54 +355,70 @@
     grad = (grad_active * slope).astype(BF16)
     active_ref[...] = active
     grad_ref[...] = grad
-    back_ref[...] = dot_nt(grad, fc_ref[...]).astype(BF16)
-    ahead_ref[...] = dot_nn(active, proj_ref[...]).astype(BF16)
+    back = dot_nt(grad, fc_ref[...]).astype(BF16)
+    ahead = dot_nn(active, proj_ref[...]).astype(BF16)
+    for place in range(parts):
+
+        @pl.when(jnp.logical_and(index >= place * steps, index < (place + 1) * steps))
+        def _(place=place):
+            back_refs[place][...] = back
+            ahead_refs[place][...] = ahead
+
     sums = jnp.sum(grad.astype(F32), axis=0, keepdims=True)
 
-    @pl.when(pl.program_id(0) == 0)
+    @pl.when(index == 0)
     def _():
         sum_ref[...] = jnp.zeros_like(sum_ref)
 
     sum_ref[...] += sums
 
 
-def feed(normed, cotangent, share_fc, share_proj, bias):
-    rows, model = normed.shape
-    width = share_fc.shape[1]
+def feed(blocks, cotangent, weights, bias, width):
+    rows, model = blocks[0].shape
+    parts = len(blocks)
     block = min(256, rows)
-    row_spec = pl.BlockSpec((block, model), lambda i: (i, 0))
+    steps = rows // block
+
+    def part_spec(place):
+        return pl.BlockSpec((block, model), lambda i: (jnp.clip(i - place * steps, 0, steps - 1), 0))
+
+    part_specs = [part_spec(place) for place in range(parts)]
+    part_shapes = [jax.ShapeDtypeStruct((rows, model), BF16)] * parts
     wide_spec = pl.BlockSpec((block, width), lambda i: (i, 0))
-    return pl.pallas_call(
-        feed_kernel,
-        grid=(rows // block,),
-        in_specs=[
-            row_spec,
-            row_spec,
+    wide_shape = jax.ShapeDtypeStruct((parts * rows, width), BF16)
+    if isinstance(weights, tuple):
+        share_fc, share_proj = weights
+        proj_place = 0
+    else:
+        share_fc = share_proj = weights
+        proj_place = 1
+    results = pl.pallas_call(
+        functools.partial(feed_kernel, parts=parts, steps=steps),
+        grid=(parts * steps,),
+        in_specs=part_specs
+        + [
+            pl.BlockSpec((block, model), lambda i: (i, 0)),
             pl.BlockSpec((model, width), lambda i: (0, 0)),
-            pl.BlockSpec((width, model), lambda i: (0, 0)),
+            pl.BlockSpec((width, model), lambda i: (0, proj_place)),
             pl.BlockSpec((1, width), lambda i: (0, 0)),
         ],
-        out_specs=[
-            wide_spec,
-            wide_spec,
-            row_spec,
-            row_spec,
-            pl.BlockSpec((1, width), lambda i: (0, 0)),
-        ],
-        out_shape=[
-            jax.ShapeDtypeStruct((rows, width), BF16),
-            jax.ShapeDtypeStruct((rows, width), BF16),
-            jax.ShapeDtypeStruct((rows, model), BF16),
-            jax.ShapeDtypeStruct((rows, model), BF16),
-            jax.ShapeDtypeStruct((1, width), F32),
-        ],
+        out_specs=[wide_spec, wide_spec]
+        + part_specs
+        + part_specs
+        + [pl.BlockSpec((1, width), lambda i: (0, 0))],
+        out_shape=[wide_shape, wide_shape]
+        + part_shapes
+        + part_shapes
+        + [jax.ShapeDtypeStruct((1, width), F32)],
         compiler_params=pltpu.CompilerParams(vmem_limit_bytes=VMEM_BYTES),
         cost_estimate=pl.CostEstimate(
-            flops=14 * rows * model * width,
-            bytes_accessed=8 * rows * model + 4 * rows * width + 4 * model * width,
-            transcendentals=rows * width,
+            flops=14 * parts * rows * model * width,
+            bytes_accessed=parts * rows * (8 * model + 4 * width) + 4 * model * width,
+            transcendentals=parts * rows * width,
         ),
-    )(normed, cotangent, share_fc, share_proj, bias)
+    )(*blocks, cotangent, share_fc, share_proj, bias)
+    back, ahead = (results[2 : 2 + parts], results[2 + parts : 2 + 2 * parts])
+    return results[0], results[1], back, ahead, results[2 + 2 * parts]
 
 
 def ring_order(shards):
@@ -348,18 +445,18 @@
 def ring_lookup(distance):
     order = ring_order(lax.axis_size("dp"))
     shards = len(order)
-    table = [0] * shards
-    for place, device in enumerate(order):
-        table[device] = order[(place + distance) % shards]
-    return jnp.array(table, jnp.int32)[lax.axis_index("dp")]
-
-
-def ring_gather(share, ties):
+    own = lax.axis_index("dp")
+    found = jnp.int32(order[distance % shards])
+    for place in range(1, shards):
+        found = jnp.where(own == order[place], order[(place + distance) % shards], found)
+    return found
+
+
+def ring_gather(share, ties, made):
     shards = lax.axis_size("dp")
     full = jnp.zeros((shards,) + share.shape, share.dtype)
     full = lax.dynamic_update_index_in_dim(full, share, lax.axis_index("dp"), 0)
     upward = downward = share
-    tied = {}
     for step in range(1, shards // 2 + 1):
         upward = ring_move(upward, 1)
         if 2 * step < shards:
@@ -367,12 +464,12 @@
         full = lax.dynamic_update_index_in_dim(full, upward, ring_lookup(-step), 0)
         if 2 * step < shards:
             full = lax.dynamic_update_index_in_dim(full, downward, ring_lookup(step), 0)
-        if step in ties:
-            upward, tied[step] = lax.optimization_barrier((upward, ties[step]))
-    return full, tied
-
-
-def ring_scatter(parts, tie):
+        for name, make in ties.get(step, ()):
+            upward, made[name] = lax.optimization_barrier((upward, make()))
+    return full
+
+
+def ring_scatter(parts, ties, made):
     shards = parts.shape[0]
     half = shards // 2
 
@@ -384,8 +481,8 @@
         held = own(-distance)
         if downward is not None:
             held = (held.astype(F32) + downward.astype(F32)).astype(BF16)
-        if distance == 1:
-            held, tie = lax.optimization_barrier((held, tie))
+        for name, make in ties.get(distance, ()):
+            held, made[name] = lax.optimization_barrier((held, make()))
         downward = ring_move(held, -1)
         if distance < half or 2 * half < shards:
             held = own(distance)
@@ -393,7 +490,7 @@
                 held = (held.astype(F32) + upward.astype(F32)).astype(BF16)
             upward = ring_move(held, 1)
     total = own(0).astype(F32) + downward.astype(F32)
-    return (total if upward is None else total + upward.astype(F32)), tie
+    return total if upward is None else total + upward.astype(F32)
 
 
 def swap(array, offset):
@@ -447,33 +544,44 @@
     ]
 
 
-def columns_kernel(rank_ref, *refs, groups, size):
-    blocks, full_ref = (refs[:-1], refs[-1])
-    ranks = len(blocks)
+def columns_kernel(rank_ref, *refs, pieces, ranks):
+    blocks, fulls = (refs[:ranks], refs[ranks:])
     for offset, block_ref in enumerate(blocks):
         owner = lax.bitwise_xor(rank_ref[0, 0], offset)
-        for group in range(groups):
-            start = pl.multiple_of((owner + group * ranks) * size, size)
-            piece = block_ref[:, group * size : (group + 1) * size]
-            full_ref[:, pl.ds(start, size)] = piece.astype(full_ref.dtype)
-
-
-def columns(blocks, groups, dtype):
-    rows, wide = blocks[0].shape
-    ranks, size = (len(blocks), wide // groups)
+        for (first, groups, size), full_ref in zip(pieces, fulls):
+            for group in range(groups):
+                start = pl.multiple_of((owner + group * ranks) * size, size)
+                place = first + group * size
+                piece = block_ref[0 : full_ref.shape[0], place : place + size]
+                full_ref[:, pl.ds(start, size)] = piece.astype(full_ref.dtype)
+
+
+def columns(blocks, pieces, dtype, rows=None):
+    rows = blocks[0].shape[0] if rows is None else rows
+    ranks = len(blocks)
     rank = lax.axis_index("seq")
-    if size % 128:
-        shaped = [block.reshape(rows, groups, 1, size) for block in blocks]
-        return placed(shaped, 2).reshape(rows, ranks * wide).astype(dtype)
+    if any(size % 128 for _, _, size in pieces):
+        results = []
+        for first, groups, size in pieces:
+            shaped = [
+                block[:rows, first : first + groups * size].reshape(rows, groups, 1, size)
+                for block in blocks
+            ]
+            results.append(placed(shaped, 2).reshape(rows, ranks * groups * size).astype(dtype))
+        return results
+    wide = sum(groups * size for _, groups, size in pieces) * ranks
     return pl.pallas_call(
-        functools.partial(columns_kernel, groups=groups, size=size),
+        functools.partial(columns_kernel, pieces=pieces, ranks=ranks),
         in_specs=[pl.BlockSpec(memory_space=pltpu.SMEM)]
         + [pl.BlockSpec(memory_space=pltpu.VMEM)] * ranks,
-        out_specs=pl.BlockSpec(memory_space=pltpu.VMEM),
-        out_shape=jax.ShapeDtypeStruct((rows, ranks * wide), dtype),
+        out_specs=[pl.BlockSpec(memory_space=pltpu.VMEM)] * len(pieces),
+        out_shape=[
+            jax.ShapeDtypeStruct((rows, ranks * groups * size), dtype)
+            for _, groups, size in pieces
+        ],
         compiler_params=pltpu.CompilerParams(vmem_limit_bytes=VMEM_BYTES),
         cost_estimate=pl.CostEstimate(
-            flops=rows * wide * ranks, bytes_accessed=6 * rows * wide * ranks, transcendentals=0
+            flops=rows * wide, bytes_accessed=6 * rows * wide, transcendentals=0
         ),
     )(rank.astype(jnp.int32).reshape(1, 1), *blocks)
 
@@ -494,11 +602,13 @@
 
 
 def vector_rows(vectors, columns_count):
-    padded = [
-        jnp.pad(item, ((0, 0), (0, columns_count - item.shape[1])))[:, None] for item in vectors
-    ]
-    stacked = jnp.concatenate(padded, axis=1)
-    return jnp.pad(stacked, ((0, 0), (0, -stacked.shape[1] % 16), (0, 0)))
+    size = max(item.shape[1] for item in vectors)
+    stacked = jnp.stack(
+        [jnp.pad(item, ((0, 0), (0, size - item.shape[1]))) for item in vectors], axis=1
+    )
+    return jnp.pad(
+        stacked, ((0, 0), (0, -stacked.shape[1] % 16), (0, columns_count - size))
+    )
 
 
 def per_device(
@@ -531,6 +641,7 @@
     tokens_own = tokens.reshape(seqs * rows, model)
     cot_own = cotangent.reshape(seqs * rows, model)
     gather_columns = 4 * width
+    *low_bits, top_bit = bits_up()
 
     def share_of(array, groups):
         size = array.shape[1] // (groups * ranks)
@@ -559,31 +670,39 @@
         ],
         axis=0,
     )
-    proj_share = lax.dynamic_slice_in_dim(w_proj, rank * units, units, 0)
-    feed_share = jnp.concatenate(
-        share_of(w_fc, shards) + [proj_share.reshape(part, units * model // part)], axis=1
-    )
-
-    all_tokens = placed(gather_offsets(tokens), 1).reshape(seqs * length, model)
-    token_values = all_tokens.astype(F32)
-    average = jnp.mean(token_values, axis=-1, keepdims=True)
-    centered = token_values - average
-    inverse_all = lax.rsqrt(jnp.mean(centered * centered, axis=-1, keepdims=True) + EPSILON)
-
+
+    token_blocks = gather_offsets(tokens)
     steps = shards // 2
-    middle_step = max(1, steps // 2)
-    first_gather, tied = ring_gather(
+    middle_step = max(2, steps // 2)
+    made = {}
+
+    def feed_share():
+        wide, tall = made["feed"]
+        tall = lax.dynamic_slice_in_dim(tall, rank * units, units, 0)
+        tall = tall.reshape(part, units * model // part)
+        return jnp.concatenate(share_of(wide, shards) + [tall], axis=1)
+
+    full = ring_gather(
         packed,
-        {middle_step: (feed_share,), steps - 1: (average, inverse_all, all_tokens)},
-    )
-    (feed_share,) = tied[middle_step]
-    average, inverse_all, all_tokens = tied[steps - 1]
-    second_gather = lax.all_gather(feed_share, "dp", axis=0)
-    share_fc = second_gather[:, :, :hidden_width].reshape(model, hidden_width)
-    share_proj = second_gather[:, :, hidden_width:].reshape(hidden_width, model)
-    full_qkv = first_gather[:, :part, : 3 * width].reshape(model, 3 * width)
-    attn_columns = first_gather[:, :part, 3 * width :].reshape(model, width)
-    vector_block = first_gather[:, part:].astype(F32)
+        {
+            1: [("feed", lambda: (w_fc, w_proj))],
+            middle_step: [("tokens", lambda: token_blocks)],
+            steps - 1: [("share", feed_share)],
+        },
+        made,
+    )
+    token_blocks = made["tokens"]
+    second_gather = lax.all_gather(made["share"], "dp", axis=0)
+    if units == part and hidden_width == model:
+        feed_weights = second_gather.reshape(model, 2 * model)
+    else:
+        feed_weights = (
+            second_gather[:, :, :hidden_width].reshape(model, hidden_width),
+            second_gather[:, :, hidden_width:].reshape(hidden_width, model),
+        )
+    full_qkv = full[:, :part, : 3 * width].reshape(model, 3 * width)
+    attn_columns = full[:, :part, 3 * width :].reshape(model, width)
+    vector_block = full[:, part:].astype(F32)
 
     def vector(index):
         return vector_block[:, index, :part].reshape(model)
@@ -600,49 +719,63 @@
     )
     fc_bias = lax.dynamic_index_in_dim(vector_block, 8 + rank, 1, keepdims=False)
     fc_bias = fc_bias[:, :units].reshape(hidden_width)
-    cot_blocks = gather_offsets(cot_own)
     half = ranks // 2
-    near_cot = jnp.concatenate(cot_blocks[:half], axis=0)
-    far_cot = jnp.concatenate(cot_blocks[half:], axis=0)
-
-    unit_all = (all_tokens.astype(F32) - average) * inverse_all
-    normed = (unit_all * gain_first + shift_first).astype(BF16)
     joint_bias = jnp.concatenate([query_bias, jnp.zeros_like(query_bias), value_bias])
-    mixed = (dot_nn(normed, full_qkv) + joint_bias).astype(BF16)
+    normed, mixed = project(token_blocks, full_qkv, gain_first, shift_first, joint_bias)
+    normed = normed.reshape(seqs * length, model)
     mixed = mixed.reshape(seqs, length, 3 * width)
-    mixed, near_cot, far_cot = lax.optimization_barrier((mixed, near_cot, far_cot))
+    mixed, cot_sent, attn_columns, attn_far = lax.optimization_barrier(
+        (mixed, cot_own, attn_columns, swap(attn_columns, top_bit))
+    )
+    cot_far = swap(cot_sent, top_bit)
     attended, logs = attend(mixed, width)
+    attended, cot_far, cot_near = lax.optimization_barrier((attended, cot_far, cot_own))
+    near_cot = jnp.concatenate(gather_offsets(cot_near, low_bits), axis=0)
+    far_cot = jnp.concatenate(gather_offsets(cot_far, low_bits), axis=0)
 
     sent = picked(attended, 1)
     arrived = [sent[0]] + [swap(sent[offset], offset) for offset in range(1, ranks)]
-    joined = columns([item.reshape(seqs * rows, width) for item in arrived], 1, BF16)
-    full_attn = columns(gather_offsets(attn_columns), 1, BF16)
+    attn_blocks = gather_offsets(attn_columns, low_bits) + gather_offsets(attn_far, low_bits)
+    (full_attn,) = columns(attn_blocks, ((0, 1, width),), BF16)
+    arrived, full_attn, near_cot, far_cot = lax.optimization_barrier(
+        (arrived, full_attn, near_cot, far_cot)
+    )
+    (joined,) = columns(
+        [item.reshape(seqs * rows, width) for item in arrived], ((0, 1, width),), BF16
+    )
 
     inputs = tokens_own.astype(F32)
     middle = inputs + (dot_nn(joined, full_attn) + attn_bias)
     unit_two, inverse_two = row_stats(middle)
     normed_two = (unit_two * gain_second + shift_second).astype(BF16)
-    *low_bits, top_bit = bits_up()
-    near_two = jnp.concatenate(gather_offsets(normed_two, low_bits), axis=0)
-    far_two = jnp.concatenate(gather_offsets(swap(normed_two, top_bit), low_bits), axis=0)
+    near_blocks = gather_offsets(normed_two, low_bits)
+    far_own = swap(normed_two, top_bit)
     feed_bias = fc_bias.reshape(1, hidden_width)
     near_active, near_grad, near_back, near_ahead, near_sum = feed(
-        near_two, near_cot, share_fc, share_proj, feed_bias
-    )
+        near_blocks, near_cot, feed_weights, feed_bias, hidden_width
+    )
+    far_own, near_active = lax.optimization_barrier((far_own, near_active))
+    far_blocks = gather_offsets(far_own, low_bits)
     far_active, far_grad, far_back, far_ahead, far_sum = feed(
-        far_two, far_cot, share_fc, share_proj, feed_bias
-    )
-
-    def reduce_halves(near, far):
-        blocks = (half, seqs * rows, model)
-        far_part = reduce_offsets(list(far.reshape(blocks)), low_bits).astype(BF16)
-        near_part = reduce_offsets(list(near.reshape(blocks)), low_bits)
-        return near_part.astype(F32), swap(far_part, top_bit)
-
-    near_part, far_part = reduce_halves(near_back, far_back)
-    grad_normed_two = near_part + far_part.astype(F32)
+        far_blocks, far_cot, feed_weights, feed_bias, hidden_width
+    )
+    near_part = reduce_offsets(near_back, low_bits)
+    far_part = reduce_offsets(far_back, low_bits).astype(BF16)
+    far_part, far_active, far_grad = lax.optimization_barrier((far_part, far_active, far_grad))
+    grad_normed_two = near_part.astype(F32) + swap(far_part, top_bit).astype(F32)
+    near_two = jnp.concatenate(near_blocks, axis=0)
+    far_two = jnp.concatenate(far_blocks, axis=0)
 
     upstream = cot_own.astype(F32)
+    grad_w_proj = dot_tn(near_active, near_cot) + dot_tn(far_active, far_cot)
+    grad_w_proj = grad_w_proj.astype(BF16).reshape(shards, part, units * model // part)
+    grad_w_fc = dot_tn(near_two, near_grad) + dot_tn(far_two, far_grad)
+    grad_w_fc = grad_w_fc.astype(BF16).reshape(shards, part, hidden_width)
+    grad_bias_fc = (near_sum + far_sum).reshape(hidden_width)
+    grad_bias_proj = jnp.sum(upstream, axis=0)
+    first_parts = jnp.concatenate([grad_w_fc, grad_w_proj], axis=2)
+    first_scatter = lax.psum_scatter(first_parts, "dp", scatter_dimension=0)
+    grad_normed_two, _ = lax.optimization_barrier((grad_normed_two, first_parts))
     grad_gain_two = jnp.sum(grad_normed_two * unit_two, axis=0)
     grad_shift_two = jnp.sum(grad_normed_two, axis=0)
     grad_middle = upstream + norm_back(grad_normed_two, gain_second, unit_two, inverse_two)
@@ -654,31 +787,25 @@
     ]
     grad_attended = placed(grad_arrived, 1)
 
-    grad_w_proj = dot_tn(near_active, near_cot) + dot_tn(far_active, far_cot)
-    grad_w_proj = grad_w_proj.astype(BF16).reshape(shards, part, units * model // part)
-    grad_w_fc = dot_tn(near_two, near_grad) + dot_tn(far_two, far_grad)
-    grad_w_fc = grad_w_fc.astype(BF16).reshape(shards, part, hidden_width)
-    grad_bias_fc = (near_sum + far_sum).reshape(hidden_width)
-    grad_bias_proj = jnp.sum(upstream, axis=0)
-    first_parts = jnp.concatenate([grad_w_fc, grad_w_proj], axis=2)
-    near_ahead, far_ahead, _ = lax.optimization_barrier((near_ahead, far_ahead, grad_branch))
-    ahead_far = reduce_offsets(
-        list(far_ahead.reshape(half, seqs * rows, model)), low_bits
-    ).astype(BF16)
-    grad_attn_part = dot_tn(joined, grad_branch).astype(BF16)
-    grad_attended, first_parts, ahead_far, grad_attn_part = lax.optimization_barrier(
-        (grad_attended, first_parts, ahead_far, grad_attn_part)
-    )
-    first_scatter = lax.psum_scatter(first_parts, "dp", scatter_dimension=0)
+    ahead, _ = lax.optimization_barrier(((near_ahead, far_ahead), grad_branch))
+    near_ahead, far_ahead = ahead
+    ahead_far = reduce_offsets(far_ahead, low_bits).astype(BF16)
+    grad_attn_part = picked(dot_tn(joined, grad_branch).astype(BF16), 1)
+    attn_near = reduce_offsets(grad_attn_part[:half], low_bits)
+    attn_far = reduce_offsets(grad_attn_part[half:], low_bits).astype(BF16)
+    grad_attended, ahead_far, attn_far, attn_near = lax.optimization_barrier(
+        (grad_attended, ahead_far, attn_far, attn_near)
+    )
     ahead_far = swap(ahead_far, top_bit)
-    ahead_part = reduce_offsets(list(near_ahead.reshape(half, seqs * rows, model)), low_bits)
-    grad_w_attn = reduce_offsets(picked(grad_attn_part, 1)).astype(BF16)
+    attn_far = swap(attn_far, top_bit)
+    ahead_part = reduce_offsets(near_ahead, low_bits)
+    grad_w_attn = (attn_near.astype(F32) + attn_far.astype(F32)).astype(BF16)
     grad_bias_attn = jnp.sum(grad_branch, axis=0, dtype=F32)
 
-    grad_mixed = attend_back(mixed, attended, grad_attended, logs, width)
+    grad_mixed, column_sums = attend_back(mixed, attended, grad_attended, logs, width)
     grad_mixed = grad_mixed.reshape(seqs * length, 3 * width)
     grad_w_qkv = dot_tn(normed, grad_mixed)
-    column_sums = jnp.sum(grad_mixed, axis=0, dtype=F32)
+    column_sums = jnp.sum(column_sums[:, 0], axis=0)
     qkv_values = full_qkv.astype(F32)
     grad_shift_one = jnp.sum(qkv_values * column_sums, axis=1)
     grad_gain_one = (
@@ -717,25 +844,42 @@
         ],
         axis=1,
     )
-    back_one = dot_nt(grad_mixed, full_qkv).astype(BF16)
-    blocks_one = [
-        item.reshape(seqs * rows, model) for item in picked(back_one.reshape(seqs, length, model), 1)
-    ]
-    grad_normed = reduce_offsets(blocks_one)
-    fed = gather_offsets(first_scatter)
-    last_scatter, fed = ring_scatter(last_parts, fed)
-    rest = gather_offsets(last_scatter.astype(BF16))
+    made = {}
+
+    def far_sum():
+        back = dot_nt(made["mixed"], full_qkv).astype(BF16).reshape(seqs, length, model)
+        blocks = [item.reshape(seqs * rows, model) for item in picked(back, 1)]
+        far = reduce_offsets(blocks[half:], low_bits).astype(BF16)
+        near, far = lax.optimization_barrier((blocks[:half], far))
+        made["near"] = reduce_offsets(near, low_bits)
+        return far
+
+    last_scatter = ring_scatter(
+        last_parts,
+        {
+            steps: [("mixed", lambda: grad_mixed)],
+            max(steps - 1, 1): [("far", far_sum)],
+            max(steps - 2, 1): [("scatter", lambda: first_scatter)],
+        },
+        made,
+    )
+    far_arrived = swap(made["far"], top_bit)
+    fed_far = swap(made["scatter"], top_bit)
+    last_scatter = last_scatter.astype(BF16)
+    far_arrived, fed_far, _ = lax.optimization_barrier((far_arrived, fed_far, last_scatter))
+    grad_normed = made["near"].astype(F32) + far_arrived.astype(F32)
+    fed = gather_offsets(made["scatter"], low_bits) + gather_offsets(fed_far, low_bits)
+    rest = gather_offsets(last_scatter)
 
     _, ahead_far = lax.optimization_barrier((grad_mixed, ahead_far))
     output = (middle + ahead_part.astype(F32) + ahead_far.astype(F32) + proj_bias).astype(BF16)
     unit_one, inverse_one = row_stats(inputs)
     grad_tokens = grad_middle + norm_back(grad_normed, gain_first, unit_one, inverse_one)
 
-    out_fc = columns([item[:, :hidden_width] for item in fed], shards, F32)
+    (out_fc,) = columns(fed, ((0, shards, units),), F32)
     proj_blocks = [item[:, hidden_width:].reshape(units, model) for item in fed]
     out_proj = placed(proj_blocks, 0).astype(F32)
-    out_qkv = columns([item[:part, : 3 * width] for item in rest], 3, F32)
-    out_attn = columns([item[:part, 3 * width :] for item in rest], 1, F32)
+    out_qkv, out_attn = columns(rest, ((0, 3, width), (3 * width, 1, width)), F32, part)
     tails = [item[part:].astype(F32) for item in rest]
     summed = sum(tails)[:, :part]
     out_bias_fc = placed([item[8, :units] for item in tails], 0)

time: 478 us -> 398 us (0.83)
  local copies, waits for them, and re-layouts: 79.3 us -> 35.4 us
  other arithmetic: 60 us -> 39.7 us
  between operations: 29.1 us -> 15.1 us
  Pallas kernels: 98.1 us -> 111 us
  matrix products: 38.8 us -> 31.4 us
    ppermute x36, waiting for transfers between devices: 93.5 us -> 74.1 us  [swap(): lax.ppermute(array, 'seq', [(rank, rank ^ offset) for rank in range(ranks)])]
    ppermute x14, waiting for transfers between devices: 35.5 us -> 50.6 us  [ring_move(): return lax.ppermute(array, 'dp', pairs)]
    pallas_call x7, Pallas kernels: 41.7 us -> 54 us  [the longest x2 31.3 us: feed(): pl.pallas_call(functools.partial(feed_kernel, parts=parts, steps=steps),...]
    slice x11 -> x5, local copies, waits for them, and re-layouts: 12.8 us -> 3.77 us  [the longest x1 1.46 us: per_device(): full_qkv = full[:, :part, :3 * width].reshape(model, 3 * width)]
    dot_general x2 -> x1, matrix products: 11.5 us -> 2.58 us  [dot_nn(): lax.dot_general(left_side, right_side, (((1,), (0,)), ((), ())), preferre...]
    reduce_sum x3 -> x0, other arithmetic: 8.38 us -> none  [the longest x1 2.99 us: per_device(): jnp.mean(centered * centered, axis=-1, keepdims=True) + EPSILON]
    broadcast_in_dim x24 -> x0, local copies, waits for them, and re-layouts: 6.87 us -> none  [vector_rows(): jnp.pad(item, ((0, 0), (0, columns_count - item.shape[1])))[:, None]]
    dynamic_update_slice x16 -> x12, local copies, waits for them, and re-layouts: 9.09 us -> 2.48 us  [placed(): lax.dynamic_update_slice_in_dim(full, block, (rank ^ offset) * size, axis)]
  transfers between devices with their start and end apart: 52 -> 52, of which waited for: 18 -> 25; matrix products, arithmetic and copies ran while one was open for 32% -> 23% of each run, Pallas kernels for 17% -> 24%
where the time goes in v3:
time: 398 us; the launch traced here: 394 us
  waiting for transfers between devices  125 us (31%)
  Pallas kernels  111 us (28%)
  other arithmetic  39.7 us (10%)
  starting transfers between devices  36.1 us (9%)
  local copies, waits for them, and re-layouts  35.4 us (9%)
  matrix products  31.4 us (8%)
  between operations  15.1 us (4%)
    ppermute x36, waiting for transfers between devices, swap(): lax.ppermute(array, 'seq', [(rank, rank ^ offset) for rank in range(ranks)])  74.1 us
    ppermute x14, waiting for transfers between devices, ring_move(): return lax.ppermute(array, 'dp', pairs)  50.6 us
    pallas_call x1, Pallas kernels, attend_back(): pl.pallas_call(functools.partial(attend_back_kernel, block=block, width=w...  39.1 us
    pallas_call x2, Pallas kernels, feed(): pl.pallas_call(functools.partial(feed_kernel, parts=parts, steps=steps),...  31.3 us
    dot_general x6, matrix products, dot_tn(): lax.dot_general(left_side, right_side, (((0,), (0,)), ((), ())), preferre...  23.7 us
    ppermute x36, starting transfers between devices, swap(): lax.ppermute(array, 'seq', [(rank, rank ^ offset) for rank in range(ranks)])  20.5 us
    pallas_call x1, Pallas kernels, attend(): pl.pallas_call(functools.partial(attend_kernel, block=block, width=width)...  17.9 us
    ppermute x14, starting transfers between devices, ring_move(): return lax.ppermute(array, 'dp', pairs)  15.6 us
  transfers between devices with their start and end apart: 52, of which 25 were waited for; matrix products, arithmetic and copies ran while one was open for 23% of the time, Pallas kernels for 24%

profile of v3, /device:TPU:0, one launch (start us, length us, event | category | flops | bytes accessed | tf_op | source)
XLA Modules:
  0.0 393.5 jit_solution(1046727101755141950)
XLA Ops:
  7.2 3.0 collective-permute-start.3
  15.3 6.1 %collective-permute-done = bf16[144,1024]{1,0:T(8,128)(2,1)S(1)} collective-permute-done((bf16[144,1024]{1,0:T(8,128)(2,1)S(1)}, bf16[144,1024]{1,0:T(8,128)(2,1)S(1)}, u32[]{:S(2)}, u32[]{:S(2)}) %collective-permute-start) | collective-permute-done | bytes 294944 | tf_op jit(solution)/shard_map/ppermute | solution.py:442
  25.3 8.4 %collective-permute-done.3.refs_2_ = bf16[1,512,1024]{2,1,0:T(8,128)(2,1)} collective-permute-done((bf16[1,512,1024]{2,1,0:T(8,128)(2,1)}, bf16[1,512,1024]{2,1,0:T(8,128)(2,1)}, u32[]{:S(2)}, u32[]{:S(2)}) %collective-permute-start.3) | collective-permute-done | bytes 1048608 | tf_op jit(solution)/shard_map/ppermute | solution.py:498
  47.4 7.1 %collective-permute-done.7 = bf16[144,1024]{1,0:T(8,128)(2,1)S(1)} collective-permute-done((bf16[144,1024]{1,0:T(8,128)(2,1)}, bf16[144,1024]{1,0:T(8,128)(2,1)S(1)}, u32[]{:S(2)}, u32[]{:S(2)}) %collective-permute-start.7) | collective-permute-done | bytes 294944 | tf_op jit(solution)/shard_map/ppermute | solution.py:442
  56.1 6.1 %collective-permute-done.9 = bf16[144,1024]{1,0:T(8,128)(2,1)} collective-permute-done((bf16[144,1024]{1,0:T(8,128)(2,1)S(1)}, bf16[144,1024]{1,0:T(8,128)(2,1)}, u32[]{:S(2)}, u32[]{:S(2)}) %collective-permute-start.9) | collective-permute-done | bytes 294944 | tf_op jit(solution)/shard_map/ppermute | solution.py:442
  68.5 11.4 %shard_map.262 = (bf16[1,4,512,1024]{3,2,1,0:T(8,128)(2,1)}, bf16[1,4,512,768]{3,2,1,0:T(8,128)(2,1)}) custom-call(s32[1]{0:T(128)} %bitcast.2.rank_ref, bf16[1,512,1024]{2,1,0:T(8,128)(2,1)} %refs_0_, bf16[1,512,1024]{2,1,0:T(8,128)(2,1)} %collective-permute-done.2.refs_1_, bf16[1,512,1024]{2,1,0:T(8,128)(2,1)} %collective-permute-done.3.refs_2_, ...), custom_call_target="tpu_custom_call" | custom-call | flops 6442450944 | bytes 13107200 | tf_op jit(solution)/shard_map/pallas_call | solution.py:83
  80.4 17.9 %shard_map.263 = (bf16[1,2048,256]{2,1,0:T(8,128)(2,1)}, f32[1,8,2048]{2,1,0:T(8,128)}) custom-call(bf16[1,2048,768]{2,1,0:T(8,128)(2,1)} %bitcast.252), custom_call_target="tpu_custom_call" | custom-call | flops 30064771072 | bytes 4194304 | tf_op jit(solution)/shard_map/pallas_call | solution.py:177
  98.3 4.1 %collective-permute-done.11 = bf16[512,1024]{1,0:T(8,128)(2,1)S(1)} collective-permute-done((bf16[512,1024]{1,0:T(8,128)(2,1)S(1)}, bf16[512,1024]{1,0:T(8,128)(2,1)S(1)}, u32[]{:S(2)}, u32[]{:S(2)}) %collective-permute-start.11) | collective-permute-done | bytes 1048608 | tf_op jit(solution)/shard_map/ppermute | solution.py:498
  103.4 4.2 %collective-permute-done.15.refs_1_ = bf16[1024,256]{1,0:T(8,128)(2,1)} collective-permute-done((bf16[1024,256]{1,0:T(8,128)(2,1)}, bf16[1024,256]{1,0:T(8,128)(2,1)}, u32[]{:S(2)}, u32[]{:S(2)}) %collective-permute-start.15) | collective-permute-done | bytes 524320 | tf_op jit(solution)/shard_map/ppermute | solution.py:498
  108.4 3.2 shard_map.264
  118.5 3.2 collective-permute-done.13
  121.7 4.5 %collective-permute-done.14 = bf16[1,512,256]{2,1,0:T(8,128)(2,1)S(1)} collective-permute-done((bf16[1,512,256]{2,1,0:T(8,128)(2,1)S(1)}, bf16[1,512,256]{2,1,0:T(8,128)(2,1)S(1)}, u32[]{:S(2)}, u32[]{:S(2)}) %collective-permute-start.14) | collective-permute-done | bytes 262176 | tf_op jit(solution)/shard_map/ppermute | solution.py:498
  137.0 15.6 %shard_map.266 = (bf16[1024,1024]{1,0:T(8,128)(2,1)}, bf16[1024,1024]{1,0:T(8,128)(2,1)}, bf16[512,1024]{1,0:T(8,128)(2,1)}, bf16[512,1024]{1,0:T(8,128)(2,1)}, ...) custom-call(bf16[512,1024]{1,0:T(8,128)(2,1)} %add_convert_fusion.6.refs_0_, ...), custom_call_target="tpu_custom_call" | custom-call | flops 15032385536 | bytes 16777216 | tf_op jit(solution)/shard_map/pallas_call | solution.py:395
  152.6 8.7 %collective-permute-done.20.refs_0_ = bf16[512,1024]{1,0:T(8,128)(2,1)} collective-permute-done((bf16[512,1024]{1,0:T(8,128)(2,1)}, bf16[512,1024]{1,0:T(8,128)(2,1)}, u32[]{:S(2)}, u32[]{:S(2)}) %collective-permute-start.20) | collective-permute-done | bytes 1048608 | tf_op jit(solution)/shard_map/ppermute | solution.py:498
  161.3 2.9 collective-permute-done.21.refs_1_
  165.2 15.7 %shard_map.267 = (bf16[1024,1024]{1,0:T(8,128)(2,1)}, bf16[1024,1024]{1,0:T(8,128)(2,1)}, bf16[512,1024]{1,0:T(8,128)(2,1)}, bf16[512,1024]{1,0:T(8,128)(2,1)}, ...) custom-call(bf16[512,1024]{1,0:T(8,128)(2,1)} %collective-permute-done.20.refs_0_, ...), custom_call_target="tpu_custom_call" | custom-call | flops 15032385536 | bytes 16777216 | tf_op jit(solution)/shard_map/pallas_call | solution.py:395
  184.0 2.9 add_convert_fusion.5
  186.9 4.2 %fusion.46 = f32[1024,1024]{1,0:T(8,128)S(1)} fusion(bf16[1024,1024]{1,0:T(8,128)(2,1)} %get-tuple-element.129, bf16[1024,1024]{1,0:T(8,128)(2,1)S(1)} %copy-done.11), kind=kOutput, calls=%fused_computation.167 | convolution fusion | flops 2147483648 | bytes 8388608 | tf_op jit(solution)/shard_map/dot_general | solution.py:39
  191.9 3.7 fusion.18
  195.6 4.1 %add_convert_fusion.1 = bf16[1024,1024]{1,0:T(8,128)(2,1)S(1)} fusion(f32[1024,1024]{1,0:T(8,128)S(1)} %fusion.18, bf16[1024,1024]{1,0:T(8,128)(2,1)S(1)} %copy-done.44, bf16[512,1024]{1,0:T(8,128)(2,1)} %collective-permute-done.19.refs_1_, bf16[512,1024]{1,0:T(8,128)(2,1)} %add_convert_fusion.6.refs_0_), kind=kOutput, calls=%fused_computation.4 | convolution fusion | flops 2153775104 | bytes 10485760 | tf_op jit(solution)/shard_map/dot_general | solution.py:39
  204.6 12.1 %collective-permute-done.24 = bf16[512,1024]{1,0:T(8,128)(2,1)} collective-permute-done((bf16[512,1024]{1,0:T(8,128)(2,1)}, bf16[512,1024]{1,0:T(8,128)(2,1)}, u32[]{:S(2)}, u32[]{:S(2)}) %collective-permute-start.24) | collective-permute-done | bytes 1048608 | tf_op jit(solution)/shard_map/ppermute | solution.py:498
  231.1 6.8 %collective-permute-done.27 = bf16[1,512,256]{2,1,0:T(8,128)(2,1)} collective-permute-done((bf16[1,512,256]{2,1,0:T(8,128)(2,1)}, bf16[1,512,256]{2,1,0:T(8,128)(2,1)}, u32[]{:S(2)}, u32[]{:S(2)}) %collective-permute-start.27) | collective-permute-done | bytes 262176 | tf_op jit(solution)/shard_map/ppermute | solution.py:498
  247.6 39.1 %shard_map.268 = (bf16[1,2048,768]{2,1,0:T(8,128)(2,1)}, f32[1,8,768]{2,1,0:T(8,128)}) custom-call(bf16[1,2048,768]{2,1,0:T(8,128)(2,1)} %bitcast.253, bf16[1,2048,256]{2,1,0:T(8,128)(2,1)} %get-tuple-element.100.out_ref, bf16[1,2048,256]{2,1,0:T(8,128)(2,1)} %copy-done.25, f32[1,8,2048]{2,1,0:T(8,128)} %get-tuple-element.136.log_ref), custom_call_target="tpu_custom_call" | custom-call | flops 60129542144 | bytes 8388608 | tf_op jit(solution)/shard_map/pallas_call | solution.py:302
  287.4 8.1 %fusion.43 = (bf16[1024,768]{1,0:T(8,128)(2,1)}, f32[1024]{0:T(1024)S(1)}) fusion(bf16[8,128,768]{2,1,0:T(8,128)(2,1)S(1)} %copy-done.14, bf16[2048,1024]{1,0:T(8,128)(2,1)} %bitcast.251, bf16[1,2048,768]{2,1,0:T(8,128)(2,1)} %get-tuple-element.137), kind=kOutput, calls=%fused_computation.164 | convolution fusion | flops 3224370176 | bytes 10489856 | tf_op jit(solution)/shard_map/dot_general | solution.py:39
  303.0 3.8 convolution_convert_fusion
  312.2 10.3 %collective-permute-done.36 = bf16[144,1024]{1,0:T(8,128)(2,1)S(1)} collective-permute-done((bf16[144,1024]{1,0:T(8,128)(2,1)S(1)}, bf16[144,1024]{1,0:T(8,128)(2,1)S(1)}, u32[]{:S(2)}, u32[]{:S(2)}) %collective-permute-start.36) | collective-permute-done | bytes 294944 | tf_op jit(solution)/shard_map/ppermute | solution.py:442
  326.5 6.7 %collective-permute-done.38 = bf16[144,1024]{1,0:T(8,128)(2,1)S(1)} collective-permute-done((bf16[144,1024]{1,0:T(8,128)(2,1)S(1)}, bf16[144,1024]{1,0:T(8,128)(2,1)S(1)}, u32[]{:S(2)}, u32[]{:S(2)}) %collective-permute-start.38) | collective-permute-done | bytes 294944 | tf_op jit(solution)/shard_map/ppermute | solution.py:442
  337.3 4.4 %collective-permute-done.40 = bf16[144,1024]{1,0:T(8,128)(2,1)} collective-permute-done((bf16[144,1024]{1,0:T(8,128)(2,1)S(1)}, bf16[144,1024]{1,0:T(8,128)(2,1)}, u32[]{:S(2)}, u32[]{:S(2)}) %collective-permute-start.40) | collective-permute-done | bytes 294944 | tf_op jit(solution)/shard_map/ppermute | solution.py:442
  344.7 3.4 fusion.24
  354.1 4.6 %collective-permute-done.41 = bf16[144,1024]{1,0:T(8,128)(2,1)S(1)} collective-permute-done((bf16[144,1024]{1,0:T(8,128)(2,1)S(1)}, bf16[144,1024]{1,0:T(8,128)(2,1)S(1)}, u32[]{:S(2)}, u32[]{:S(2)}) %collective-permute-start.41) | collective-permute-done | bytes 294944 | tf_op jit(solution)/shard_map/ppermute | solution.py:442
  362.2 11.2 %collective-permute-done.39.refs_2_ = bf16[128,2048]{1,0:T(8,128)(2,1)S(1)} collective-permute-done((bf16[128,2048]{1,0:T(8,128)(2,1)S(1)}, bf16[128,2048]{1,0:T(8,128)(2,1)S(1)}, u32[]{:S(2)}, u32[]{:S(2)}) %collective-permute-start.39) | collective-permute-done | bytes 524320 | tf_op jit(solution)/shard_map/ppermute | solution.py:498
  379.9 3.1 shard_map.270
  (295 shorter events, 127.7 us)
Async XLA Ops:
  7.2 129.8 %all-gather.3.cloned.1.call-start = ((), (), s32[]{:S(2)}) async-start(), calls=%async_computation.2 | async-start | bytes 4718592 | tf_op jit(solution)/shard_map/all_gather | solution.py:695
  7.2 26.5 %collective-permute-start.3 = (bf16[1,512,1024]{2,1,0:T(8,128)(2,1)}, bf16[1,512,1024]{2,1,0:T(8,128)(2,1)}, u32[]{:S(2)}, u32[]{:S(2)}) collective-permute-start(bf16[1,512,1024]{2,1,0:T(8,128)(2,1)} %refs_0_), channel_id=1, source_target_pairs={{0,2},{1,3},{2,0},{3,1},{4,6},{5,7},{6,4},{7,5},{8,10},{9,11},{10,... | collective-permute-start | bytes 3145736 | tf_op jit(solution)/shard_map/ppermute | solution.py:498
  14.5 20.0 %collective-permute-start.5 = (bf16[144,1024]{1,0:T(8,128)(2,1)S(1)}, bf16[144,1024]{1,0:T(8,128)(2,1)}, u32[]{:S(2)}, u32[]{:S(2)}) collective-permute-start(bf16[144,1024]{1,0:T(8,128)(2,1)S(1)} %pad_maximum_fusion.3), channel_id=1, source_target_pairs={{0,4},{8,0},{16,8},{24,16},{28,24},{20,28},{12,20},{4,12},{1,5},{9... | collective-permute-start | bytes 884744 | tf_op jit(solution)/shard_map/ppermute | solution.py:442
  15.0 30.9 %collective-permute-start.2 = (bf16[1,512,1024]{2,1,0:T(8,128)(2,1)}, bf16[1,512,1024]{2,1,0:T(8,128)(2,1)}, u32[]{:S(2)}, u32[]{:S(2)}) collective-permute-start(bf16[1,512,1024]{2,1,0:T(8,128)(2,1)} %refs_0_), channel_id=1, source_target_pairs={{0,1},{1,0},{2,3},{3,2},{4,5},{5,4},{6,7},{7,6},{8,9},{9,8},{10,11... | collective-permute-start | bytes 3145736 | tf_op jit(solution)/shard_map/ppermute | solution.py:498
  21.4 24.5 %collective-permute-start.1 = (bf16[144,1024]{1,0:T(8,128)(2,1)S(1)}, bf16[144,1024]{1,0:T(8,128)(2,1)}, u32[]{:S(2)}, u32[]{:S(2)}) collective-permute-start(bf16[144,1024]{1,0:T(8,128)(2,1)S(1)} %collective-permute-done), channel_id=1, source_target_pairs={{0,8},{8,16},{16,24},{24,28},{28,20},{20,12},{12,4},{4,0},{1,9},{9... | collective-permute-start | bytes 884744 | tf_op jit(solution)/shard_map/ppermute | solution.py:442
  33.7 12.2 %collective-permute-start.4 = (bf16[1,512,1024]{2,1,0:T(8,128)(2,1)}, bf16[1,512,1024]{2,1,0:T(8,128)(2,1)}, u32[]{:S(2)}, u32[]{:S(2)}) collective-permute-start(bf16[1,512,1024]{2,1,0:T(8,128)(2,1)} %collective-permute-done.3.refs_2_), channel_id=1, source_target_pairs={{0,1},{1,0},{2,3},{3,2},{4,5},{5,4},{6,7},{7,6},{8,9},{9,8},{10,11... | collective-permute-start | bytes 3145736 | tf_op jit(solution)/shard_map/ppermute | solution.py:498
  44.2 10.8 %collective-permute-start.8 = (bf16[144,1024]{1,0:T(8,128)(2,1)S(1)}, bf16[144,1024]{1,0:T(8,128)(2,1)}, u32[]{:S(2)}, u32[]{:S(2)}) collective-permute-start(bf16[144,1024]{1,0:T(8,128)(2,1)S(1)} %collective-permute-done.6), channel_id=1, source_target_pairs={{0,4},{8,0},{16,8},{24,16},{28,24},{20,28},{12,20},{4,12},{1,5},{9... | collective-permute-start | bytes 884744 | tf_op jit(solution)/shard_map/ppermute | solution.py:442
  55.0 278.2 %reduce-scatter.2.cloned.1.call-start = ((), (), s32[]{:S(2)}) async-start(), calls=%async_computation.1 | async-start | bytes 4718592 | tf_op jit(solution)/shard_map/reduce_scatter | solution.py:777
  66.9 12.9 %collective-permute-start.10 = (bf16[1024,256]{1,0:T(8,128)(2,1)}, bf16[1024,256]{1,0:T(8,128)(2,1)}, u32[]{:S(2)}, u32[]{:S(2)}) collective-permute-start(bf16[1024,256]{1,0:T(8,128)(2,1)} %bitcast.31.refs_0_), channel_id=1, source_target_pairs={{0,2},{1,3},{2,0},{3,1},{4,6},{5,7},{6,4},{7,5},{8,10},{9,11},{10,... | collective-permute-start | bytes 1572872 | tf_op jit(solution)/shard_map/ppermute | solution.py:498
  79.8 22.5 %collective-permute-start.11 = (bf16[512,1024]{1,0:T(8,128)(2,1)S(1)}, bf16[512,1024]{1,0:T(8,128)(2,1)S(1)}, u32[]{:S(2)}, u32[]{:S(2)}) collective-permute-start(bf16[512,1024]{1,0:T(8,128)(2,1)S(1)} %bitcast.202), channel_id=1, source_target_pairs={{0,2},{1,3},{2,0},{3,1},{4,6},{5,7},{6,4},{7,5},{8,10},{9,11},{10,... | collective-permute-start | bytes 3145736 | tf_op jit(solution)/shard_map/ppermute | solution.py:498
  102.4 11.9 %collective-permute-start.18 = (bf16[512,1024]{1,0:T(8,128)(2,1)S(1)}, bf16[512,1024]{1,0:T(8,128)(2,1)}, u32[]{:S(2)}, u32[]{:S(2)}) collective-permute-start(bf16[512,1024]{1,0:T(8,128)(2,1)S(1)} %collective-permute-done.11), channel_id=1, source_target_pairs={{0,1},{1,0},{2,3},{3,2},{4,5},{5,4},{6,7},{7,6},{8,9},{9,8},{10,11... | collective-permute-start | bytes 3145736 | tf_op jit(solution)/shard_map/ppermute | solution.py:498
  102.4 14.6 %collective-permute-start.17 = (bf16[512,1024]{1,0:T(8,128)(2,1)S(1)}, bf16[512,1024]{1,0:T(8,128)(2,1)S(1)}, u32[]{:S(2)}, u32[]{:S(2)}) collective-permute-start(bf16[512,1024]{1,0:T(8,128)(2,1)S(1)} %bitcast.203), channel_id=1, source_target_pairs={{0,1},{1,0},{2,3},{3,2},{4,5},{5,4},{6,7},{7,6},{8,9},{9,8},{10,11... | collective-permute-start | bytes 3145736 | tf_op jit(solution)/shard_map/ppermute | solution.py:498
  113.2 12.9 %collective-permute-start.14 = (bf16[1,512,256]{2,1,0:T(8,128)(2,1)S(1)}, bf16[1,512,256]{2,1,0:T(8,128)(2,1)S(1)}, u32[]{:S(2)}, u32[]{:S(2)}) collective-permute-start(bf16[1,512,256]{2,1,0:T(8,128)(2,1)S(1)} %get-tuple-element.184), channel_id=1, source_target_pairs={{0,3},{1,2},{2,1},{3,0},{4,7},{5,6},{6,5},{7,4},{8,11},{9,10},{10,... | collective-permute-start | bytes 786440 | tf_op jit(solution)/shard_map/ppermute | solution.py:498
  135.9 25.4 %collective-permute-start.20 = (bf16[512,1024]{1,0:T(8,128)(2,1)}, bf16[512,1024]{1,0:T(8,128)(2,1)}, u32[]{:S(2)}, u32[]{:S(2)}) collective-permute-start(bf16[512,1024]{1,0:T(8,128)(2,1)} %add_convert_fusion.6.refs_0_), channel_id=1, source_target_pairs={{0,2},{1,3},{2,0},{3,1},{4,6},{5,7},{6,4},{7,5},{8,10},{9,11},{10,... | collective-permute-start | bytes 3145736 | tf_op jit(solution)/shard_map/ppermute | solution.py:498
  181.3 23.2 %collective-permute-start.22 = (bf16[512,1024]{1,0:T(8,128)(2,1)}, bf16[512,1024]{1,0:T(8,128)(2,1)}, u32[]{:S(2)}, u32[]{:S(2)}) collective-permute-start(bf16[512,1024]{1,0:T(8,128)(2,1)} %get-tuple-element.120), channel_id=1, source_target_pairs={{0,1},{1,0},{2,3},{3,2},{4,5},{5,4},{6,7},{7,6},{8,9},{9,8},{10,11... | collective-permute-start | bytes 3145736 | tf_op jit(solution)/shard_map/ppermute | solution.py:498
  191.1 25.6 %collective-permute-start.24 = (bf16[512,1024]{1,0:T(8,128)(2,1)}, bf16[512,1024]{1,0:T(8,128)(2,1)}, u32[]{:S(2)}, u32[]{:S(2)}) collective-permute-start(bf16[512,1024]{1,0:T(8,128)(2,1)} %add_convert_fusion.5), channel_id=1, source_target_pairs={{0,2},{1,3},{2,0},{3,1},{4,6},{5,7},{6,4},{7,5},{8,10},{9,11},{10,... | collective-permute-start | bytes 3145736 | tf_op jit(solution)/shard_map/ppermute | solution.py:498
  225.3 19.0 %collective-permute-start.29 = (bf16[512,1024]{1,0:T(8,128)(2,1)}, bf16[512,1024]{1,0:T(8,128)(2,1)}, u32[]{:S(2)}, u32[]{:S(2)}) collective-permute-start(bf16[512,1024]{1,0:T(8,128)(2,1)} %get-tuple-element.134), channel_id=1, source_target_pairs={{0,1},{1,0},{2,3},{3,2},{4,5},{5,4},{6,7},{7,6},{8,9},{9,8},{10,11... | collective-permute-start | bytes 3145736 | tf_op jit(solution)/shard_map/ppermute | solution.py:498
  227.9 13.7 %collective-permute-start.30 = (bf16[1024,256]{1,0:T(8,128)(2,1)}, bf16[1024,256]{1,0:T(8,128)(2,1)}, u32[]{:S(2)}, u32[]{:S(2)}) collective-permute-start(bf16[1024,256]{1,0:T(8,128)(2,1)} %get-tuple-element.180), channel_id=1, source_target_pairs={{0,1},{1,0},{2,3},{3,2},{4,5},{5,4},{6,7},{7,6},{8,9},{9,8},{10,11... | collective-permute-start | bytes 1572872 | tf_op jit(solution)/shard_map/ppermute | solution.py:498
  227.9 13.7 %collective-permute-start.31 = (bf16[1024,256]{1,0:T(8,128)(2,1)}, bf16[1024,256]{1,0:T(8,128)(2,1)}, u32[]{:S(2)}, u32[]{:S(2)}) collective-permute-start(bf16[1024,256]{1,0:T(8,128)(2,1)} %get-tuple-element.179), channel_id=1, source_target_pairs={{0,1},{1,0},{2,3},{3,2},{4,5},{5,4},{6,7},{7,6},{8,9},{9,8},{10,11... | collective-permute-start | bytes 1572872 | tf_op jit(solution)/shard_map/ppermute | solution.py:498
  229.2 12.4 %collective-permute-start.28 = (bf16[1,512,256]{2,1,0:T(8,128)(2,1)S(1)}, bf16[1,512,256]{2,1,0:T(8,128)(2,1)S(1)}, u32[]{:S(2)}, u32[]{:S(2)}) collective-permute-start(bf16[1,512,256]{2,1,0:T(8,128)(2,1)S(1)} %get-tuple-element.181), channel_id=1, source_target_pairs={{0,3},{1,2},{2,1},{3,0},{4,7},{5,6},{6,5},{7,4},{8,11},{9,10},{10,... | collective-permute-start | bytes 786440 | tf_op jit(solution)/shard_map/ppermute | solution.py:498
  246.9 51.2 %collective-permute-start.33 = (bf16[1024,256]{1,0:T(8,128)(2,1)}, bf16[1024,256]{1,0:T(8,128)(2,1)}, u32[]{:S(2)}, u32[]{:S(2)}) collective-permute-start(bf16[1024,256]{1,0:T(8,128)(2,1)} %get-tuple-element.142), channel_id=1, source_target_pairs={{0,2},{1,3},{2,0},{3,1},{4,6},{5,7},{6,4},{7,5},{8,10},{9,11},{10,... | collective-permute-start | bytes 1572872 | tf_op jit(solution)/shard_map/ppermute | solution.py:498
  308.5 14.2 %collective-permute-start.34 = (bf16[512,1024]{1,0:T(8,128)(2,1)S(1)}, bf16[512,1024]{1,0:T(8,128)(2,1)S(1)}, u32[]{:S(2)}, u32[]{:S(2)}) collective-permute-start(bf16[512,1024]{1,0:T(8,128)(2,1)S(1)} %get-tuple-element.168), channel_id=1, source_target_pairs={{0,1},{1,0},{2,3},{3,2},{4,5},{5,4},{6,7},{7,6},{8,9},{9,8},{10,11... | collective-permute-start | bytes 3145736 | tf_op jit(solution)/shard_map/ppermute | solution.py:498
  309.3 13.3 %collective-permute-start.36 = (bf16[144,1024]{1,0:T(8,128)(2,1)S(1)}, bf16[144,1024]{1,0:T(8,128)(2,1)S(1)}, u32[]{:S(2)}, u32[]{:S(2)}) collective-permute-start(bf16[144,1024]{1,0:T(8,128)(2,1)S(1)} %get-tuple-element.149), channel_id=1, source_target_pairs={{0,4},{8,0},{16,8},{24,16},{28,24},{20,28},{12,20},{4,12},{1,5},{9... | collective-permute-start | bytes 884744 | tf_op jit(solution)/shard_map/ppermute | solution.py:442
  310.8 25.1 %collective-permute-start.32 = (bf16[512,1024]{1,0:T(8,128)(2,1)}, bf16[512,1024]{1,0:T(8,128)(2,1)}, u32[]{:S(2)}, u32[]{:S(2)}) collective-permute-start(bf16[512,1024]{1,0:T(8,128)(2,1)} %add_convert_fusion.4), channel_id=1, source_target_pairs={{0,2},{1,3},{2,0},{3,1},{4,6},{5,7},{6,4},{7,5},{8,10},{9,11},{10,... | collective-permute-start | bytes 3145736 | tf_op jit(solution)/shard_map/ppermute | solution.py:498
  324.3 20.4 %collective-permute-start.25 = (bf16[512,1024]{1,0:T(8,128)(2,1)}, bf16[512,1024]{1,0:T(8,128)(2,1)}, u32[]{:S(2)}, u32[]{:S(2)}) collective-permute-start(bf16[512,1024]{1,0:T(8,128)(2,1)} %get-tuple-element.132), channel_id=1, source_target_pairs={{0,1},{1,0},{2,3},{3,2},{4,5},{5,4},{6,7},{7,6},{8,9},{9,8},{10,11... | collective-permute-start | bytes 3145736 | tf_op jit(solution)/shard_map/ppermute | solution.py:498
  324.5 12.9 %collective-permute-start.42 = (bf16[144,1024]{1,0:T(8,128)(2,1)}, bf16[144,1024]{1,0:T(8,128)(2,1)}, u32[]{:S(2)}, u32[]{:S(2)}) collective-permute-start(bf16[144,1024]{1,0:T(8,128)(2,1)} %get-tuple-element.175), channel_id=1, source_target_pairs={{0,8},{8,16},{16,24},{24,28},{28,20},{20,12},{12,4},{4,0},{1,9},{9... | collective-permute-start | bytes 884744 | tf_op jit(solution)/shard_map/ppermute | solution.py:442
  335.9 26.3 %collective-permute-start.37 = (bf16[512,1024]{1,0:T(8,128)(2,1)}, bf16[512,1024]{1,0:T(8,128)(2,1)S(1)}, u32[]{:S(2)}, u32[]{:S(2)}) collective-permute-start(bf16[512,1024]{1,0:T(8,128)(2,1)} %add_convert_fusion.2), channel_id=1, source_target_pairs={{0,2},{1,3},{2,0},{3,1},{4,6},{5,7},{6,4},{7,5},{8,10},{9,11},{10,... | collective-permute-start | bytes 3145736 | tf_op jit(solution)/shard_map/ppermute | solution.py:498
  337.3 15.2 %collective-permute-start.48 = (bf16[128,2048]{1,0:T(8,128)(2,1)}, bf16[128,2048]{1,0:T(8,128)(2,1)S(1)}, u32[]{:S(2)}, u32[]{:S(2)}) collective-permute-start(bf16[128,2048]{1,0:T(8,128)(2,1)} %bitcast.211), channel_id=1, source_target_pairs={{0,1},{1,0},{2,3},{3,2},{4,5},{5,4},{6,7},{7,6},{8,9},{9,8},{10,11... | collective-permute-start | bytes 1572872 | tf_op jit(solution)/shard_map/ppermute | solution.py:498
  348.1 25.4 %collective-permute-start.35 = (bf16[512,1024]{1,0:T(8,128)(2,1)S(1)}, bf16[512,1024]{1,0:T(8,128)(2,1)S(1)}, u32[]{:S(2)}, u32[]{:S(2)}) collective-permute-start(bf16[512,1024]{1,0:T(8,128)(2,1)S(1)} %copy-done.27), channel_id=1, source_target_pairs={{0,1},{1,0},{2,3},{3,2},{4,5},{5,4},{6,7},{7,6},{8,9},{9,8},{10,11... | collective-permute-start | bytes 3145736 | tf_op jit(solution)/shard_map/ppermute | solution.py:498
  348.1 25.4 %collective-permute-start.39 = (bf16[128,2048]{1,0:T(8,128)(2,1)S(1)}, bf16[128,2048]{1,0:T(8,128)(2,1)S(1)}, u32[]{:S(2)}, u32[]{:S(2)}) collective-permute-start(bf16[128,2048]{1,0:T(8,128)(2,1)S(1)} %bitcast.213), channel_id=1, source_target_pairs={{0,2},{1,3},{2,0},{3,1},{4,6},{5,7},{6,4},{7,5},{8,10},{9,11},{10,... | collective-permute-start | bytes 1572872 | tf_op jit(solution)/shard_map/ppermute | solution.py:498
  361.4 16.3 %collective-permute-start.45 = (bf16[144,1024]{1,0:T(8,128)(2,1)S(1)}, bf16[144,1024]{1,0:T(8,128)(2,1)S(1)}, u32[]{:S(2)}, u32[]{:S(2)}) collective-permute-start(bf16[144,1024]{1,0:T(8,128)(2,1)S(1)} %fusion.29.refs_0_), channel_id=1, source_target_pairs={{0,1},{1,0},{2,3},{3,2},{4,5},{5,4},{6,7},{7,6},{8,9},{9,8},{10,11... | collective-permute-start | bytes 884744 | tf_op jit(solution)/shard_map/ppermute | solution.py:498
  361.5 16.4 %collective-permute-start.46 = (bf16[144,1024]{1,0:T(8,128)(2,1)S(1)}, bf16[144,1024]{1,0:T(8,128)(2,1)S(1)}, u32[]{:S(2)}, u32[]{:S(2)}) collective-permute-start(bf16[144,1024]{1,0:T(8,128)(2,1)S(1)} %fusion.29.refs_0_), channel_id=1, source_target_pairs={{0,2},{1,3},{2,0},{3,1},{4,6},{5,7},{6,4},{7,5},{8,10},{9,11},{10,... | collective-permute-start | bytes 884744 | tf_op jit(solution)/shard_map/ppermute | solution.py:498
  (65 other events, 477.4 us)
Sparse Core Ops, SparseCore 0:
  55.1 74.7 all-gather.2
  229.3 90.4 reduce-scatter.1

commit v4 on v3

--- a/solution.py
+++ b/solution.py
@@ -671,7 +671,7 @@
         axis=0,
     )
 
-    token_blocks = gather_offsets(tokens)
+    token_far = swap(tokens, top_bit)
     steps = shards // 2
     middle_step = max(2, steps // 2)
     made = {}
@@ -686,12 +686,12 @@
         packed,
         {
             1: [("feed", lambda: (w_fc, w_proj))],
-            middle_step: [("tokens", lambda: token_blocks)],
+            middle_step: [("tokens", lambda: token_far)],
             steps - 1: [("share", feed_share)],
         },
         made,
     )
-    token_blocks = made["tokens"]
+    token_blocks = gather_offsets(tokens, low_bits) + gather_offsets(made["tokens"], low_bits)
     second_gather = lax.all_gather(made["share"], "dp", axis=0)
     if units == part and hidden_width == model:
         feed_weights = second_gather.reshape(model, 2 * model)
@@ -729,11 +729,13 @@
     )
     cot_far = swap(cot_sent, top_bit)
     attended, logs = attend(mixed, width)
-    attended, cot_far, cot_near = lax.optimization_barrier((attended, cot_far, cot_own))
+    sent = picked(attended, 1)
+    _, cot_far, cot_near, attn_columns, attn_far = lax.optimization_barrier(
+        (sent, cot_far, cot_own, attn_columns, attn_far)
+    )
     near_cot = jnp.concatenate(gather_offsets(cot_near, low_bits), axis=0)
     far_cot = jnp.concatenate(gather_offsets(cot_far, low_bits), axis=0)
 
-    sent = picked(attended, 1)
     arrived = [sent[0]] + [swap(sent[offset], offset) for offset in range(1, ranks)]
     attn_blocks = gather_offsets(attn_columns, low_bits) + gather_offsets(attn_far, low_bits)
     (full_attn,) = columns(attn_blocks, ((0, 1, width),), BF16)
@@ -793,8 +795,8 @@
     grad_attn_part = picked(dot_tn(joined, grad_branch).astype(BF16), 1)
     attn_near = reduce_offsets(grad_attn_part[:half], low_bits)
     attn_far = reduce_offsets(grad_attn_part[half:], low_bits).astype(BF16)
-    grad_attended, ahead_far, attn_far, attn_near = lax.optimization_barrier(
-        (grad_attended, ahead_far, attn_far, attn_near)
+    grad_attended, ahead_far, attn_far = lax.optimization_barrier(
+        (grad_attended, ahead_far, attn_far)
     )
     ahead_far = swap(ahead_far, top_bit)
     attn_far = swap(attn_far, top_bit)
@@ -804,6 +806,10 @@
 
     grad_mixed, column_sums = attend_back(mixed, attended, grad_attended, logs, width)
     grad_mixed = grad_mixed.reshape(seqs * length, 3 * width)
+    back = dot_nt(grad_mixed, full_qkv).astype(BF16).reshape(seqs, length, model)
+    back_blocks = [item.reshape(seqs * rows, model) for item in picked(back, 1)]
+    back_blocks, grad_mixed = lax.optimization_barrier((back_blocks, grad_mixed))
+    far_back = reduce_offsets(back_blocks[half:], low_bits).astype(BF16)
     grad_w_qkv = dot_tn(normed, grad_mixed)
     column_sums = jnp.sum(column_sums[:, 0], axis=0)
     qkv_values = full_qkv.astype(F32)
@@ -844,30 +850,19 @@
         ],
         axis=1,
     )
+    last_parts, far_back, near_back = lax.optimization_barrier(
+        (last_parts, far_back, back_blocks[:half])
+    )
+    far_arrived = swap(far_back, top_bit)
+    near_back = reduce_offsets(near_back, low_bits)
     made = {}
-
-    def far_sum():
-        back = dot_nt(made["mixed"], full_qkv).astype(BF16).reshape(seqs, length, model)
-        blocks = [item.reshape(seqs * rows, model) for item in picked(back, 1)]
-        far = reduce_offsets(blocks[half:], low_bits).astype(BF16)
-        near, far = lax.optimization_barrier((blocks[:half], far))
-        made["near"] = reduce_offsets(near, low_bits)
-        return far
-
     last_scatter = ring_scatter(
-        last_parts,
-        {
-            steps: [("mixed", lambda: grad_mixed)],
-            max(steps - 1, 1): [("far", far_sum)],
-            max(steps - 2, 1): [("scatter", lambda: first_scatter)],
-        },
-        made,
-    )
-    far_arrived = swap(made["far"], top_bit)
+        last_parts, {max(steps - 2, 1): [("scatter", lambda: first_scatter)]}, made
+    )
     fed_far = swap(made["scatter"], top_bit)
     last_scatter = last_scatter.astype(BF16)
     far_arrived, fed_far, _ = lax.optimization_barrier((far_arrived, fed_far, last_scatter))
-    grad_normed = made["near"].astype(F32) + far_arrived.astype(F32)
+    grad_normed = near_back.astype(F32) + far_arrived.astype(F32)
     fed = gather_offsets(made["scatter"], low_bits) + gather_offsets(fed_far, low_bits)
     rest = gather_offsets(last_scatter)
 

time: 398 us -> 384 us (0.965)
  waiting for transfers between devices: 125 us -> 112 us
    ppermute x14, waiting for transfers between devices: 50.6 us -> 39.6 us  [ring_move(): return lax.ppermute(array, 'dp', pairs)]
    convert_element_type x1 -> x2, other arithmetic: 1.42 us -> 5.41 us  [the longest x1 2.89 us: per_device(): far_back = reduce_offsets(back_blocks[half:], low_bits).astype(BF16)]
    unnamed x99 -> x105, local copies, waits for them, and re-layouts: 11.6 us -> 10.9 us
where the time goes in v4:
time: 384 us; the launch traced here: 379 us
  waiting for transfers between devices  112 us (29%)
  Pallas kernels  111 us (29%)
  other arithmetic  38.5 us (10%)
  local copies, waits for them, and re-layouts  36.9 us (10%)
  starting transfers between devices  35 us (9%)
  matrix products  30.1 us (8%)
  between operations  15.4 us (4%)
    ppermute x36, waiting for transfers between devices, swap(): lax.ppermute(array, 'seq', [(rank, rank ^ offset) for rank in range(ranks)])  71.9 us
    ppermute x14, waiting for transfers between devices, ring_move(): return lax.ppermute(array, 'dp', pairs)  39.6 us
    pallas_call x1, Pallas kernels, attend_back(): pl.pallas_call(functools.partial(attend_back_kernel, block=block, width=w...  39.1 us
    pallas_call x2, Pallas kernels, feed(): pl.pallas_call(functools.partial(feed_kernel, parts=parts, steps=steps),...  31.3 us
    dot_general x6, matrix products, dot_tn(): lax.dot_general(left_side, right_side, (((0,), (0,)), ((), ())), preferre...  20.4 us
    ppermute x36, starting transfers between devices, swap(): lax.ppermute(array, 'seq', [(rank, rank ^ offset) for rank in range(ranks)])  19.2 us
    pallas_call x1, Pallas kernels, attend(): pl.pallas_call(functools.partial(attend_kernel, block=block, width=width)...  17.8 us
    ppermute x14, starting transfers between devices, ring_move(): return lax.ppermute(array, 'dp', pairs)  15.8 us
  transfers between devices with their start and end apart: 52, of which 25 were waited for; matrix products, arithmetic and copies ran while one was open for 23% of the time, Pallas kernels for 24%

profile of v4, /device:TPU:0, one launch (start us, length us, event | category | flops | bytes accessed | tf_op | source)
XLA Modules:
  0.0 379.2 jit_solution(10930694091839243745)
XLA Ops:
  9.9 3.1 collective-permute-start.1
  15.3 4.6 %collective-permute-done.1 = bf16[144,1024]{1,0:T(8,128)(2,1)S(1)} collective-permute-done((bf16[144,1024]{1,0:T(8,128)(2,1)S(1)}, bf16[144,1024]{1,0:T(8,128)(2,1)S(1)}, u32[]{:S(2)}, u32[]{:S(2)}) %collective-permute-start.1) | collective-permute-done | bytes 294944 | tf_op jit(solution)/shard_map/ppermute | solution.py:442
  33.3 4.6 %collective-permute-done.3.refs_2_ = bf16[1,512,1024]{2,1,0:T(8,128)(2,1)} collective-permute-done((bf16[1,512,1024]{2,1,0:T(8,128)(2,1)}, bf16[1,512,1024]{2,1,0:T(8,128)(2,1)}, u32[]{:S(2)}, u32[]{:S(2)}) %collective-permute-start.3) | collective-permute-done | bytes 1048608 | tf_op jit(solution)/shard_map/ppermute | solution.py:498
  40.8 4.9 %collective-permute-done.7 = bf16[144,1024]{1,0:T(8,128)(2,1)S(1)} collective-permute-done((bf16[144,1024]{1,0:T(8,128)(2,1)}, bf16[144,1024]{1,0:T(8,128)(2,1)S(1)}, u32[]{:S(2)}, u32[]{:S(2)}) %collective-permute-start.7) | collective-permute-done | bytes 294944 | tf_op jit(solution)/shard_map/ppermute | solution.py:442
  48.2 4.3 %collective-permute-done.9 = bf16[144,1024]{1,0:T(8,128)(2,1)} collective-permute-done((bf16[144,1024]{1,0:T(8,128)(2,1)S(1)}, bf16[144,1024]{1,0:T(8,128)(2,1)}, u32[]{:S(2)}, u32[]{:S(2)}) %collective-permute-start.9) | collective-permute-done | bytes 294944 | tf_op jit(solution)/shard_map/ppermute | solution.py:442
  58.2 11.3 %shard_map.262 = (bf16[1,4,512,1024]{3,2,1,0:T(8,128)(2,1)}, bf16[1,4,512,768]{3,2,1,0:T(8,128)(2,1)}) custom-call(s32[1]{0:T(128)} %bitcast.2.rank_ref, bf16[1,512,1024]{2,1,0:T(8,128)(2,1)} %refs_0_.1, bf16[1,512,1024]{2,1,0:T(8,128)(2,1)} %collective-permute-done.refs_1_, bf16[1,512,1024]{2,1,0:T(8,128)(2,1)} %collective-permute-done.3.refs_2_, ...), custom_call_target="tpu_custom_call" | custom-call | flops 6442450944 | bytes 13107200 | tf_op jit(solution)/shard_map/pallas_call | solution.py:83
  70.3 17.8 %shard_map.263 = (bf16[1,2048,256]{2,1,0:T(8,128)(2,1)}, f32[1,8,2048]{2,1,0:T(8,128)}) custom-call(bf16[1,2048,768]{2,1,0:T(8,128)(2,1)} %bitcast.253), custom_call_target="tpu_custom_call" | custom-call | flops 30064771072 | bytes 4194304 | tf_op jit(solution)/shard_map/pallas_call | solution.py:177
  92.1 3.8 %collective-permute-done.15.refs_1_ = bf16[1024,256]{1,0:T(8,128)(2,1)S(1)} collective-permute-done((bf16[1024,256]{1,0:T(8,128)(2,1)S(1)}, bf16[1024,256]{1,0:T(8,128)(2,1)S(1)}, u32[]{:S(2)}, u32[]{:S(2)}) %collective-permute-start.15) | collective-permute-done | bytes 524320 | tf_op jit(solution)/shard_map/ppermute | solution.py:498
  97.6 3.1 shard_map.264
  105.0 4.0 %collective-permute-done.13 = bf16[1,512,256]{2,1,0:T(8,128)(2,1)S(1)} collective-permute-done((bf16[1,512,256]{2,1,0:T(8,128)(2,1)S(1)}, bf16[1,512,256]{2,1,0:T(8,128)(2,1)S(1)}, u32[]{:S(2)}, u32[]{:S(2)}) %collective-permute-start.13) | collective-permute-done | bytes 262176 | tf_op jit(solution)/shard_map/ppermute | solution.py:498
  120.9 15.6 %shard_map.266 = (bf16[1024,1024]{1,0:T(8,128)(2,1)}, bf16[1024,1024]{1,0:T(8,128)(2,1)}, bf16[512,1024]{1,0:T(8,128)(2,1)}, bf16[512,1024]{1,0:T(8,128)(2,1)}, ...) custom-call(bf16[512,1024]{1,0:T(8,128)(2,1)} %add_convert_fusion.6.refs_0_, ...), custom_call_target="tpu_custom_call" | custom-call | flops 15032385536 | bytes 16777216 | tf_op jit(solution)/shard_map/pallas_call | solution.py:395
  136.5 7.9 %collective-permute-done.20.refs_0_ = bf16[512,1024]{1,0:T(8,128)(2,1)} collective-permute-done((bf16[512,1024]{1,0:T(8,128)(2,1)}, bf16[512,1024]{1,0:T(8,128)(2,1)}, u32[]{:S(2)}, u32[]{:S(2)}) %collective-permute-start.20) | collective-permute-done | bytes 1048608 | tf_op jit(solution)/shard_map/ppermute | solution.py:498
  148.3 15.7 %shard_map.267 = (bf16[1024,1024]{1,0:T(8,128)(2,1)}, bf16[1024,1024]{1,0:T(8,128)(2,1)}, bf16[512,1024]{1,0:T(8,128)(2,1)}, bf16[512,1024]{1,0:T(8,128)(2,1)}, ...) custom-call(bf16[512,1024]{1,0:T(8,128)(2,1)} %collective-permute-done.20.refs_0_, ...), custom_call_target="tpu_custom_call" | custom-call | flops 15032385536 | bytes 16777216 | tf_op jit(solution)/shard_map/pallas_call | solution.py:395
  167.1 2.9 add_convert_fusion.5
  170.0 4.2 %fusion.45 = f32[1024,1024]{1,0:T(8,128)S(1)} fusion(bf16[1024,1024]{1,0:T(8,128)(2,1)} %get-tuple-element.126, bf16[1024,1024]{1,0:T(8,128)(2,1)S(1)} %copy-done.14), kind=kOutput, calls=%fused_computation.166 | convolution fusion | flops 2147483648 | bytes 8388608 | tf_op jit(solution)/shard_map/dot_general | solution.py:39
  175.2 3.7 fusion.18
  178.9 4.1 %add_convert_fusion.1 = bf16[1024,1024]{1,0:T(8,128)(2,1)S(1)} fusion(f32[1024,1024]{1,0:T(8,128)S(1)} %fusion.18, bf16[1024,1024]{1,0:T(8,128)(2,1)S(1)} %copy-done.47, bf16[512,1024]{1,0:T(8,128)(2,1)} %collective-permute-done.19.refs_1_, bf16[512,1024]{1,0:T(8,128)(2,1)} %add_convert_fusion.6.refs_0_), kind=kOutput, calls=%fused_computation.4 | convolution fusion | flops 2153775104 | bytes 10485760 | tf_op jit(solution)/shard_map/dot_general | solution.py:39
  187.8 12.0 %collective-permute-done.24 = bf16[512,1024]{1,0:T(8,128)(2,1)} collective-permute-done((bf16[512,1024]{1,0:T(8,128)(2,1)}, bf16[512,1024]{1,0:T(8,128)(2,1)}, u32[]{:S(2)}, u32[]{:S(2)}) %collective-permute-start.24) | collective-permute-done | bytes 1048608 | tf_op jit(solution)/shard_map/ppermute | solution.py:498
  215.6 4.9 %collective-permute-done.27 = bf16[1,512,256]{2,1,0:T(8,128)(2,1)} collective-permute-done((bf16[1,512,256]{2,1,0:T(8,128)(2,1)}, bf16[1,512,256]{2,1,0:T(8,128)(2,1)}, u32[]{:S(2)}, u32[]{:S(2)}) %collective-permute-start.27) | collective-permute-done | bytes 262176 | tf_op jit(solution)/shard_map/ppermute | solution.py:498
  221.6 3.8 collective-permute-done.28
  229.3 39.1 %shard_map.268 = (bf16[1,2048,768]{2,1,0:T(8,128)(2,1)}, f32[1,8,768]{2,1,0:T(8,128)}) custom-call(bf16[1,2048,768]{2,1,0:T(8,128)(2,1)} %bitcast.254, bf16[1,2048,256]{2,1,0:T(8,128)(2,1)} %get-tuple-element.94.out_ref, bf16[1,2048,256]{2,1,0:T(8,128)(2,1)} %copy-done.25, f32[1,8,2048]{2,1,0:T(8,128)} %get-tuple-element.133.log_ref), custom_call_target="tpu_custom_call" | custom-call | flops 60129542144 | bytes 8388608 | tf_op jit(solution)/shard_map/pallas_call | solution.py:302
  268.3 5.8 %convolution_convert_fusion = bf16[2048,1024]{1,0:T(8,128)(2,1)S(1)} fusion(bf16[1024,768]{1,0:T(8,128)(2,1)S(1)} %bitcast.210, bf16[1,2048,768]{2,1,0:T(8,128)(2,1)} %get-tuple-element.134), kind=kOutput, calls=%fused_computation.5 | convolution fusion | flops 3223322624 | bytes 8912896 | tf_op jit(solution)/shard_map/dot_general | solution.py:33
  278.9 4.8 %fusion.42 = (bf16[1024,768]{1,0:T(8,128)(2,1)}, f32[1024]{0:T(1024)S(1)}) fusion(bf16[8,128,768]{2,1,0:T(8,128)(2,1)S(1)} %copy-done.15, bf16[2048,1024]{1,0:T(8,128)(2,1)S(1)} %bitcast.252, bf16[2048,768]{1,0:T(8,128)(2,1)S(1)} %bitcast.255), kind=kOutput, calls=%fused_computation.163 | convolution fusion | flops 3224370176 | bytes 10489856 | tf_op jit(solution)/shard_map/dot_general | solution.py:39
  286.4 4.7 %collective-permute-done.33 = bf16[1024,256]{1,0:T(8,128)(2,1)S(1)} collective-permute-done((bf16[1024,256]{1,0:T(8,128)(2,1)}, bf16[1024,256]{1,0:T(8,128)(2,1)S(1)}, u32[]{:S(2)}, u32[]{:S(2)}) %collective-permute-start.33) | collective-permute-done | bytes 524320 | tf_op jit(solution)/shard_map/ppermute | solution.py:498
  299.4 6.7 %collective-permute-done.37 = bf16[144,1024]{1,0:T(8,128)(2,1)S(1)} collective-permute-done((bf16[144,1024]{1,0:T(8,128)(2,1)S(1)}, bf16[144,1024]{1,0:T(8,128)(2,1)S(1)}, u32[]{:S(2)}, u32[]{:S(2)}) %collective-permute-start.37) | collective-permute-done | bytes 294944 | tf_op jit(solution)/shard_map/ppermute | solution.py:442
  308.5 5.4 %collective-permute-done.38 = bf16[144,1024]{1,0:T(8,128)(2,1)S(1)} collective-permute-done((bf16[144,1024]{1,0:T(8,128)(2,1)S(1)}, bf16[144,1024]{1,0:T(8,128)(2,1)S(1)}, u32[]{:S(2)}, u32[]{:S(2)}) %collective-permute-start.38) | collective-permute-done | bytes 294944 | tf_op jit(solution)/shard_map/ppermute | solution.py:442
  317.0 8.2 %collective-permute-done.31 = bf16[512,1024]{1,0:T(8,128)(2,1)} collective-permute-done((bf16[512,1024]{1,0:T(8,128)(2,1)}, bf16[512,1024]{1,0:T(8,128)(2,1)}, u32[]{:S(2)}, u32[]{:S(2)}) %collective-permute-start.31) | collective-permute-done | bytes 1048608 | tf_op jit(solution)/shard_map/ppermute | solution.py:498
  327.9 3.4 fusion.24
  332.0 4.2 %collective-permute-done.43 = bf16[144,1024]{1,0:T(8,128)(2,1)S(1)} collective-permute-done((bf16[144,1024]{1,0:T(8,128)(2,1)S(1)}, bf16[144,1024]{1,0:T(8,128)(2,1)S(1)}, u32[]{:S(2)}, u32[]{:S(2)}) %collective-permute-start.43) | collective-permute-done | bytes 294944 | tf_op jit(solution)/shard_map/ppermute | solution.py:442
  339.6 4.7 %collective-permute-done.41 = bf16[144,1024]{1,0:T(8,128)(2,1)S(1)} collective-permute-done((bf16[144,1024]{1,0:T(8,128)(2,1)S(1)}, bf16[144,1024]{1,0:T(8,128)(2,1)S(1)}, u32[]{:S(2)}, u32[]{:S(2)}) %collective-permute-start.41) | collective-permute-done | bytes 294944 | tf_op jit(solution)/shard_map/ppermute | solution.py:442
  348.5 10.4 %collective-permute-done.39.refs_2_ = bf16[128,2048]{1,0:T(8,128)(2,1)S(1)} collective-permute-done((bf16[128,2048]{1,0:T(8,128)(2,1)S(1)}, bf16[128,2048]{1,0:T(8,128)(2,1)S(1)}, u32[]{:S(2)}, u32[]{:S(2)}) %collective-permute-start.39) | collective-permute-done | bytes 524320 | tf_op jit(solution)/shard_map/ppermute | solution.py:498
  365.3 3.1 shard_map.270
  (301 shorter events, 126.8 us)
Async XLA Ops:
  7.2 113.8 %all-gather.3.cloned.1.call-start = ((), (), s32[]{:S(2)}) async-start(), calls=%async_computation.2 | async-start | bytes 4718592 | tf_op jit(solution)/shard_map/all_gather | solution.py:695
  13.0 11.8 %collective-permute-start.5 = (bf16[144,1024]{1,0:T(8,128)(2,1)S(1)}, bf16[144,1024]{1,0:T(8,128)(2,1)}, u32[]{:S(2)}, u32[]{:S(2)}) collective-permute-start(bf16[144,1024]{1,0:T(8,128)(2,1)S(1)} %pad_maximum_fusion.3), channel_id=1, source_target_pairs={{0,4},{8,0},{16,8},{24,16},{28,24},{20,28},{12,20},{4,12},{1,5},{9... | collective-permute-start | bytes 884744 | tf_op jit(solution)/shard_map/ppermute | solution.py:442
  13.0 24.9 %collective-permute-start.3 = (bf16[1,512,1024]{2,1,0:T(8,128)(2,1)}, bf16[1,512,1024]{2,1,0:T(8,128)(2,1)}, u32[]{:S(2)}, u32[]{:S(2)}) collective-permute-start(bf16[1,512,1024]{2,1,0:T(8,128)(2,1)} %refs_0_.1), channel_id=1, source_target_pairs={{0,2},{1,3},{2,0},{3,1},{4,6},{5,7},{6,4},{7,5},{8,10},{9,11},{10,... | collective-permute-start | bytes 3145736 | tf_op jit(solution)/shard_map/ppermute | solution.py:498
  14.9 43.3 %collective-permute-start = (bf16[1,512,1024]{2,1,0:T(8,128)(2,1)}, bf16[1,512,1024]{2,1,0:T(8,128)(2,1)}, u32[]{:S(2)}, u32[]{:S(2)}) collective-permute-start(bf16[1,512,1024]{2,1,0:T(8,128)(2,1)} %refs_0_.1), channel_id=1, source_target_pairs={{0,1},{1,0},{2,3},{3,2},{4,5},{5,4},{6,7},{7,6},{8,9},{9,8},{10,11... | collective-permute-start | bytes 3145736 | tf_op jit(solution)/shard_map/ppermute | solution.py:498
  19.9 13.4 %collective-permute-start.2 = (bf16[144,1024]{1,0:T(8,128)(2,1)S(1)}, bf16[144,1024]{1,0:T(8,128)(2,1)}, u32[]{:S(2)}, u32[]{:S(2)}) collective-permute-start(bf16[144,1024]{1,0:T(8,128)(2,1)S(1)} %collective-permute-done.1), channel_id=1, source_target_pairs={{0,8},{8,16},{16,24},{24,28},{28,20},{20,12},{12,4},{4,0},{1,9},{9... | collective-permute-start | bytes 884744 | tf_op jit(solution)/shard_map/ppermute | solution.py:442
  32.8 14.5 %collective-permute-start.8 = (bf16[144,1024]{1,0:T(8,128)(2,1)S(1)}, bf16[144,1024]{1,0:T(8,128)(2,1)}, u32[]{:S(2)}, u32[]{:S(2)}) collective-permute-start(bf16[144,1024]{1,0:T(8,128)(2,1)S(1)} %collective-permute-done.6), channel_id=1, source_target_pairs={{0,4},{8,0},{16,8},{24,16},{28,24},{20,28},{12,20},{4,12},{1,5},{9... | collective-permute-start | bytes 884744 | tf_op jit(solution)/shard_map/ppermute | solution.py:442
  40.7 17.5 %collective-permute-start.4 = (bf16[1,512,1024]{2,1,0:T(8,128)(2,1)}, bf16[1,512,1024]{2,1,0:T(8,128)(2,1)}, u32[]{:S(2)}, u32[]{:S(2)}) collective-permute-start(bf16[1,512,1024]{2,1,0:T(8,128)(2,1)} %collective-permute-done.3.refs_2_), channel_id=1, source_target_pairs={{0,1},{1,0},{2,3},{3,2},{4,5},{5,4},{6,7},{7,6},{8,9},{9,8},{10,11... | collective-permute-start | bytes 3145736 | tf_op jit(solution)/shard_map/ppermute | solution.py:498
  47.2 266.9 %reduce-scatter.2.cloned.1.call-start = ((), (), s32[]{:S(2)}) async-start(), calls=%async_computation.1 | async-start | bytes 4718592 | tf_op jit(solution)/shard_map/reduce_scatter | solution.py:779
  56.8 12.7 %collective-permute-start.10 = (bf16[1024,256]{1,0:T(8,128)(2,1)S(1)}, bf16[1024,256]{1,0:T(8,128)(2,1)S(1)}, u32[]{:S(2)}, u32[]{:S(2)}) collective-permute-start(bf16[1024,256]{1,0:T(8,128)(2,1)S(1)} %bitcast.204), channel_id=1, source_target_pairs={{0,2},{1,3},{2,0},{3,1},{4,6},{5,7},{6,4},{7,5},{8,10},{9,11},{10,... | collective-permute-start | bytes 1572872 | tf_op jit(solution)/shard_map/ppermute | solution.py:498
  69.6 21.4 %collective-permute-start.14 = (bf16[512,1024]{1,0:T(8,128)(2,1)S(1)}, bf16[512,1024]{1,0:T(8,128)(2,1)S(1)}, u32[]{:S(2)}, u32[]{:S(2)}) collective-permute-start(bf16[512,1024]{1,0:T(8,128)(2,1)S(1)} %bitcast.200), channel_id=1, source_target_pairs={{0,2},{1,3},{2,0},{3,1},{4,6},{5,7},{6,4},{7,5},{8,10},{9,11},{10,... | collective-permute-start | bytes 3145736 | tf_op jit(solution)/shard_map/ppermute | solution.py:498
  91.0 11.2 %collective-permute-start.17 = (bf16[512,1024]{1,0:T(8,128)(2,1)S(1)}, bf16[512,1024]{1,0:T(8,128)(2,1)S(1)}, u32[]{:S(2)}, u32[]{:S(2)}) collective-permute-start(bf16[512,1024]{1,0:T(8,128)(2,1)S(1)} %bitcast.201), channel_id=1, source_target_pairs={{0,1},{1,0},{2,3},{3,2},{4,5},{5,4},{6,7},{7,6},{8,9},{9,8},{10,11... | collective-permute-start | bytes 3145736 | tf_op jit(solution)/shard_map/ppermute | solution.py:498
  92.0 11.7 %collective-permute-start.11 = (bf16[1,512,256]{2,1,0:T(8,128)(2,1)S(1)}, bf16[1,512,256]{2,1,0:T(8,128)(2,1)S(1)}, u32[]{:S(2)}, u32[]{:S(2)}) collective-permute-start(bf16[1,512,256]{2,1,0:T(8,128)(2,1)S(1)} %get-tuple-element.183), channel_id=1, source_target_pairs={{0,1},{1,0},{2,3},{3,2},{4,5},{5,4},{6,7},{7,6},{8,9},{9,8},{10,11... | collective-permute-start | bytes 786440 | tf_op jit(solution)/shard_map/ppermute | solution.py:498
  96.7 12.3 %collective-permute-start.13 = (bf16[1,512,256]{2,1,0:T(8,128)(2,1)S(1)}, bf16[1,512,256]{2,1,0:T(8,128)(2,1)S(1)}, u32[]{:S(2)}, u32[]{:S(2)}) collective-permute-start(bf16[1,512,256]{2,1,0:T(8,128)(2,1)S(1)} %get-tuple-element.181), channel_id=1, source_target_pairs={{0,3},{1,2},{2,1},{3,0},{4,7},{5,6},{6,5},{7,4},{8,11},{9,10},{10,... | collective-permute-start | bytes 786440 | tf_op jit(solution)/shard_map/ppermute | solution.py:498
  119.0 25.4 %collective-permute-start.20 = (bf16[512,1024]{1,0:T(8,128)(2,1)}, bf16[512,1024]{1,0:T(8,128)(2,1)}, u32[]{:S(2)}, u32[]{:S(2)}) collective-permute-start(bf16[512,1024]{1,0:T(8,128)(2,1)} %add_convert_fusion.6.refs_0_), channel_id=1, source_target_pairs={{0,2},{1,3},{2,0},{3,1},{4,6},{5,7},{6,4},{7,5},{8,10},{9,11},{10,... | collective-permute-start | bytes 3145736 | tf_op jit(solution)/shard_map/ppermute | solution.py:498
  164.4 23.4 %collective-permute-start.22 = (bf16[512,1024]{1,0:T(8,128)(2,1)}, bf16[512,1024]{1,0:T(8,128)(2,1)}, u32[]{:S(2)}, u32[]{:S(2)}) collective-permute-start(bf16[512,1024]{1,0:T(8,128)(2,1)} %get-tuple-element.117), channel_id=1, source_target_pairs={{0,1},{1,0},{2,3},{3,2},{4,5},{5,4},{6,7},{7,6},{8,9},{9,8},{10,11... | collective-permute-start | bytes 3145736 | tf_op jit(solution)/shard_map/ppermute | solution.py:498
  174.2 25.6 %collective-permute-start.24 = (bf16[512,1024]{1,0:T(8,128)(2,1)}, bf16[512,1024]{1,0:T(8,128)(2,1)}, u32[]{:S(2)}, u32[]{:S(2)}) collective-permute-start(bf16[512,1024]{1,0:T(8,128)(2,1)} %add_convert_fusion.5), channel_id=1, source_target_pairs={{0,2},{1,3},{2,0},{3,1},{4,6},{5,7},{6,4},{7,5},{8,10},{9,11},{10,... | collective-permute-start | bytes 3145736 | tf_op jit(solution)/shard_map/ppermute | solution.py:498
  209.7 15.6 %collective-permute-start.30 = (bf16[1024,256]{1,0:T(8,128)(2,1)}, bf16[1024,256]{1,0:T(8,128)(2,1)}, u32[]{:S(2)}, u32[]{:S(2)}) collective-permute-start(bf16[1024,256]{1,0:T(8,128)(2,1)} %get-tuple-element.177), channel_id=1, source_target_pairs={{0,1},{1,0},{2,3},{3,2},{4,5},{5,4},{6,7},{7,6},{8,9},{9,8},{10,11... | collective-permute-start | bytes 1572872 | tf_op jit(solution)/shard_map/ppermute | solution.py:498
  209.7 18.2 %collective-permute-start.29 = (bf16[512,1024]{1,0:T(8,128)(2,1)}, bf16[512,1024]{1,0:T(8,128)(2,1)S(1)}, u32[]{:S(2)}, u32[]{:S(2)}) collective-permute-start(bf16[512,1024]{1,0:T(8,128)(2,1)} %get-tuple-element.131), channel_id=1, source_target_pairs={{0,1},{1,0},{2,3},{3,2},{4,5},{5,4},{6,7},{7,6},{8,9},{9,8},{10,11... | collective-permute-start | bytes 3145736 | tf_op jit(solution)/shard_map/ppermute | solution.py:498
  212.0 13.3 %collective-permute-start.28 = (bf16[1,512,256]{2,1,0:T(8,128)(2,1)S(1)}, bf16[1,512,256]{2,1,0:T(8,128)(2,1)S(1)}, u32[]{:S(2)}, u32[]{:S(2)}) collective-permute-start(bf16[1,512,256]{2,1,0:T(8,128)(2,1)S(1)} %get-tuple-element.178), channel_id=1, source_target_pairs={{0,3},{1,2},{2,1},{3,0},{4,7},{5,6},{6,5},{7,4},{8,11},{9,10},{10,... | collective-permute-start | bytes 786440 | tf_op jit(solution)/shard_map/ppermute | solution.py:498
  214.3 72.0 %collective-permute-start.32 = (bf16[1024,256]{1,0:T(8,128)(2,1)}, bf16[1024,256]{1,0:T(8,128)(2,1)}, u32[]{:S(2)}, u32[]{:S(2)}) collective-permute-start(bf16[1024,256]{1,0:T(8,128)(2,1)} %get-tuple-element.176), channel_id=1, source_target_pairs={{0,1},{1,0},{2,3},{3,2},{4,5},{5,4},{6,7},{7,6},{8,9},{9,8},{10,11... | collective-permute-start | bytes 1572872 | tf_op jit(solution)/shard_map/ppermute | solution.py:498
  276.4 16.4 %collective-permute-start.34 = (bf16[512,1024]{1,0:T(8,128)(2,1)}, bf16[512,1024]{1,0:T(8,128)(2,1)}, u32[]{:S(2)}, u32[]{:S(2)}) collective-permute-start(bf16[512,1024]{1,0:T(8,128)(2,1)} %get-tuple-element.144), channel_id=1, source_target_pairs={{0,1},{1,0},{2,3},{3,2},{4,5},{5,4},{6,7},{7,6},{8,9},{9,8},{10,11... | collective-permute-start | bytes 3145736 | tf_op jit(solution)/shard_map/ppermute | solution.py:498
  277.0 14.0 %collective-permute-start.33 = (bf16[1024,256]{1,0:T(8,128)(2,1)}, bf16[1024,256]{1,0:T(8,128)(2,1)S(1)}, u32[]{:S(2)}, u32[]{:S(2)}) collective-permute-start(bf16[1024,256]{1,0:T(8,128)(2,1)} %add_convert_fusion.8), channel_id=1, source_target_pairs={{0,2},{1,3},{2,0},{3,1},{4,6},{5,7},{6,4},{7,5},{8,10},{9,11},{10,... | collective-permute-start | bytes 1572872 | tf_op jit(solution)/shard_map/ppermute | solution.py:498
  298.9 26.4 %collective-permute-start.31 = (bf16[512,1024]{1,0:T(8,128)(2,1)}, bf16[512,1024]{1,0:T(8,128)(2,1)}, u32[]{:S(2)}, u32[]{:S(2)}) collective-permute-start(bf16[512,1024]{1,0:T(8,128)(2,1)} %add_convert_fusion.4), channel_id=1, source_target_pairs={{0,2},{1,3},{2,0},{3,1},{4,6},{5,7},{6,4},{7,5},{8,10},{9,11},{10,... | collective-permute-start | bytes 3145736 | tf_op jit(solution)/shard_map/ppermute | solution.py:498
  307.4 20.5 %collective-permute-start.25 = (bf16[512,1024]{1,0:T(8,128)(2,1)}, bf16[512,1024]{1,0:T(8,128)(2,1)}, u32[]{:S(2)}, u32[]{:S(2)}) collective-permute-start(bf16[512,1024]{1,0:T(8,128)(2,1)} %get-tuple-element.129), channel_id=1, source_target_pairs={{0,1},{1,0},{2,3},{3,2},{4,5},{5,4},{6,7},{7,6},{8,9},{9,8},{10,11... | collective-permute-start | bytes 3145736 | tf_op jit(solution)/shard_map/ppermute | solution.py:498
  307.5 17.8 %collective-permute-start.42 = (bf16[144,1024]{1,0:T(8,128)(2,1)}, bf16[144,1024]{1,0:T(8,128)(2,1)}, u32[]{:S(2)}, u32[]{:S(2)}) collective-permute-start(bf16[144,1024]{1,0:T(8,128)(2,1)} %get-tuple-element.174), channel_id=1, source_target_pairs={{0,8},{8,16},{16,24},{24,28},{28,20},{20,12},{12,4},{4,0},{1,9},{9... | collective-permute-start | bytes 884744 | tf_op jit(solution)/shard_map/ppermute | solution.py:442
  314.1 11.7 %collective-permute-start.40 = (bf16[144,1024]{1,0:T(8,128)(2,1)S(1)}, bf16[144,1024]{1,0:T(8,128)(2,1)}, u32[]{:S(2)}, u32[]{:S(2)}) collective-permute-start(bf16[144,1024]{1,0:T(8,128)(2,1)S(1)} %fusion.31), channel_id=1, source_target_pairs={{0,4},{8,0},{16,8},{24,16},{28,24},{20,28},{12,20},{4,12},{1,5},{9... | collective-permute-start | bytes 884744 | tf_op jit(solution)/shard_map/ppermute | solution.py:442
  315.2 33.3 %collective-permute-start.36 = (bf16[512,1024]{1,0:T(8,128)(2,1)}, bf16[512,1024]{1,0:T(8,128)(2,1)S(1)}, u32[]{:S(2)}, u32[]{:S(2)}) collective-permute-start(bf16[512,1024]{1,0:T(8,128)(2,1)} %add_convert_fusion.2), channel_id=1, source_target_pairs={{0,2},{1,3},{2,0},{3,1},{4,6},{5,7},{6,4},{7,5},{8,10},{9,11},{10,... | collective-permute-start | bytes 3145736 | tf_op jit(solution)/shard_map/ppermute | solution.py:498
  325.3 33.6 %collective-permute-start.35 = (bf16[512,1024]{1,0:T(8,128)(2,1)}, bf16[512,1024]{1,0:T(8,128)(2,1)S(1)}, u32[]{:S(2)}, u32[]{:S(2)}) collective-permute-start(bf16[512,1024]{1,0:T(8,128)(2,1)} %get-tuple-element.148), channel_id=1, source_target_pairs={{0,1},{1,0},{2,3},{3,2},{4,5},{5,4},{6,7},{7,6},{8,9},{9,8},{10,11... | collective-permute-start | bytes 3145736 | tf_op jit(solution)/shard_map/ppermute | solution.py:498
  325.3 13.5 %collective-permute-start.48 = (bf16[128,2048]{1,0:T(8,128)(2,1)}, bf16[128,2048]{1,0:T(8,128)(2,1)S(1)}, u32[]{:S(2)}, u32[]{:S(2)}) collective-permute-start(bf16[128,2048]{1,0:T(8,128)(2,1)} %bitcast.212), channel_id=1, source_target_pairs={{0,1},{1,0},{2,3},{3,2},{4,5},{5,4},{6,7},{7,6},{8,9},{9,8},{10,11... | collective-permute-start | bytes 1572872 | tf_op jit(solution)/shard_map/ppermute | solution.py:498
  331.2 27.6 %collective-permute-start.39 = (bf16[128,2048]{1,0:T(8,128)(2,1)S(1)}, bf16[128,2048]{1,0:T(8,128)(2,1)S(1)}, u32[]{:S(2)}, u32[]{:S(2)}) collective-permute-start(bf16[128,2048]{1,0:T(8,128)(2,1)S(1)} %bitcast.214), channel_id=1, source_target_pairs={{0,2},{1,3},{2,0},{3,1},{4,6},{5,7},{6,4},{7,5},{8,10},{9,11},{10,... | collective-permute-start | bytes 1572872 | tf_op jit(solution)/shard_map/ppermute | solution.py:498
  347.8 15.3 %collective-permute-start.45 = (bf16[144,1024]{1,0:T(8,128)(2,1)S(1)}, bf16[144,1024]{1,0:T(8,128)(2,1)S(1)}, u32[]{:S(2)}, u32[]{:S(2)}) collective-permute-start(bf16[144,1024]{1,0:T(8,128)(2,1)S(1)} %fusion.29.refs_0_), channel_id=1, source_target_pairs={{0,1},{1,0},{2,3},{3,2},{4,5},{5,4},{6,7},{7,6},{8,9},{9,8},{10,11... | collective-permute-start | bytes 884744 | tf_op jit(solution)/shard_map/ppermute | solution.py:498
  347.9 15.4 %collective-permute-start.46 = (bf16[144,1024]{1,0:T(8,128)(2,1)S(1)}, bf16[144,1024]{1,0:T(8,128)(2,1)S(1)}, u32[]{:S(2)}, u32[]{:S(2)}) collective-permute-start(bf16[144,1024]{1,0:T(8,128)(2,1)S(1)} %fusion.29.refs_0_), channel_id=1, source_target_pairs={{0,2},{1,3},{2,0},{3,1},{4,6},{5,7},{6,4},{7,5},{8,10},{9,11},{10,... | collective-permute-start | bytes 884744 | tf_op jit(solution)/shard_map/ppermute | solution.py:498
  (68 other events, 530.3 us)
Sparse Core Ops, SparseCore 0:
  47.3 73.6 all-gather.2
  212.2 88.8 reduce-scatter.1

commit v5 on v4

--- a/solution.py
+++ b/solution.py
@@ -730,13 +730,13 @@
     cot_far = swap(cot_sent, top_bit)
     attended, logs = attend(mixed, width)
     sent = picked(attended, 1)
+    arrived = [sent[0]] + [swap(sent[offset], offset) for offset in range(1, ranks)]
     _, cot_far, cot_near, attn_columns, attn_far = lax.optimization_barrier(
-        (sent, cot_far, cot_own, attn_columns, attn_far)
+        (arrived[1], cot_far, cot_own, attn_columns, attn_far)
     )
     near_cot = jnp.concatenate(gather_offsets(cot_near, low_bits), axis=0)
     far_cot = jnp.concatenate(gather_offsets(cot_far, low_bits), axis=0)
 
-    arrived = [sent[0]] + [swap(sent[offset], offset) for offset in range(1, ranks)]
     attn_blocks = gather_offsets(attn_columns, low_bits) + gather_offsets(attn_far, low_bits)
     (full_attn,) = columns(attn_blocks, ((0, 1, width),), BF16)
     arrived, full_attn, near_cot, far_cot = lax.optimization_barrier(
@@ -801,10 +801,11 @@
     ahead_far = swap(ahead_far, top_bit)
     attn_far = swap(attn_far, top_bit)
     ahead_part = reduce_offsets(near_ahead, low_bits)
+    grad_bias_attn = jnp.sum(grad_branch, axis=0, dtype=F32)
+
+    grad_mixed, column_sums = attend_back(mixed, attended, grad_attended, logs, width)
+    grad_mixed, attn_far, ahead_far = lax.optimization_barrier((grad_mixed, attn_far, ahead_far))
     grad_w_attn = (attn_near.astype(F32) + attn_far.astype(F32)).astype(BF16)
-    grad_bias_attn = jnp.sum(grad_branch, axis=0, dtype=F32)
-
-    grad_mixed, column_sums = attend_back(mixed, attended, grad_attended, logs, width)
     grad_mixed = grad_mixed.reshape(seqs * length, 3 * width)
     back = dot_nt(grad_mixed, full_qkv).astype(BF16).reshape(seqs, length, model)
     back_blocks = [item.reshape(seqs * rows, model) for item in picked(back, 1)]
@@ -866,7 +867,6 @@
     fed = gather_offsets(made["scatter"], low_bits) + gather_offsets(fed_far, low_bits)
     rest = gather_offsets(last_scatter)
 
-    _, ahead_far = lax.optimization_barrier((grad_mixed, ahead_far))
     output = (middle + ahead_part.astype(F32) + ahead_far.astype(F32) + proj_bias).astype(BF16)
     unit_one, inverse_one = row_stats(inputs)
     grad_tokens = grad_middle + norm_back(grad_normed, gain_first, unit_one, inverse_one)

time: 384 us -> 375 us (0.977)
  waiting for transfers between devices: 112 us -> 97.1 us
    ppermute x36, waiting for transfers between devices: 71.9 us -> 49.7 us  [swap(): lax.ppermute(array, 'seq', [(rank, rank ^ offset) for rank in range(ranks)])]
    ppermute x14, waiting for transfers between devices: 39.6 us -> 43.6 us  [ring_move(): return lax.ppermute(array, 'dp', pairs)]
    unnamed x105 -> x109, local copies, waits for them, and re-layouts: 10.9 us -> 13.4 us
  transfers between devices with their start and end apart: 52 -> 52, of which waited for: 25 -> 22; matrix products, arithmetic and copies ran while one was open for 23% -> 24% of each run, Pallas kernels for 24% -> 25%
where the time goes in v5:
time: 375 us; the launch traced here: 370 us
  Pallas kernels  111 us (30%)
  waiting for transfers between devices  97.1 us (26%)
  local copies, waits for them, and re-layouts  39.6 us (11%)
  other arithmetic  39.1 us (10%)
  starting transfers between devices  37.8 us (10%)
  matrix products  30.6 us (8%)
  between operations  15.2 us (4%)
    ppermute x36, waiting for transfers between devices, swap(): lax.ppermute(array, 'seq', [(rank, rank ^ offset) for rank in range(ranks)])  49.7 us
    ppermute x14, waiting for transfers between devices, ring_move(): return lax.ppermute(array, 'dp', pairs)  43.6 us
    pallas_call x1, Pallas kernels, attend_back(): pl.pallas_call(functools.partial(attend_back_kernel, block=block, width=w...  39.1 us
    pallas_call x2, Pallas kernels, feed(): pl.pallas_call(functools.partial(feed_kernel, parts=parts, steps=steps),...  31.4 us
    ppermute x36, starting transfers between devices, swap(): lax.ppermute(array, 'seq', [(rank, rank ^ offset) for rank in range(ranks)])  21.2 us
    dot_general x6, matrix products, dot_tn(): lax.dot_general(left_side, right_side, (((0,), (0,)), ((), ())), preferre...  20.5 us
    pallas_call x1, Pallas kernels, attend(): pl.pallas_call(functools.partial(attend_kernel, block=block, width=width)...  17.6 us
    ppermute x14, starting transfers between devices, ring_move(): return lax.ppermute(array, 'dp', pairs)  16.5 us
  transfers between devices with their start and end apart: 52, of which 22 were waited for; matrix products, arithmetic and copies ran while one was open for 24% of the time, Pallas kernels for 25%

profile of v5, /device:TPU:0, one launch (start us, length us, event | category | flops | bytes accessed | tf_op | source)
XLA Modules:
  0.0 370.3 jit_solution(4425694822269602618)
XLA Ops:
  9.9 3.1 collective-permute-start.1
  15.3 4.6 %collective-permute-done.1 = bf16[144,1024]{1,0:T(8,128)(2,1)S(1)} collective-permute-done((bf16[144,1024]{1,0:T(8,128)(2,1)S(1)}, bf16[144,1024]{1,0:T(8,128)(2,1)S(1)}, u32[]{:S(2)}, u32[]{:S(2)}) %collective-permute-start.1) | collective-permute-done | bytes 294944 | tf_op jit(solution)/shard_map/ppermute | solution.py:442
  33.3 4.6 %collective-permute-done.3.refs_2_ = bf16[1,512,1024]{2,1,0:T(8,128)(2,1)} collective-permute-done((bf16[1,512,1024]{2,1,0:T(8,128)(2,1)}, bf16[1,512,1024]{2,1,0:T(8,128)(2,1)}, u32[]{:S(2)}, u32[]{:S(2)}) %collective-permute-start.3) | collective-permute-done | bytes 1048608 | tf_op jit(solution)/shard_map/ppermute | solution.py:498
  40.8 4.9 %collective-permute-done.7 = bf16[144,1024]{1,0:T(8,128)(2,1)S(1)} collective-permute-done((bf16[144,1024]{1,0:T(8,128)(2,1)}, bf16[144,1024]{1,0:T(8,128)(2,1)S(1)}, u32[]{:S(2)}, u32[]{:S(2)}) %collective-permute-start.7) | collective-permute-done | bytes 294944 | tf_op jit(solution)/shard_map/ppermute | solution.py:442
  48.2 4.3 %collective-permute-done.9 = bf16[144,1024]{1,0:T(8,128)(2,1)} collective-permute-done((bf16[144,1024]{1,0:T(8,128)(2,1)S(1)}, bf16[144,1024]{1,0:T(8,128)(2,1)}, u32[]{:S(2)}, u32[]{:S(2)}) %collective-permute-start.9) | collective-permute-done | bytes 294944 | tf_op jit(solution)/shard_map/ppermute | solution.py:442
  58.3 11.5 %shard_map.262 = (bf16[1,4,512,1024]{3,2,1,0:T(8,128)(2,1)}, bf16[1,4,512,768]{3,2,1,0:T(8,128)(2,1)}) custom-call(s32[1]{0:T(128)} %bitcast.2.rank_ref, bf16[1,512,1024]{2,1,0:T(8,128)(2,1)} %refs_0_.1, bf16[1,512,1024]{2,1,0:T(8,128)(2,1)} %collective-permute-done.refs_1_, bf16[1,512,1024]{2,1,0:T(8,128)(2,1)} %collective-permute-done.3.refs_2_, ...), custom_call_target="tpu_custom_call" | custom-call | flops 6442450944 | bytes 13107200 | tf_op jit(solution)/shard_map/pallas_call | solution.py:83
  70.6 17.6 %shard_map.263 = (bf16[1,2048,256]{2,1,0:T(8,128)(2,1)}, f32[1,8,2048]{2,1,0:T(8,128)}) custom-call(bf16[1,2048,768]{2,1,0:T(8,128)(2,1)} %bitcast.253), custom_call_target="tpu_custom_call" | custom-call | flops 30064771072 | bytes 4194304 | tf_op jit(solution)/shard_map/pallas_call | solution.py:177
  98.5 3.1 shard_map.264
  117.2 3.7 %all-gather.3.cloned.1.call-done.refs_3_.refs_4_ = bf16[1024,2048]{1,0:T(8,128)(2,1)} async-done(((bf16[128,2048]{1,0:T(8,128)(2,1)}), bf16[1024,2048]{1,0:T(8,128)(2,1)}) %all-gather.3.cloned.1.call-update) | async-done | bytes 4194320 | tf_op jit(solution)/shard_map/all_gather | solution.py:695
  120.9 15.6 %shard_map.266 = (bf16[1024,1024]{1,0:T(8,128)(2,1)}, bf16[1024,1024]{1,0:T(8,128)(2,1)}, bf16[512,1024]{1,0:T(8,128)(2,1)}, bf16[512,1024]{1,0:T(8,128)(2,1)}, ...) custom-call(bf16[512,1024]{1,0:T(8,128)(2,1)} %add_convert_fusion.6.refs_0_, ...), custom_call_target="tpu_custom_call" | custom-call | flops 15032385536 | bytes 16777216 | tf_op jit(solution)/shard_map/pallas_call | solution.py:395
  136.6 4.6 %collective-permute-done.20.refs_0_ = bf16[512,1024]{1,0:T(8,128)(2,1)} collective-permute-done((bf16[512,1024]{1,0:T(8,128)(2,1)}, bf16[512,1024]{1,0:T(8,128)(2,1)}, u32[]{:S(2)}, u32[]{:S(2)}) %collective-permute-start.20) | collective-permute-done | bytes 1048608 | tf_op jit(solution)/shard_map/ppermute | solution.py:498
  141.2 2.9 collective-permute-done.21.refs_1_
  145.1 15.8 %shard_map.267 = (bf16[1024,1024]{1,0:T(8,128)(2,1)}, bf16[1024,1024]{1,0:T(8,128)(2,1)}, bf16[512,1024]{1,0:T(8,128)(2,1)}, bf16[512,1024]{1,0:T(8,128)(2,1)}, ...) custom-call(bf16[512,1024]{1,0:T(8,128)(2,1)} %collective-permute-done.20.refs_0_, ...), custom_call_target="tpu_custom_call" | custom-call | flops 15032385536 | bytes 16777216 | tf_op jit(solution)/shard_map/pallas_call | solution.py:395
  163.9 2.9 add_convert_fusion.5
  166.8 4.2 %fusion.45 = f32[1024,1024]{1,0:T(8,128)S(1)} fusion(bf16[1024,1024]{1,0:T(8,128)(2,1)} %get-tuple-element.128, bf16[1024,1024]{1,0:T(8,128)(2,1)S(1)} %copy-done.14), kind=kOutput, calls=%fused_computation.166 | convolution fusion | flops 2147483648 | bytes 8388608 | tf_op jit(solution)/shard_map/dot_general | solution.py:39
  172.5 3.7 fusion.18
  176.2 4.1 %add_convert_fusion.1 = bf16[1024,1024]{1,0:T(8,128)(2,1)S(1)} fusion(f32[1024,1024]{1,0:T(8,128)S(1)} %fusion.18, bf16[1024,1024]{1,0:T(8,128)(2,1)S(1)} %copy-done.49, bf16[512,1024]{1,0:T(8,128)(2,1)} %collective-permute-done.19.refs_1_, bf16[512,1024]{1,0:T(8,128)(2,1)} %add_convert_fusion.6.refs_0_), kind=kOutput, calls=%fused_computation.4 | convolution fusion | flops 2153775104 | bytes 10485760 | tf_op jit(solution)/shard_map/dot_general | solution.py:39
  185.2 11.4 %collective-permute-done.24 = bf16[512,1024]{1,0:T(8,128)(2,1)} collective-permute-done((bf16[512,1024]{1,0:T(8,128)(2,1)}, bf16[512,1024]{1,0:T(8,128)(2,1)}, u32[]{:S(2)}, u32[]{:S(2)}) %collective-permute-start.24) | collective-permute-done | bytes 1048608 | tf_op jit(solution)/shard_map/ppermute | solution.py:498
  212.7 4.9 %collective-permute-done.27 = bf16[1,512,256]{2,1,0:T(8,128)(2,1)} collective-permute-done((bf16[1,512,256]{2,1,0:T(8,128)(2,1)}, bf16[1,512,256]{2,1,0:T(8,128)(2,1)}, u32[]{:S(2)}, u32[]{:S(2)}) %collective-permute-start.27) | collective-permute-done | bytes 262176 | tf_op jit(solution)/shard_map/ppermute | solution.py:498
  218.6 3.8 %collective-permute-done.28 = bf16[1,512,256]{2,1,0:T(8,128)(2,1)S(1)} collective-permute-done((bf16[1,512,256]{2,1,0:T(8,128)(2,1)S(1)}, bf16[1,512,256]{2,1,0:T(8,128)(2,1)S(1)}, u32[]{:S(2)}, u32[]{:S(2)}) %collective-permute-start.28) | collective-permute-done | bytes 262176 | tf_op jit(solution)/shard_map/ppermute | solution.py:498
  228.3 39.1 %shard_map.268 = (bf16[1,2048,768]{2,1,0:T(8,128)(2,1)}, f32[1,8,768]{2,1,0:T(8,128)}) custom-call(bf16[1,2048,768]{2,1,0:T(8,128)(2,1)} %bitcast.254, bf16[1,2048,256]{2,1,0:T(8,128)(2,1)} %get-tuple-element.96.out_ref, bf16[1,2048,256]{2,1,0:T(8,128)(2,1)} %copy-done.26, f32[1,8,2048]{2,1,0:T(8,128)} %get-tuple-element.135.log_ref), custom_call_target="tpu_custom_call" | custom-call | flops 60129542144 | bytes 8388608 | tf_op jit(solution)/shard_map/pallas_call | solution.py:302
  270.0 6.2 %convolution_convert_fusion = bf16[2048,1024]{1,0:T(8,128)(2,1)S(1)} fusion(bf16[1024,768]{1,0:T(8,128)(2,1)} %bitcast.210, bf16[1,2048,768]{2,1,0:T(8,128)(2,1)} %get-tuple-element.141), kind=kOutput, calls=%fused_computation.5 | convolution fusion | flops 3223322624 | bytes 8912896 | tf_op jit(solution)/shard_map/dot_general | solution.py:33
  280.5 4.8 %fusion.42 = (bf16[1024,768]{1,0:T(8,128)(2,1)}, f32[1024]{0:T(1024)S(1)}) fusion(bf16[8,128,768]{2,1,0:T(8,128)(2,1)S(1)} %copy-done.15, bf16[2048,1024]{1,0:T(8,128)(2,1)S(1)} %bitcast.252, bf16[2048,768]{1,0:T(8,128)(2,1)S(1)} %bitcast.255), kind=kOutput, calls=%fused_computation.163 | convolution fusion | flops 3224370176 | bytes 10489856 | tf_op jit(solution)/shard_map/dot_general | solution.py:39
  289.5 2.9 add_convert_fusion.2
  294.5 8.3 %collective-permute-done.37 = bf16[144,1024]{1,0:T(8,128)(2,1)S(1)} collective-permute-done((bf16[144,1024]{1,0:T(8,128)(2,1)S(1)}, bf16[144,1024]{1,0:T(8,128)(2,1)S(1)}, u32[]{:S(2)}, u32[]{:S(2)}) %collective-permute-start.37) | collective-permute-done | bytes 294944 | tf_op jit(solution)/shard_map/ppermute | solution.py:442
  305.4 6.4 %collective-permute-done.38 = bf16[144,1024]{1,0:T(8,128)(2,1)S(1)} collective-permute-done((bf16[144,1024]{1,0:T(8,128)(2,1)S(1)}, bf16[144,1024]{1,0:T(8,128)(2,1)S(1)}, u32[]{:S(2)}, u32[]{:S(2)}) %collective-permute-start.38) | collective-permute-done | bytes 294944 | tf_op jit(solution)/shard_map/ppermute | solution.py:442
  314.2 5.7 %collective-permute-done.40 = bf16[144,1024]{1,0:T(8,128)(2,1)} collective-permute-done((bf16[144,1024]{1,0:T(8,128)(2,1)S(1)}, bf16[144,1024]{1,0:T(8,128)(2,1)}, u32[]{:S(2)}, u32[]{:S(2)}) %collective-permute-start.40) | collective-permute-done | bytes 294944 | tf_op jit(solution)/shard_map/ppermute | solution.py:442
  323.2 3.4 fusion.24
  331.9 5.3 %collective-permute-done.41 = bf16[144,1024]{1,0:T(8,128)(2,1)S(1)} collective-permute-done((bf16[144,1024]{1,0:T(8,128)(2,1)S(1)}, bf16[144,1024]{1,0:T(8,128)(2,1)S(1)}, u32[]{:S(2)}, u32[]{:S(2)}) %collective-permute-start.41) | collective-permute-done | bytes 294944 | tf_op jit(solution)/shard_map/ppermute | solution.py:442
  340.3 10.0 %collective-permute-done.39.refs_2_ = bf16[128,2048]{1,0:T(8,128)(2,1)S(1)} collective-permute-done((bf16[128,2048]{1,0:T(8,128)(2,1)S(1)}, bf16[128,2048]{1,0:T(8,128)(2,1)S(1)}, u32[]{:S(2)}, u32[]{:S(2)}) %collective-permute-start.39) | collective-permute-done | bytes 524320 | tf_op jit(solution)/shard_map/ppermute | solution.py:498
  356.7 3.1 shard_map.270
  360.6 2.7 shard_map.269
  (305 shorter events, 125.8 us)
Async XLA Ops:
  7.2 113.8 %all-gather.3.cloned.1.call-start = ((), (), s32[]{:S(2)}) async-start(), calls=%async_computation.2 | async-start | bytes 4718592 | tf_op jit(solution)/shard_map/all_gather | solution.py:695
  9.9 10.0 %collective-permute-start.1 = (bf16[144,1024]{1,0:T(8,128)(2,1)S(1)}, bf16[144,1024]{1,0:T(8,128)(2,1)S(1)}, u32[]{:S(2)}, u32[]{:S(2)}) collective-permute-start(bf16[144,1024]{1,0:T(8,128)(2,1)S(1)} %pad_maximum_fusion.3), channel_id=1, source_target_pairs={{0,8},{8,16},{16,24},{24,28},{28,20},{20,12},{12,4},{4,0},{1,9},{9... | collective-permute-start | bytes 884744 | tf_op jit(solution)/shard_map/ppermute | solution.py:442
  13.0 11.8 %collective-permute-start.5 = (bf16[144,1024]{1,0:T(8,128)(2,1)S(1)}, bf16[144,1024]{1,0:T(8,128)(2,1)}, u32[]{:S(2)}, u32[]{:S(2)}) collective-permute-start(bf16[144,1024]{1,0:T(8,128)(2,1)S(1)} %pad_maximum_fusion.3), channel_id=1, source_target_pairs={{0,4},{8,0},{16,8},{24,16},{28,24},{20,28},{12,20},{4,12},{1,5},{9... | collective-permute-start | bytes 884744 | tf_op jit(solution)/shard_map/ppermute | solution.py:442
  13.0 24.9 %collective-permute-start.3 = (bf16[1,512,1024]{2,1,0:T(8,128)(2,1)}, bf16[1,512,1024]{2,1,0:T(8,128)(2,1)}, u32[]{:S(2)}, u32[]{:S(2)}) collective-permute-start(bf16[1,512,1024]{2,1,0:T(8,128)(2,1)} %refs_0_.1), channel_id=1, source_target_pairs={{0,2},{1,3},{2,0},{3,1},{4,6},{5,7},{6,4},{7,5},{8,10},{9,11},{10,... | collective-permute-start | bytes 3145736 | tf_op jit(solution)/shard_map/ppermute | solution.py:498
  14.9 43.3 %collective-permute-start = (bf16[1,512,1024]{2,1,0:T(8,128)(2,1)}, bf16[1,512,1024]{2,1,0:T(8,128)(2,1)}, u32[]{:S(2)}, u32[]{:S(2)}) collective-permute-start(bf16[1,512,1024]{2,1,0:T(8,128)(2,1)} %refs_0_.1), channel_id=1, source_target_pairs={{0,1},{1,0},{2,3},{3,2},{4,5},{5,4},{6,7},{7,6},{8,9},{9,8},{10,11... | collective-permute-start | bytes 3145736 | tf_op jit(solution)/shard_map/ppermute | solution.py:498
  19.9 13.4 %collective-permute-start.2 = (bf16[144,1024]{1,0:T(8,128)(2,1)S(1)}, bf16[144,1024]{1,0:T(8,128)(2,1)}, u32[]{:S(2)}, u32[]{:S(2)}) collective-permute-start(bf16[144,1024]{1,0:T(8,128)(2,1)S(1)} %collective-permute-done.1), channel_id=1, source_target_pairs={{0,8},{8,16},{16,24},{24,28},{28,20},{20,12},{12,4},{4,0},{1,9},{9... | collective-permute-start | bytes 884744 | tf_op jit(solution)/shard_map/ppermute | solution.py:442
  32.8 14.5 %collective-permute-start.8 = (bf16[144,1024]{1,0:T(8,128)(2,1)S(1)}, bf16[144,1024]{1,0:T(8,128)(2,1)}, u32[]{:S(2)}, u32[]{:S(2)}) collective-permute-start(bf16[144,1024]{1,0:T(8,128)(2,1)S(1)} %collective-permute-done.6), channel_id=1, source_target_pairs={{0,4},{8,0},{16,8},{24,16},{28,24},{20,28},{12,20},{4,12},{1,5},{9... | collective-permute-start | bytes 884744 | tf_op jit(solution)/shard_map/ppermute | solution.py:442
  40.7 17.5 %collective-permute-start.4 = (bf16[1,512,1024]{2,1,0:T(8,128)(2,1)}, bf16[1,512,1024]{2,1,0:T(8,128)(2,1)}, u32[]{:S(2)}, u32[]{:S(2)}) collective-permute-start(bf16[1,512,1024]{2,1,0:T(8,128)(2,1)} %collective-permute-done.3.refs_2_), channel_id=1, source_target_pairs={{0,1},{1,0},{2,3},{3,2},{4,5},{5,4},{6,7},{7,6},{8,9},{9,8},{10,11... | collective-permute-start | bytes 3145736 | tf_op jit(solution)/shard_map/ppermute | solution.py:498
  47.2 264.7 %reduce-scatter.2.cloned.1.call-start = ((), (), s32[]{:S(2)}) async-start(), calls=%async_computation.1 | async-start | bytes 4718592 | tf_op jit(solution)/shard_map/reduce_scatter | solution.py:779
  56.9 13.0 %collective-permute-start.10 = (bf16[1024,256]{1,0:T(8,128)(2,1)S(1)}, bf16[1024,256]{1,0:T(8,128)(2,1)S(1)}, u32[]{:S(2)}, u32[]{:S(2)}) collective-permute-start(bf16[1024,256]{1,0:T(8,128)(2,1)S(1)} %bitcast.204), channel_id=1, source_target_pairs={{0,2},{1,3},{2,0},{3,1},{4,6},{5,7},{6,4},{7,5},{8,10},{9,11},{10,... | collective-permute-start | bytes 1572872 | tf_op jit(solution)/shard_map/ppermute | solution.py:498
  69.9 21.8 %collective-permute-start.14 = (bf16[512,1024]{1,0:T(8,128)(2,1)S(1)}, bf16[512,1024]{1,0:T(8,128)(2,1)S(1)}, u32[]{:S(2)}, u32[]{:S(2)}) collective-permute-start(bf16[512,1024]{1,0:T(8,128)(2,1)S(1)} %bitcast.200), channel_id=1, source_target_pairs={{0,2},{1,3},{2,0},{3,1},{4,6},{5,7},{6,4},{7,5},{8,10},{9,11},{10,... | collective-permute-start | bytes 3145736 | tf_op jit(solution)/shard_map/ppermute | solution.py:498
  91.6 10.0 %collective-permute-start.18 = (bf16[512,1024]{1,0:T(8,128)(2,1)S(1)}, bf16[512,1024]{1,0:T(8,128)(2,1)S(1)}, u32[]{:S(2)}, u32[]{:S(2)}) collective-permute-start(bf16[512,1024]{1,0:T(8,128)(2,1)S(1)} %collective-permute-done.14), channel_id=1, source_target_pairs={{0,1},{1,0},{2,3},{3,2},{4,5},{5,4},{6,7},{7,6},{8,9},{9,8},{10,11... | collective-permute-start | bytes 3145736 | tf_op jit(solution)/shard_map/ppermute | solution.py:498
  91.8 11.4 %collective-permute-start.17 = (bf16[512,1024]{1,0:T(8,128)(2,1)S(1)}, bf16[512,1024]{1,0:T(8,128)(2,1)S(1)}, u32[]{:S(2)}, u32[]{:S(2)}) collective-permute-start(bf16[512,1024]{1,0:T(8,128)(2,1)S(1)} %bitcast.201), channel_id=1, source_target_pairs={{0,1},{1,0},{2,3},{3,2},{4,5},{5,4},{6,7},{7,6},{8,9},{9,8},{10,11... | collective-permute-start | bytes 3145736 | tf_op jit(solution)/shard_map/ppermute | solution.py:498
  92.7 12.0 %collective-permute-start.12 = (bf16[1,512,256]{2,1,0:T(8,128)(2,1)S(1)}, bf16[1,512,256]{2,1,0:T(8,128)(2,1)S(1)}, u32[]{:S(2)}, u32[]{:S(2)}) collective-permute-start(bf16[1,512,256]{2,1,0:T(8,128)(2,1)S(1)} %get-tuple-element.186), channel_id=1, source_target_pairs={{0,2},{1,3},{2,0},{3,1},{4,6},{5,7},{6,4},{7,5},{8,10},{9,11},{10,... | collective-permute-start | bytes 786440 | tf_op jit(solution)/shard_map/ppermute | solution.py:498
  115.8 25.4 %collective-permute-start.20 = (bf16[512,1024]{1,0:T(8,128)(2,1)}, bf16[512,1024]{1,0:T(8,128)(2,1)}, u32[]{:S(2)}, u32[]{:S(2)}) collective-permute-start(bf16[512,1024]{1,0:T(8,128)(2,1)} %add_convert_fusion.6.refs_0_), channel_id=1, source_target_pairs={{0,2},{1,3},{2,0},{3,1},{4,6},{5,7},{6,4},{7,5},{8,10},{9,11},{10,... | collective-permute-start | bytes 3145736 | tf_op jit(solution)/shard_map/ppermute | solution.py:498
  161.3 23.9 %collective-permute-start.22 = (bf16[512,1024]{1,0:T(8,128)(2,1)}, bf16[512,1024]{1,0:T(8,128)(2,1)}, u32[]{:S(2)}, u32[]{:S(2)}) collective-permute-start(bf16[512,1024]{1,0:T(8,128)(2,1)} %get-tuple-element.119), channel_id=1, source_target_pairs={{0,1},{1,0},{2,3},{3,2},{4,5},{5,4},{6,7},{7,6},{8,9},{9,8},{10,11... | collective-permute-start | bytes 3145736 | tf_op jit(solution)/shard_map/ppermute | solution.py:498
  171.0 25.6 %collective-permute-start.24 = (bf16[512,1024]{1,0:T(8,128)(2,1)}, bf16[512,1024]{1,0:T(8,128)(2,1)}, u32[]{:S(2)}, u32[]{:S(2)}) collective-permute-start(bf16[512,1024]{1,0:T(8,128)(2,1)} %add_convert_fusion.5), channel_id=1, source_target_pairs={{0,2},{1,3},{2,0},{3,1},{4,6},{5,7},{6,4},{7,5},{8,10},{9,11},{10,... | collective-permute-start | bytes 3145736 | tf_op jit(solution)/shard_map/ppermute | solution.py:498
  206.8 15.7 %collective-permute-start.30 = (bf16[1024,256]{1,0:T(8,128)(2,1)}, bf16[1024,256]{1,0:T(8,128)(2,1)}, u32[]{:S(2)}, u32[]{:S(2)}) collective-permute-start(bf16[1024,256]{1,0:T(8,128)(2,1)} %get-tuple-element.181), channel_id=1, source_target_pairs={{0,1},{1,0},{2,3},{3,2},{4,5},{5,4},{6,7},{7,6},{8,9},{9,8},{10,11... | collective-permute-start | bytes 1572872 | tf_op jit(solution)/shard_map/ppermute | solution.py:498
  206.8 18.2 %collective-permute-start.29 = (bf16[512,1024]{1,0:T(8,128)(2,1)}, bf16[512,1024]{1,0:T(8,128)(2,1)S(1)}, u32[]{:S(2)}, u32[]{:S(2)}) collective-permute-start(bf16[512,1024]{1,0:T(8,128)(2,1)} %get-tuple-element.133), channel_id=1, source_target_pairs={{0,1},{1,0},{2,3},{3,2},{4,5},{5,4},{6,7},{7,6},{8,9},{9,8},{10,11... | collective-permute-start | bytes 3145736 | tf_op jit(solution)/shard_map/ppermute | solution.py:498
  209.7 12.7 %collective-permute-start.28 = (bf16[1,512,256]{2,1,0:T(8,128)(2,1)S(1)}, bf16[1,512,256]{2,1,0:T(8,128)(2,1)S(1)}, u32[]{:S(2)}, u32[]{:S(2)}) collective-permute-start(bf16[1,512,256]{2,1,0:T(8,128)(2,1)S(1)} %get-tuple-element.182), channel_id=1, source_target_pairs={{0,3},{1,2},{2,1},{3,0},{4,7},{5,6},{6,5},{7,4},{8,11},{9,10},{10,... | collective-permute-start | bytes 786440 | tf_op jit(solution)/shard_map/ppermute | solution.py:498
  211.4 75.0 %collective-permute-start.33 = (bf16[1024,256]{1,0:T(8,128)(2,1)}, bf16[1024,256]{1,0:T(8,128)(2,1)}, u32[]{:S(2)}, u32[]{:S(2)}) collective-permute-start(bf16[1024,256]{1,0:T(8,128)(2,1)} %get-tuple-element.180), channel_id=1, source_target_pairs={{0,1},{1,0},{2,3},{3,2},{4,5},{5,4},{6,7},{7,6},{8,9},{9,8},{10,11... | collective-permute-start | bytes 1572872 | tf_op jit(solution)/shard_map/ppermute | solution.py:498
  226.3 43.7 %collective-permute-start.32 = (bf16[512,1024]{1,0:T(8,128)(2,1)}, bf16[512,1024]{1,0:T(8,128)(2,1)S(1)}, u32[]{:S(2)}, u32[]{:S(2)}) collective-permute-start(bf16[512,1024]{1,0:T(8,128)(2,1)} %add_convert_fusion.4), channel_id=1, source_target_pairs={{0,2},{1,3},{2,0},{3,1},{4,6},{5,7},{6,4},{7,5},{8,10},{9,11},{10,... | collective-permute-start | bytes 3145736 | tf_op jit(solution)/shard_map/ppermute | solution.py:498
  227.7 42.3 %collective-permute-start.31 = (bf16[1024,256]{1,0:T(8,128)(2,1)}, bf16[1024,256]{1,0:T(8,128)(2,1)}, u32[]{:S(2)}, u32[]{:S(2)}) collective-permute-start(bf16[1024,256]{1,0:T(8,128)(2,1)} %add_convert_fusion.8), channel_id=1, source_target_pairs={{0,2},{1,3},{2,0},{3,1},{4,6},{5,7},{6,4},{7,5},{8,10},{9,11},{10,... | collective-permute-start | bytes 1572872 | tf_op jit(solution)/shard_map/ppermute | solution.py:498
  278.6 10.0 %collective-permute-start.34 = (bf16[512,1024]{1,0:T(8,128)(2,1)}, bf16[512,1024]{1,0:T(8,128)(2,1)}, u32[]{:S(2)}, u32[]{:S(2)}) collective-permute-start(bf16[512,1024]{1,0:T(8,128)(2,1)} %get-tuple-element.148), channel_id=1, source_target_pairs={{0,1},{1,0},{2,3},{3,2},{4,5},{5,4},{6,7},{7,6},{8,9},{9,8},{10,11... | collective-permute-start | bytes 3145736 | tf_op jit(solution)/shard_map/ppermute | solution.py:498
  303.8 19.3 %collective-permute-start.25 = (bf16[512,1024]{1,0:T(8,128)(2,1)}, bf16[512,1024]{1,0:T(8,128)(2,1)}, u32[]{:S(2)}, u32[]{:S(2)}) collective-permute-start(bf16[512,1024]{1,0:T(8,128)(2,1)} %get-tuple-element.131), channel_id=1, source_target_pairs={{0,1},{1,0},{2,3},{3,2},{4,5},{5,4},{6,7},{7,6},{8,9},{9,8},{10,11... | collective-permute-start | bytes 3145736 | tf_op jit(solution)/shard_map/ppermute | solution.py:498
  303.9 10.3 %collective-permute-start.42 = (bf16[144,1024]{1,0:T(8,128)(2,1)}, bf16[144,1024]{1,0:T(8,128)(2,1)}, u32[]{:S(2)}, u32[]{:S(2)}) collective-permute-start(bf16[144,1024]{1,0:T(8,128)(2,1)} %get-tuple-element.178), channel_id=1, source_target_pairs={{0,8},{8,16},{16,24},{24,28},{28,20},{20,12},{12,4},{4,0},{1,9},{9... | collective-permute-start | bytes 884744 | tf_op jit(solution)/shard_map/ppermute | solution.py:442
  312.7 27.6 %collective-permute-start.36 = (bf16[512,1024]{1,0:T(8,128)(2,1)}, bf16[512,1024]{1,0:T(8,128)(2,1)S(1)}, u32[]{:S(2)}, u32[]{:S(2)}) collective-permute-start(bf16[512,1024]{1,0:T(8,128)(2,1)} %add_convert_fusion.2), channel_id=1, source_target_pairs={{0,2},{1,3},{2,0},{3,1},{4,6},{5,7},{6,4},{7,5},{8,10},{9,11},{10,... | collective-permute-start | bytes 3145736 | tf_op jit(solution)/shard_map/ppermute | solution.py:498
  314.2 15.7 %collective-permute-start.48 = (bf16[128,2048]{1,0:T(8,128)(2,1)}, bf16[128,2048]{1,0:T(8,128)(2,1)S(1)}, u32[]{:S(2)}, u32[]{:S(2)}) collective-permute-start(bf16[128,2048]{1,0:T(8,128)(2,1)} %bitcast.212), channel_id=1, source_target_pairs={{0,1},{1,0},{2,3},{3,2},{4,5},{5,4},{6,7},{7,6},{8,9},{9,8},{10,11... | collective-permute-start | bytes 1572872 | tf_op jit(solution)/shard_map/ppermute | solution.py:498
  326.6 23.7 %collective-permute-start.35 = (bf16[512,1024]{1,0:T(8,128)(2,1)S(1)}, bf16[512,1024]{1,0:T(8,128)(2,1)S(1)}, u32[]{:S(2)}, u32[]{:S(2)}) collective-permute-start(bf16[512,1024]{1,0:T(8,128)(2,1)S(1)} %copy-done.22), channel_id=1, source_target_pairs={{0,1},{1,0},{2,3},{3,2},{4,5},{5,4},{6,7},{7,6},{8,9},{9,8},{10,11... | collective-permute-start | bytes 3145736 | tf_op jit(solution)/shard_map/ppermute | solution.py:498
  326.6 23.7 %collective-permute-start.39 = (bf16[128,2048]{1,0:T(8,128)(2,1)S(1)}, bf16[128,2048]{1,0:T(8,128)(2,1)S(1)}, u32[]{:S(2)}, u32[]{:S(2)}) collective-permute-start(bf16[128,2048]{1,0:T(8,128)(2,1)S(1)} %bitcast.214), channel_id=1, source_target_pairs={{0,2},{1,3},{2,0},{3,1},{4,6},{5,7},{6,4},{7,5},{8,10},{9,11},{10,... | collective-permute-start | bytes 1572872 | tf_op jit(solution)/shard_map/ppermute | solution.py:498
  339.7 14.8 %collective-permute-start.45 = (bf16[144,1024]{1,0:T(8,128)(2,1)S(1)}, bf16[144,1024]{1,0:T(8,128)(2,1)S(1)}, u32[]{:S(2)}, u32[]{:S(2)}) collective-permute-start(bf16[144,1024]{1,0:T(8,128)(2,1)S(1)} %fusion.29.refs_0_), channel_id=1, source_target_pairs={{0,1},{1,0},{2,3},{3,2},{4,5},{5,4},{6,7},{7,6},{8,9},{9,8},{10,11... | collective-permute-start | bytes 884744 | tf_op jit(solution)/shard_map/ppermute | solution.py:498
  339.7 14.9 %collective-permute-start.46 = (bf16[144,1024]{1,0:T(8,128)(2,1)S(1)}, bf16[144,1024]{1,0:T(8,128)(2,1)S(1)}, u32[]{:S(2)}, u32[]{:S(2)}) collective-permute-start(bf16[144,1024]{1,0:T(8,128)(2,1)S(1)} %fusion.29.refs_0_), channel_id=1, source_target_pairs={{0,2},{1,3},{2,0},{3,1},{4,6},{5,7},{6,4},{7,5},{8,10},{9,11},{10,... | collective-permute-start | bytes 884744 | tf_op jit(solution)/shard_map/ppermute | solution.py:498
  (70 other events, 529.4 us)
Sparse Core Ops, SparseCore 0:
  47.3 73.6 all-gather.2
  209.8 88.3 reduce-scatter.1
